TPU v7x, 512 devices: a whole 4x8x8 slice. The times are simulated.
512 devices in a mesh: dp: 16 (over y, x_hi), ctx: 8 (over z), tp: 4 (over x_lo, core).
Axes of the slice: x: 4 (x_hi: 2, x_lo: 2; x = x_hi * 2 + x_lo), y: 8, z: 8, core: 2. Of those that a mesh axis runs over, the one named last changes fastest.
Arguments:
- queries: bfloat16 [32768, 1280], P(('dp', 'ctx'), 'tp'), may hold values from -300 to 300, as said below
- keys: bfloat16 [32768, 1280], P(('dp', 'ctx'), 'tp'), may hold values from -7 to 7, as said below
- values: bfloat16 [32768, 1280], P(('dp', 'ctx'), 'tp'), may hold values from -6 to 6
- saved_out: bfloat16 [32768, 1280], P(('dp', 'ctx'), 'tp'), may hold values from -6 to 6
- cotangent: bfloat16 [32768, 1280], P(('dp', 'ctx'), 'tp'), may hold values from -24 to 24
- proj_weight: bfloat16 [1280, 1280], P('tp'), may hold values from -0.15625 to 0.15625
Outputs:
- query_grad: bfloat16 [32768, 1280], P(('dp', 'ctx'), 'tp')
- key_grad: bfloat16 [32768, 1280], P(('dp', 'ctx'), 'tp')
- value_grad: bfloat16 [32768, 1280], P(('dp', 'ctx'), 'tp')
- proj_grad: float32 [1280, 1280], P('tp', ('dp', 'ctx'))
Inputs may be any that keep to these rules, and one draw needn't show every extreme that they name: `keys`: keys of order one. `queries`: Queries; some rows may be far larger than others.
All inputs are finite; a program needn't handle non-finite values.
Results may differ from a plain program's by a relative error of at most 0.014.
Values may be sent and summed in bfloat16 or wider, within the bound.
No kernel may reach another device: no remote copies, remote signals or barrier semaphores. Data moves between devices by JAX's collectives and lax.ppermute only.
A program may use at most 64 MiB of HBM per device.

v0:
```python
import jax
import jax.numpy as jnp
from jax import lax
from jax.sharding import PartitionSpec as P

HD = 80


def split_heads(rows):
    return rows.reshape(rows.shape[0], rows.shape[1] // HD, HD)


def block_rows(number):
    size = number
    while size > 1024 and size % 2 == 0:
        size = size // 2
    return size


def on_device(queries, keys, values, saved_out, cotangent, proj_weight):
    factor = HD ** (-0.5)
    number = queries.shape[0]
    heads_here = queries.shape[1] // HD
    full_cot = lax.all_gather(cotangent, "tp", axis=1, tiled=True)
    d_attn = lax.dot_general(
        full_cot, proj_weight, (((1,), (1,)), ((), ())), preferred_element_type=jnp.float32
    ).astype(jnp.bfloat16)
    term = lax.dot_general(
        full_cot, saved_out, (((0,), (0,)), ((), ())), preferred_element_type=jnp.float32
    )
    proj_share = lax.psum_scatter(term, ("dp", "ctx"), scatter_dimension=0, tiled=True)
    proj_grad = proj_share.T
    query_heads = split_heads(queries)
    attn_heads = split_heads(d_attn)
    delta = jnp.sum(
        attn_heads.astype(jnp.float32) * split_heads(saved_out).astype(jnp.float32), axis=2
    )
    delta_heads = delta.T
    start_peak = jnp.full((heads_here, number), -jnp.inf, jnp.float32)
    start_total = jnp.zeros((heads_here, number), jnp.float32)
    zeros_grad = jnp.zeros((number, heads_here, HD), jnp.float32)
    key_local = split_heads(keys)
    value_local = split_heads(values)
    piece = lax.all_gather(keys, "ctx", axis=0, tiled=True)
    peak = start_peak
    total = start_total
    size = block_rows(piece.shape[0])
    for first in range(0, piece.shape[0], size):
        scores = (
            jnp.einsum(
                "thd,nhd->htn",
                query_heads,
                split_heads(piece[first : first + size]),
                preferred_element_type=jnp.float32,
            )
            * factor
        )
        higher = jnp.maximum(peak, jnp.max(scores, axis=2))
        total = total * jnp.exp(peak - higher) + jnp.sum(
            jnp.exp(scores - higher[:, :, None]), axis=2
        )
        peak = higher
    peak, total = (peak, total)
    lse = peak + jnp.log(total)
    all_lse, all_delta = (
        lax.all_gather(lse.T, "ctx", axis=0, tiled=True),
        lax.all_gather(delta, "ctx", axis=0, tiled=True),
    )
    carry = zeros_grad
    key_piece = lax.all_gather(keys, "ctx", axis=0, tiled=True)
    value_piece = lax.all_gather(values, "ctx", axis=0, tiled=True)
    size = block_rows(key_piece.shape[0])
    for first in range(0, key_piece.shape[0], size):
        key_split = split_heads(key_piece[first : first + size])
        value_split = split_heads(value_piece[first : first + size])
        scores = (
            jnp.einsum("thd,nhd->htn", query_heads, key_split, preferred_element_type=jnp.float32)
            * factor
        )
        prob = jnp.exp(scores - lse[:, :, None])
        dprob = jnp.einsum(
            "thd,nhd->htn", attn_heads, value_split, preferred_element_type=jnp.float32
        )
        dscore = (factor * prob * (dprob - delta_heads[:, :, None])).astype(jnp.bfloat16)
        carry = carry + jnp.einsum(
            "htn,nhd->thd", dscore, key_split, preferred_element_type=jnp.float32
        )
    key_acc = zeros_grad
    value_acc = zeros_grad
    query_piece = lax.all_gather(queries, "ctx", axis=0, tiled=True)
    attn_piece = lax.all_gather(d_attn, "ctx", axis=0, tiled=True)
    size = block_rows(query_piece.shape[0])
    for first in range(0, query_piece.shape[0], size):
        query_split = split_heads(query_piece[first : first + size])
        attn_split = split_heads(attn_piece[first : first + size])
        lse_block = all_lse[first : first + size].T
        delta_block = all_delta[first : first + size].T
        scores = (
            jnp.einsum("nhd,thd->hnt", query_split, key_local, preferred_element_type=jnp.float32)
            * factor
        )
        prob = jnp.exp(scores - lse_block[:, :, None])
        dprob = jnp.einsum(
            "nhd,thd->hnt", attn_split, value_local, preferred_element_type=jnp.float32
        )
        dscore = (factor * prob * (dprob - delta_block[:, :, None])).astype(jnp.bfloat16)
        key_acc = key_acc + jnp.einsum(
            "hnt,nhd->thd", dscore, query_split, preferred_element_type=jnp.float32
        )
        value_acc = value_acc + jnp.einsum(
            "hnt,nhd->thd",
            prob.astype(jnp.bfloat16),
            attn_split,
            preferred_element_type=jnp.float32,
        )
    key_grad = key_acc
    value_grad = value_acc
    key_grad = key_grad.reshape(number, -1)
    value_grad = value_grad.reshape(number, -1)
    return (
        carry.reshape(number, -1).astype(jnp.bfloat16),
        key_grad.astype(jnp.bfloat16),
        value_grad.astype(jnp.bfloat16),
        proj_grad,
    )


def solution(mesh):
    in_specs = (
        P(("dp", "ctx"), "tp"),
        P(("dp", "ctx"), "tp"),
        P(("dp", "ctx"), "tp"),
        P(("dp", "ctx"), "tp"),
        P(("dp", "ctx"), "tp"),
        P("tp", None),
    )
    out_specs = (
        P(("dp", "ctx"), "tp"),
        P(("dp", "ctx"), "tp"),
        P(("dp", "ctx"), "tp"),
        P("tp", ("dp", "ctx")),
    )
    return jax.shard_map(
        on_device, mesh=mesh, in_specs=in_specs, out_specs=out_specs, check_vma=False
    )
```

profile of v0, /device:TPU:32, one launch (start us, length us, event | category | flops | bytes accessed | tf_op | source)
XLA Modules:
  0.0 1469.2 jit_solution(6409432430538214902)
XLA Ops:
  8.0 0.0 copy-start
  8.0 0.0 copy-start.6
  8.0 0.0 all-reduce.3.cloned.1.call-start
  8.1 8.2 all_gather.23
  16.3 2.7 fusion.43
  19.0 0.0 copy-start.4
  19.0 0.0 all-reduce.3.cloned.1.call-update
  19.0 0.0 all-gather.5.cloned.1.call-start
  19.1 0.5 all-gather.5.cloned.1.call-update
  19.6 0.0 all-gather.7.cloned.1.call-start
  19.6 0.5 all-gather.7.cloned.1.call-update
  20.2 0.0 all-gather.9.cloned.1.call-start
  20.2 0.5 all-gather.9.cloned.1.call-update
  20.8 0.0 all-gather.11.cloned.1.call-start
  20.8 0.0 copy-done
  20.8 1.1 convolution_convert_fusion
  21.9 0.0 all-gather.11.cloned.1.call-update
  21.9 0.0 copy-done.6
  21.9 1.0 fusion.24
  22.9 30.8 %all_gather.28 = f32[2048,4]{0,1:T(4,128)S(1)} all-gather(f32[256,4]{0,1:T(4,128)S(1)} %fusion.24), channel_id=1, replica_groups=mesh['dp'=16,'ctx'=8,'tp'=4] {'ctx'}, dimensions={0}, use_global_device_ids=true | all-gather | bytes 36864 | tf_op jit(solution)/shard_map/all_gather | solution.py:67
  53.7 1.3 dynamic-slice
  55.6 1338.3 %all-reduce.3.cloned.1.call-done = f32[1280,320]{1,0:T(8,128)} async-done(((f32[1280,320]{1,0:T(8,128)}), f32[1280,320]{1,0:T(8,128)}) %all-reduce.3.cloned.1.call-update) | async-done | bytes 1638416
  1394.0 1.4 dynamic-slice_bitcast_fusion
  1395.3 0.0 all-gather.5.cloned.1.call-done
  1395.3 1.4 fusion.40
  1396.7 0.0 copy-done.4
  1396.7 0.8 multiply_reduce_fusion.1
  1397.6 0.0 copy-start.2
  1397.6 0.8 multiply_reduce_fusion
  1398.4 0.0 copy-start.1
  1398.4 1.8 exponential_reduce_fusion
  1400.2 0.0 copy-done.2
  1400.3 0.5 copy-done.1
  1400.8 24.6 %all_gather.26 = f32[2048,4]{0,1:T(4,128)S(1)} all-gather(f32[256,4]{0,1:T(4,128)S(1)} %fusion.26), channel_id=1, replica_groups=mesh['dp'=16,'ctx'=8,'tp'=4] {'ctx'}, dimensions={0}, use_global_device_ids=true | all-gather | bytes 36864 | tf_op jit(solution)/shard_map/all_gather | solution.py:66
  1425.4 0.0 all-gather.7.cloned.1.call-done
  1425.5 2.4 fusion.39
  1427.9 0.0 all-gather.9.cloned.1.call-done
  1427.9 0.0 copy-start.5
  1427.9 1.4 fusion.38
  1429.3 3.6 fusion.41
  1433.0 0.0 copy-done.5
  1433.0 2.7 fusion.42
  1435.7 5.1 fusion.12
  1440.8 5.0 fusion.23
  1445.8 0.0 all-gather.11.cloned.1.call-done
  1445.8 0.0 copy-start.3
  1445.8 1.5 fusion.37
  1447.4 2.9 fusion.2
  1450.3 0.0 copy-done.3
  1450.3 1.8 fusion.19
  1452.1 4.7 fusion.10
  1456.9 4.7 fusion.22
  (5 shorter events, 0.0 us)
Async XLA Ops:
  8.0 12.8 copy-start
  8.0 13.9 copy-start.6
  8.0 1385.9 %all-reduce.3.cloned.1.call-start = ((), (), s32[]{:S(2)}) async-start(), calls=%async_computation.4 | async-start | bytes 3932160
  19.0 1377.7 %copy-start.4 = (bf16[256,320]{0,1:T(8,128)(2,1)S(1)}, bf16[256,320]{0,1:T(8,128)(2,1)}, u32[]{:S(2)}) copy-start(bf16[256,320]{0,1:T(8,128)(2,1)} %param.6) | copy-start | bytes 491524
  19.0 1376.3 %all-gather.5.cloned.1.call-start = ((), (), s32[]{:S(2)}) async-start(), calls=%async_computation | async-start | bytes 1474560 | tf_op jit(solution)/shard_map/all_gather | solution.py:70
  19.6 1405.9 %all-gather.7.cloned.1.call-start = ((), (), s32[]{:S(2)}) async-start(), calls=%async_computation.1 | async-start | bytes 1474560 | tf_op jit(solution)/shard_map/all_gather | solution.py:71
  20.2 1407.7 %all-gather.9.cloned.1.call-start = ((), (), s32[]{:S(2)}) async-start(), calls=%async_computation.2 | async-start | bytes 1474560 | tf_op jit(solution)/shard_map/all_gather | solution.py:90
  20.8 1425.1 %all-gather.11.cloned.1.call-start = ((), (), s32[]{:S(2)}) async-start(), calls=%async_computation.3 | async-start | bytes 1474560 | tf_op jit(solution)/shard_map/all_gather | solution.py:91
  1397.6 2.7 copy-start.2
  1398.4 2.4 copy-start.1
  1427.9 5.1 copy-start.5
  1445.8 4.5 copy-start.3
Sparse Core Ops, SparseCore 0:
  19.1 1374.7 all-reduce.2
Sparse Core Ops, SparseCore 1:
  21.5 49.2 all-gather.4
  72.6 44.0 all-gather.6
  118.6 43.8 all-gather.8
  165.1 43.8 all-gather.10
where the time goes:
time: 1470 us
  waiting for transfers between devices  1340 us (91%)
  blocking collectives  63.7 us (4%)
  matrix products  36.1 us (2%)
  between operations  16.5 us (1%)
    unnamed x6, waiting for transfers between devices  1340 us
    all_gather x1, blocking collectives, on_device(): lax.all_gather(delta, 'ctx', axis=0, tiled=True)  30.8 us
  transfers between devices with their start and end apart: 5, of which 1 were waited for; matrix products, arithmetic and copies ran while one was open for 2% of the time, Pallas kernels for 0%

commit v1 on v0

v1 whole, which is shorter than its diff:
```python
import functools
import math

import jax
import jax.numpy as jnp
from jax import lax
from jax.experimental import pallas as pl
from jax.experimental.pallas import tpu as pltpu
from jax.sharding import PartitionSpec as P

HD = 80
HEADS_HERE = 4
SHARDS = 8
ROWS = 256
HALF = 128
WIDE = HEADS_HERE * HD
FACTOR = HD ** (-0.5)
LOG2E = math.log2(math.e)
Q_AT, G_AT, K_AT, V_AT, IN_ROWS = 0, 80, 176, 336, 496
EXT = 96
DK_AT, DV_AT, PG_AT, OUT_ROWS = 80, 240, 400, 448
PG_COLS = 10

NT = (((1,), (1,)), ((), ()))
TN = (((0,), (0,)), ((), ()))
NN = (((1,), (0,)), ((), ()))


def dot(left, right, dims):
    return lax.dot_general(left, right, dims, preferred_element_type=jnp.float32)


def turned(block):
    return block.astype(jnp.float32).T.astype(jnp.bfloat16)


def pack_kernel(q_ref, k_ref, v_ref, o_ref, cot_ref, w_ref, out_ref):
    grad = dot(w_ref[...], cot_ref[...], NT).astype(jnp.bfloat16)
    out_t = o_ref[...].astype(jnp.float32).T
    q_t, k_t, v_t = turned(q_ref[...]), turned(k_ref[...]), turned(v_ref[...])
    for j in range(HEADS_HERE):
        cols = slice(j * HD, (j + 1) * HD)
        g = grad[cols]
        delta = jnp.sum(g.astype(jnp.float32) * out_t[cols], axis=0, keepdims=True)
        high = delta.astype(jnp.bfloat16).astype(jnp.float32)
        rest = delta - high
        middle = rest.astype(jnp.bfloat16).astype(jnp.float32)
        low = rest - middle
        row = lax.broadcasted_iota(jnp.int32, (EXT - HD, ROWS), 0)
        extra = jnp.where(
            row == 0, high, jnp.where(row == 1, middle, jnp.where(row == 2, low, 0.0))
        ).astype(jnp.bfloat16)
        for h in range(2):
            slot = out_ref.at[h * HEADS_HERE + j]
            mine = slice(h * HALF, (h + 1) * HALF)
            slot[Q_AT : Q_AT + HD] = q_t[cols, mine]
            slot[G_AT : G_AT + HD] = g[:, mine]
            slot[G_AT + HD : G_AT + EXT] = extra[:, mine]
            for b in range(2):
                tokens = slice(b * HALF, (b + 1) * HALF)
                slot[K_AT + b * HD : K_AT + (b + 1) * HD] = k_t[cols, tokens]
                slot[V_AT + b * HD : V_AT + (b + 1) * HD] = v_t[cols, tokens]


def grad_kernel(x_ref, pg_ref, out_ref, k_t, v_t, dk, dv):
    for s in range(SHARDS):
        for b in range(2):
            tokens = slice((2 * s + b) * HALF, (2 * s + b + 1) * HALF)
            k_t[:, tokens] = x_ref[s, K_AT + b * HD : K_AT + (b + 1) * HD]
            v_t[:HD, tokens] = x_ref[s, V_AT + b * HD : V_AT + (b + 1) * HD]
    row = lax.broadcasted_iota(jnp.int32, (EXT - HD, SHARDS * ROWS), 0)
    v_t[HD:] = jnp.where(row < 3, -1.0, 0.0).astype(jnp.bfloat16)
    for i in range(SHARDS // 2):
        q = jnp.concatenate([x_ref[2 * i + e, Q_AT : Q_AT + HD] for e in range(2)], axis=1)
        g = jnp.concatenate([x_ref[2 * i + e, G_AT : G_AT + EXT] for e in range(2)], axis=1)
        scores = dot(q, k_t[...], TN)
        peak = jnp.max(scores, axis=1, keepdims=True) * (FACTOR * LOG2E)
        raised = jnp.exp2(scores * (FACTOR * LOG2E) - peak)
        prob = raised * (1.0 / jnp.sum(raised, axis=1, keepdims=True))
        shifted = dot(g, v_t[...], TN)
        dscore = (prob * shifted).astype(jnp.bfloat16)
        dv_part = dot(g[:HD], prob.astype(jnp.bfloat16), NN)
        dk_part = dot(q, dscore, NN)
        if i == 0:
            dv[...] = dv_part
            dk[...] = dk_part
        else:
            dv[...] += dv_part
            dk[...] += dk_part
        dq = (dot(k_t[...], dscore, NT) * FACTOR).astype(jnp.bfloat16)
        for e in range(2):
            out_ref[2 * i + e, :HD] = dq[:, e * HALF : (e + 1) * HALF]
    for s in range(SHARDS):
        for b in range(2):
            tokens = slice((2 * s + b) * HALF, (2 * s + b + 1) * HALF)
            at = b * HD
            out_ref[s, DK_AT + at : DK_AT + at + HD] = (dk[:, tokens] * FACTOR).astype(jnp.bfloat16)
            out_ref[s, DV_AT + at : DV_AT + at + HD] = dv[:, tokens].astype(jnp.bfloat16)
        out_ref[s, PG_AT:] = pg_ref[s]


def unpack_kernel(x_ref, dq_ref, dk_ref, dv_ref, pg_ref):
    def both(j, at):
        return x_ref[j, at : at + HD].astype(jnp.float32), x_ref[
            HEADS_HERE + j, at : at + HD
        ].astype(jnp.float32)

    def put(ref, heads):
        ref[...] = jnp.concatenate(heads, axis=0).T.astype(jnp.bfloat16)

    put(dq_ref, [jnp.concatenate(both(j, 0), axis=1) for j in range(HEADS_HERE)])
    for ref, start in ((dk_ref, DK_AT), (dv_ref, DV_AT)):
        heads = []
        for j in range(HEADS_HERE):
            low = both(j, start)
            high = both(j, start + HD)
            heads.append(jnp.concatenate([low[0] + low[1], high[0] + high[1]], axis=1))
        put(ref, heads)
    total = x_ref[0, PG_AT:].astype(jnp.float32)
    for s in range(1, SHARDS):
        total = total + x_ref[s, PG_AT:].astype(jnp.float32)
    wide = jnp.concatenate([total[16 * c : 16 * (c + 1)] for c in range(3)], axis=1)
    pg_ref[...] = wide.T[:WIDE, :PG_COLS]


def call(kernel, outs, flops, transcendentals=0, scratch=()):
    return pl.pallas_call(
        kernel,
        out_shape=outs,
        scratch_shapes=scratch,
        compiler_params=pltpu.CompilerParams(vmem_limit_bytes=48 * 1024 * 1024),
        cost_estimate=pl.CostEstimate(
            flops=flops, bytes_accessed=2 * 1024 * 1024, transcendentals=transcendentals
        ),
    )


def on_device(queries, keys, values, saved_out, cotangent, proj_weight):
    half = jnp.bfloat16
    full_cot = lax.all_gather(cotangent, "tp", axis=1, tiled=True)
    packed = call(
        pack_kernel,
        jax.ShapeDtypeStruct((SHARDS, IN_ROWS, HALF), half),
        2 * ROWS * WIDE * 4 * WIDE,
    )(queries, keys, values, saved_out, full_cot, proj_weight)
    arrived = lax.all_to_all(packed, "ctx", 0, 0, tiled=True)

    term = dot(full_cot, saved_out, TN).astype(half)
    along_y = [[2 * y + x for y in range(8)] for x in range(2)]
    share = lax.psum_scatter(
        term, "dp", scatter_dimension=0, tiled=True, axis_index_groups=along_y
    )
    upper = lax.axis_index("dp") % 2
    lower_part, upper_part = share[:80], share[80:]
    kept = jnp.where(upper == 1, upper_part, lower_part).astype(jnp.float32)
    given = jnp.where(upper == 1, lower_part, upper_part)
    taken = lax.ppermute(given, "dp", [(i, i ^ 1) for i in range(16)])
    share = (kept + taken.astype(jnp.float32)).astype(half)
    share = jnp.pad(share.reshape(SHARDS, PG_COLS, WIDE), ((0, 0), (0, 6), (0, 64)))
    share = share.reshape(SHARDS, 16, 3, HALF).transpose(0, 2, 1, 3)
    share = share.reshape(SHARDS, OUT_ROWS - PG_AT, HALF)

    tokens = SHARDS * ROWS
    sent = call(
        grad_kernel,
        jax.ShapeDtypeStruct((SHARDS, OUT_ROWS, HALF), half),
        5 * 2 * tokens * (tokens // 2) * HD,
        tokens * (tokens // 2),
        [
            pltpu.VMEM((HD, tokens), half),
            pltpu.VMEM((EXT, tokens), half),
            pltpu.VMEM((HD, tokens), jnp.float32),
            pltpu.VMEM((HD, tokens), jnp.float32),
        ],
    )(arrived, share)
    back = lax.all_to_all(sent, "ctx", 0, 0, tiled=True)
    grad = jax.ShapeDtypeStruct((ROWS, WIDE), half)
    return call(
        unpack_kernel,
        (grad, grad, grad, jax.ShapeDtypeStruct((WIDE, PG_COLS), jnp.float32)),
        0,
    )(back)


def solution(mesh):
    rows = P(("dp", "ctx"), "tp")
    return jax.shard_map(
        on_device,
        mesh=mesh,
        in_specs=(rows, rows, rows, rows, rows, P("tp", None)),
        out_specs=(rows, rows, rows, P("tp", ("dp", "ctx"))),
        check_vma=False,
    )
```

time: 1470 us -> 118 us (0.08)
  the two profiles are of different devices: /device:TPU:32 before, /device:TPU:4 now
where the time goes in v1:
time: 118 us
  waiting for transfers between devices  36.7 us (31%)
  blocking collectives  35.9 us (30%)
  between operations  14.2 us (12%)
  starting transfers between devices  12.8 us (11%)
  Pallas kernels  9.01 us (8%)
  local copies, waits for them, and re-layouts  5.24 us (4%)
  matrix products  2.44 us (2%)
  other arithmetic  1.76 us (1%)
    reduce_scatter x1, waiting for transfers between devices, on_device(): lax.psum_scatter(term, 'dp', scatter_dimension=0, tiled=True, axis_index_...  31.6 us
    all_to_all x1, blocking collectives, on_device(): back = lax.all_to_all(sent, 'ctx', 0, 0, tiled=True)  28.1 us
    all_to_all x1, starting transfers between devices, on_device(): arrived = lax.all_to_all(packed, 'ctx', 0, 0, tiled=True)  10.3 us
    all_gather x1, blocking collectives, on_device(): full_cot = lax.all_gather(cotangent, 'tp', axis=1, tiled=True)  7.8 us
    pallas_call x1, Pallas kernels, on_device(): call(grad_kernel, jax.ShapeDtypeStruct((SHARDS, OUT_ROWS, HALF), half), 5...  7.3 us
    ppermute x1, waiting for transfers between devices, on_device(): taken = lax.ppermute(given, 'dp', [(i, i ^ 1) for i in range(16)])  5.14 us
    pallas_call x4, local copies, waits for them, and re-layouts, on_device(): call(unpack_kernel, (grad, grad, grad, jax.ShapeDtypeStruct((WIDE, PG_COL...  3.12 us
    ppermute x1, starting transfers between devices, on_device(): taken = lax.ppermute(given, 'dp', [(i, i ^ 1) for i in range(16)])  2.48 us
  transfers between devices with their start and end apart: 3, of which 2 were waited for; matrix products, arithmetic and copies ran while one was open for 2% of the time, Pallas kernels for 1%

profile of v1, /device:TPU:4, one launch (start us, length us, event | category | flops | bytes accessed | tf_op | source)
XLA Modules:
  0.0 118.1 jit_solution(6136658535096245378)
XLA Ops:
  7.2 0.0 reduce-scatter.2.cloned.1.call-start
  7.2 7.8 %all_gather.3 = bf16[256,1280]{0,1:T(8,128)(2,1)S(1)} all-gather(bf16[256,320]{0,1:T(8,128)(2,1)} %param.10), channel_id=1, replica_groups=mesh['dp'=16,'ctx'=8,'tp'=4] {'tp'}, dimensions={1}, use_global_device_ids=true | all-gather | bytes 819200 | tf_op jit(solution)/shard_map/all_gather | solution.py:140
  15.0 2.4 %convolution_convert_fusion = bf16[1280,320]{1,0:T(8,128)(2,1)} fusion(bf16[256,1280]{0,1:T(8,128)(2,1)S(1)} %all_gather.3, bf16[256,320]{0,1:T(8,128)(2,1)} %param.9), kind=kOutput, calls=%fused_computation | convolution fusion | flops 210124800 | bytes 1638400 | tf_op jit(solution)/shard_map/dot_general | solution.py:30
  17.4 0.0 copy-start.1
  17.5 0.0 reduce-scatter.2.cloned.1.call-update
  17.5 0.0 copy-start.2
  17.5 0.0 copy-start.3
  17.5 0.0 copy-start.4
  17.5 0.2 copy.33.cot_ref
  17.8 0.6 copy-done.1
  18.4 0.0 copy-start
  18.4 0.2 copy.32.o_ref
  18.5 0.0 copy-done.2
  18.5 0.2 copy.29.q_ref
  18.7 0.0 copy-done.3
  18.7 0.2 copy.30.k_ref
  18.9 0.0 copy-done.4
  18.9 0.2 copy.31.v_ref
  19.1 0.5 copy-done
  19.6 1.4 %shard_map.93 = bf16[8,496,128]{2,1,0:T(8,128)(2,1)} custom-call(bf16[256,320]{1,0:T(8,128)(2,1)S(1)} %copy.29.q_ref, bf16[256,320]{1,0:T(8,128)(2,1)S(1)} %copy.30.k_ref, bf16[256,320]{1,0:T(8,128)(2,1)S(1)} %copy.31.v_ref, bf16[256,320]{1,0:T(8,128)(2,1)S(1)} %copy.32.o_ref, bf16[256,1280]{1,0:T(8,128)(2,1)S(1)} %copy.33.cot_ref, bf16[320,1280]{1,0:T(8,128)(2,1)S(1)} %copy-done), custom_call_target="tpu_custom_call" | custom-call | flops 209715200 | bytes 2097152 | tf_op jit(solution)/shard_map/pallas_call | solution.py:141
  21.0 10.3 %all-to-all-start = ((bf16[8,496,128]{2,1,0:T(8,128)(2,1)}), bf16[8,496,128]{2,1,0:T(8,128)(2,1)S(1)}, u32[]{:S(2)}, u32[]{:S(2)}) async-start(bf16[8,496,128]{2,1,0:T(8,128)(2,1)} %shard_map.93), calls=%async_computation | async-start | bytes 2031616 | tf_op jit(solution)/shard_map/all_to_all | solution.py:146
  31.3 31.6 %reduce-scatter.2.cloned.1.call-done = bf16[160,320]{1,0:T(8,128)(2,1)} async-done(((bf16[1280,320]{1,0:T(8,128)(2,1)}), bf16[160,320]{1,0:T(8,128)(2,1)}) %reduce-scatter.2.cloned.1.call-update) | async-done | bytes 102416 | tf_op jit(solution)/shard_map/reduce_scatter | solution.py:150
  62.9 0.9 broadcast_select_fusion
  63.8 2.5 %collective-permute-start = (bf16[80,320]{1,0:T(8,128)(2,1)S(1)}, bf16[80,320]{1,0:T(8,128)(2,1)S(1)}, u32[]{:S(2)}, u32[]{:S(2)}) collective-permute-start(bf16[80,320]{1,0:T(8,128)(2,1)S(1)} %broadcast_select_fusion), channel_id=1, source_target_pairs={{0,32},{32,0},{64,96},{96,64},{128,160},{160,128},{192,224},{224,1... | collective-permute-start | bytes 153608 | tf_op jit(solution)/shard_map/ppermute | solution.py:157
  66.2 5.1 %collective-permute-done = bf16[80,320]{1,0:T(8,128)(2,1)S(1)} collective-permute-done((bf16[80,320]{1,0:T(8,128)(2,1)S(1)}, bf16[80,320]{1,0:T(8,128)(2,1)S(1)}, u32[]{:S(2)}, u32[]{:S(2)}) %collective-permute-start) | collective-permute-done | bytes 51232 | tf_op jit(solution)/shard_map/ppermute | solution.py:157
  71.4 0.9 add_convert_fusion
  72.4 0.0 all-to-all-done.x_ref
  72.4 7.3 %shard_map.94 = bf16[8,448,128]{2,1,0:T(8,128)(2,1)S(1)} custom-call(bf16[8,496,128]{2,1,0:T(8,128)(2,1)S(1)} %all-to-all-done.x_ref, bf16[8,48,128]{2,1,0:T(8,128)(2,1)S(1)} %bitcast.4), custom_call_target="tpu_custom_call" | custom-call | flops 1677721600 | bytes 2097152 | tf_op jit(solution)/shard_map/pallas_call | solution.py:164
  79.7 28.1 %all_to_all.10.x_ref = bf16[8,448,128]{2,1,0:T(8,128)(2,1)S(1)} all-to-all(bf16[8,448,128]{2,1,0:T(8,128)(2,1)S(1)} %shard_map.94), channel_id=1, replica_groups=mesh['dp'=16,'ctx'=8,'tp'=4] {'ctx'}, dimensions={0} | all-to-all | bytes 1835008 | tf_op jit(solution)/shard_map/all_to_all | solution.py:176
  107.9 0.3 shard_map.95
  108.1 0.8 copy.35
  108.9 0.8 copy.36
  109.7 0.8 copy.37
  110.5 0.7 copy.38
  (4 shorter events, 0.1 us)
Async XLA Ops:
  7.2 55.7 %reduce-scatter.2.cloned.1.call-start = ((), (), s32[]{:S(2)}) async-start(), calls=%async_computation.3 | async-start | bytes 1105920 | tf_op jit(solution)/shard_map/reduce_scatter | solution.py:150
  17.4 0.9 copy-start.1
  17.5 1.1 copy-start.2
  17.5 1.2 %copy-start.3 = (bf16[256,320]{0,1:T(8,128)(2,1)S(1)}, bf16[256,320]{0,1:T(8,128)(2,1)}, u32[]{:S(2)}) copy-start(bf16[256,320]{0,1:T(8,128)(2,1)} %param.7) | copy-start | bytes 491524
  17.5 1.4 %copy-start.4 = (bf16[256,320]{0,1:T(8,128)(2,1)S(1)}, bf16[256,320]{0,1:T(8,128)(2,1)}, u32[]{:S(2)}) copy-start(bf16[256,320]{0,1:T(8,128)(2,1)} %param.8) | copy-start | bytes 491524
  18.4 1.2 %copy-start = (bf16[320,1280]{1,0:T(8,128)(2,1)S(1)}, bf16[320,1280]{1,0:T(8,128)(2,1)}, u32[]{:S(2)}) copy-start(bf16[320,1280]{1,0:T(8,128)(2,1)} %w_ref.1) | copy-start | bytes 2457604
  21.0 51.4 %all-to-all-start = ((bf16[8,496,128]{2,1,0:T(8,128)(2,1)}), bf16[8,496,128]{2,1,0:T(8,128)(2,1)S(1)}, u32[]{:S(2)}, u32[]{:S(2)}) async-start(bf16[8,496,128]{2,1,0:T(8,128)(2,1)} %shard_map.93), calls=%async_computation | async-start | bytes 2031616 | tf_op jit(solution)/shard_map/all_to_all | solution.py:146
  63.8 7.6 %collective-permute-start = (bf16[80,320]{1,0:T(8,128)(2,1)S(1)}, bf16[80,320]{1,0:T(8,128)(2,1)S(1)}, u32[]{:S(2)}, u32[]{:S(2)}) collective-permute-start(bf16[80,320]{1,0:T(8,128)(2,1)S(1)} %broadcast_select_fusion), channel_id=1, source_target_pairs={{0,32},{32,0},{64,96},{96,64},{128,160},{160,128},{192,224},{224,1... | collective-permute-start | bytes 153608 | tf_op jit(solution)/shard_map/ppermute | solution.py:157
Sparse Core Ops, SparseCore 0:
  17.6 45.2 reduce-scatter.1

commit v2 on v1

v2 whole, which is shorter than its diff:
```python
import math

import jax
import jax.numpy as jnp
from jax import lax
from jax.experimental import pallas as pl
from jax.experimental.pallas import tpu as pltpu
from jax.sharding import PartitionSpec as P

HD = 80
HEADS_HERE = 4
SHARDS = 8
DP = 16
ROWS = 256
HALF = 128
WIDE = HEADS_HERE * HD
FACTOR = HD ** (-0.5)
LOG2E = math.log2(math.e)
EXT = 96
QG_ROWS = HD + EXT
K_AT, V_AT, KV_ROWS = 0, 2 * HD, 4 * HD
PG_AT, OUT_ROWS = 4 * HD, 4 * HD + 48
PG_COLS = 10
PG_ROWS = 80
PG_USED = 208
NEAR = (0, 6, 1, 7)

NT = (((1,), (1,)), ((), ()))
TN = (((0,), (0,)), ((), ()))
NN = (((1,), (0,)), ((), ()))


def dot(left, right, dims):
    return lax.dot_general(left, right, dims, preferred_element_type=jnp.float32)


def pack_keys_kernel(k_hbm, v_hbm, out_ref, k_ref, v_ref, sems):
    pairs = ((k_hbm, k_ref), (v_hbm, v_ref))
    copies = [pltpu.make_async_copy(x, y, sems.at[i]) for i, (x, y) in enumerate(pairs)]
    for copy in copies:
        copy.start()
    for copy, ref, first in zip(copies, (k_ref, v_ref), (K_AT, V_AT)):
        copy.wait()
        for s in range(SHARDS):
            j = s % HEADS_HERE
            for b in range(2):
                at = first + b * HD
                out_ref[s, at : at + HD] = ref[j * HD : (j + 1) * HD, b * HALF : (b + 1) * HALF]


def pack_queries_and_proj_kernel(q_hbm, o_hbm, cot_ref, w_ref, *refs):
    out_refs, (out_ref, q_ref, o_ref, g_ref, extra_ref, sems) = refs[: len(NEAR)], refs[len(NEAR) :]
    pairs = ((q_hbm, q_ref), (o_hbm, o_ref))
    copies = [pltpu.make_async_copy(x, y, sems.at[i]) for i, (x, y) in enumerate(pairs)]
    for copy in copies:
        copy.start()
    g_ref[...] = dot(w_ref[...], cot_ref[...], NN).astype(jnp.bfloat16)
    for copy in copies:
        copy.wait()
    for j in range(HEADS_HERE):
        cols = slice(j * HD, (j + 1) * HD)
        delta = jnp.sum(
            g_ref[cols].astype(jnp.float32) * o_ref[cols].astype(jnp.float32),
            axis=0,
            keepdims=True,
        )
        high = delta.astype(jnp.bfloat16).astype(jnp.float32)
        rest = delta - high
        middle = rest.astype(jnp.bfloat16).astype(jnp.float32)
        low = rest - middle
        row = lax.broadcasted_iota(jnp.int32, (EXT - HD, ROWS), 0)
        extra = jnp.where(
            row == 0, high, jnp.where(row == 1, middle, jnp.where(row == 2, low, 0.0))
        )
        extra_ref[j * (EXT - HD) : (j + 1) * (EXT - HD)] = extra.astype(jnp.bfloat16)
    here = lax.axis_index("ctx")
    for away, ref in zip(NEAR, out_refs):
        j = lax.rem(here + away, HEADS_HERE)
        cols = pl.ds(pl.multiple_of(j * HD, 16), HD)
        ref[:HD] = q_ref[cols]
        ref[HD : 2 * HD] = g_ref[cols]
        rows = pl.ds(pl.multiple_of(j * (EXT - HD), 16), EXT - HD)
        ref[2 * HD :] = extra_ref[rows]
    empty = jnp.zeros((PG_USED - 200, HALF), jnp.float32)
    for d in range(DP):
        part = dot(cot_ref[d * PG_ROWS : (d + 1) * PG_ROWS], o_ref[...], NT)
        for c in range(2):
            at = c * PG_ROWS
            out_ref[d, at : at + PG_ROWS] = part[:, HALF * c : HALF * (c + 1)].astype(out_ref.dtype)
        last = part[:, 2 * HALF :]
        last = jnp.concatenate([last[: PG_ROWS // 2], last[PG_ROWS // 2 :]], axis=1)
        out_ref[d, 2 * PG_ROWS :] = jnp.concatenate([last, empty], axis=0).astype(out_ref.dtype)


def add_share_kernel(parts_ref, sent_in_ref, sent_ref, pieces, sem):
    total = parts_ref[0].astype(jnp.float32)
    for k in range(1, DP):
        total = total + parts_ref[k].astype(jnp.float32)
    for s in range(SHARDS):
        last = total[2 * PG_ROWS + s % 4 * PG_COLS :][:PG_COLS]
        last = last[:, s // 4 * 64 :][:, :64]
        blocks = [total[c * PG_ROWS + s * PG_COLS :][:PG_COLS] for c in range(2)]
        blocks.append(jnp.concatenate([last, jnp.zeros_like(last)], axis=1))
        for c, block in enumerate(blocks):
            block = jnp.concatenate([block, jnp.zeros((6, HALF), jnp.float32)], axis=0)
            pieces[s, 16 * c : 16 * (c + 1)] = block.astype(jnp.bfloat16)
    copy = pltpu.make_async_copy(pieces, sent_ref.at[:, pl.ds(PG_AT, OUT_ROWS - PG_AT)], sem)
    copy.start()
    copy.wait()


def grad_kernel(x_ref, *refs):
    near, (out_ref, *dq_refs) = refs[: len(NEAR)], refs[len(NEAR) : 2 * len(NEAR) + 1]
    k_t, v_t, dk, dv = refs[2 * len(NEAR) + 1 :]
    for s in range(SHARDS):
        for b in range(2):
            tokens = slice((2 * s + b) * HALF, (2 * s + b + 1) * HALF)
            k_t[:, tokens] = x_ref[s, K_AT + b * HD : K_AT + (b + 1) * HD]
            v_t[:HD, tokens] = x_ref[s, V_AT + b * HD : V_AT + (b + 1) * HD]
    row = lax.broadcasted_iota(jnp.int32, (EXT - HD, SHARDS * ROWS), 0)
    v_t[HD:] = jnp.where(row < 3, -1.0, 0.0).astype(jnp.bfloat16)
    for i, (block, dq_ref) in enumerate(zip(near, dq_refs)):
        q, g = block[:HD], block[HD:]
        scores = dot(q, k_t[...], TN)
        peak = jnp.max(scores, axis=1, keepdims=True) * (FACTOR * LOG2E)
        raised = jnp.exp2(scores * (FACTOR * LOG2E) - peak)
        prob = raised * (1.0 / jnp.sum(raised, axis=1, keepdims=True))
        shifted = dot(g, v_t[...], TN)
        dscore = (prob * shifted).astype(jnp.bfloat16)
        dv_part = dot(g[:HD], prob.astype(jnp.bfloat16), NN)
        dk_part = dot(q, dscore, NN)
        if i == 0:
            dv[...] = dv_part
            dk[...] = dk_part
        else:
            dv[...] += dv_part
            dk[...] += dk_part
        dq_ref[...] = (dot(k_t[...], dscore, NT) * FACTOR).astype(jnp.bfloat16)
    for s in range(SHARDS):
        for b in range(2):
            tokens = slice((2 * s + b) * HALF, (2 * s + b + 1) * HALF)
            at = b * HD
            out_ref[s, K_AT + at : K_AT + at + HD] = (dk[:, tokens] * FACTOR).astype(jnp.bfloat16)
            out_ref[s, V_AT + at : V_AT + at + HD] = dv[:, tokens].astype(jnp.bfloat16)


def unpack_kernel(x_ref, *refs):
    near, (dq_ref, dk_ref, dv_ref, pg_ref) = refs[: len(NEAR)], refs[len(NEAR) :]
    here = lax.axis_index("ctx")
    for away, ref in zip(NEAR, near):
        j = lax.rem(here + away, HEADS_HERE)
        dq_ref[pl.ds(pl.multiple_of(j * HD, 16), HD)] = ref[...]
    for j in range(HEADS_HERE):
        for ref, start in ((dk_ref, K_AT), (dv_ref, V_AT)):
            for b in range(2):
                rows = slice(start + b * HD, start + (b + 1) * HD)
                total = x_ref[j, rows].astype(jnp.float32)
                total = total + x_ref[HEADS_HERE + j, rows].astype(jnp.float32)
                total = total.astype(jnp.bfloat16)
                ref[j * HD : (j + 1) * HD, b * HALF : (b + 1) * HALF] = total
    total = x_ref[0, PG_AT:].astype(jnp.float32)
    for s in range(1, SHARDS):
        total = total + x_ref[s, PG_AT:].astype(jnp.float32)
    wide = jnp.concatenate([total[16 * c : 16 * (c + 1)] for c in range(3)], axis=1)
    pg_ref[...] = wide[:PG_COLS, :WIDE]


def call(kernel, outs, flops, transcendentals=0, scratch=(), mib=48, **more):
    return pl.pallas_call(
        kernel,
        out_shape=outs,
        scratch_shapes=scratch,
        compiler_params=pltpu.CompilerParams(vmem_limit_bytes=mib * 1024 * 1024),
        cost_estimate=pl.CostEstimate(
            flops=flops, bytes_accessed=2 * 1024 * 1024, transcendentals=transcendentals
        ),
        **more,
    )


def shifted_round(x, away):
    return lax.ppermute(x, "ctx", [(z, (z + away) % SHARDS) for z in range(SHARDS)])


def on_device(queries, keys, values, saved_out, cotangent, proj_weight):
    half, single = jnp.bfloat16, jnp.float32
    shape = jax.ShapeDtypeStruct
    vmem, anywhere = pl.BlockSpec(memory_space=pltpu.VMEM), pl.BlockSpec(memory_space=pl.ANY)
    whole = pltpu.VMEM((WIDE, ROWS), half)
    q, k, v, o, cot = (x.T for x in (queries, keys, values, saved_out, cotangent))

    pairs = call(
        pack_keys_kernel,
        shape((SHARDS, KV_ROWS, HALF), half),
        0,
        scratch=[whole] * 2 + [pltpu.SemaphoreType.DMA((2,))],
        in_specs=[anywhere] * 2,
        mib=60,
    )(k, v)
    pairs = lax.all_to_all(pairs, "ctx", 0, 0, tiled=True)

    full_cot = lax.all_gather(cot, "tp", axis=0, tiled=True)
    flops = 2 * ROWS * WIDE * 4 * WIDE
    *near, parts = call(
        pack_queries_and_proj_kernel,
        [shape((QG_ROWS, ROWS), half)] * len(NEAR) + [shape((DP, PG_USED, HALF), half)],
        2 * flops,
        scratch=[whole] * 3
        + [pltpu.VMEM((HEADS_HERE * (EXT - HD), ROWS), half), pltpu.SemaphoreType.DMA((2,))],
        in_specs=[anywhere] * 2 + [vmem] * 2,
        mib=48,
    )(q, o, full_cot, proj_weight)
    near = [near[0]] + [shifted_round(x, away) for away, x in zip(NEAR[1:], near[1:])]
    parts = lax.all_to_all(parts, "dp", 0, 0, tiled=True)

    tokens = SHARDS * ROWS
    sent, *dq = call(
        grad_kernel,
        [shape((SHARDS, OUT_ROWS, HALF), half)]
        + [shape((HD, ROWS), half)] * len(NEAR),
        5 * 2 * tokens * (tokens // 2) * HD,
        tokens * (tokens // 2),
        [
            pltpu.VMEM((HD, tokens), half),
            pltpu.VMEM((EXT, tokens), half),
            pltpu.VMEM((HD, tokens), single),
            pltpu.VMEM((HD, tokens), single),
        ],
    )(pairs, *near)
    sent = call(
        add_share_kernel,
        shape(sent.shape, half),
        0,
        scratch=[
            pltpu.VMEM((SHARDS, OUT_ROWS - PG_AT, HALF), half),
            pltpu.SemaphoreType.DMA,
        ],
        in_specs=[vmem, anywhere],
        out_specs=anywhere,
        input_output_aliases={1: 0},
    )(parts, sent)
    back = lax.all_to_all(sent, "ctx", 0, 0, tiled=True)
    dq = [dq[0]] + [shifted_round(x, -away) for away, x in zip(NEAR[1:], dq[1:])]
    grad = shape((WIDE, ROWS), half)
    outs = call(unpack_kernel, (grad, grad, grad, shape((PG_COLS, WIDE), single)), 0)(back, *dq)
    return tuple(x.T for x in outs)


def solution(mesh):
    rows = P(("dp", "ctx"), "tp")
    return jax.shard_map(
        on_device,
        mesh=mesh,
        in_specs=(rows, rows, rows, rows, rows, P("tp", None)),
        out_specs=(rows, rows, rows, P("tp", ("dp", "ctx"))),
        check_vma=False,
    )
```

time: 118 us -> 96 us (0.81)
  the two profiles are of different devices: /device:TPU:4 before, /device:TPU:24 now
where the time goes in v2:
time: 96 us; the launch traced here: 95.5 us
  starting transfers between devices  43.7 us (46%)
  waiting for transfers between devices  28.7 us (30%)
  Pallas kernels  14.3 us (15%)
  blocking collectives  8.02 us (8%)
    ppermute x6, starting transfers between devices, shifted_round(): lax.ppermute(x, 'ctx', [(z, (z + away) % SHARDS) for z in range(SHARDS)])  19.9 us
    ppermute x6, waiting for transfers between devices, shifted_round(): lax.ppermute(x, 'ctx', [(z, (z + away) % SHARDS) for z in range(SHARDS)])  15 us
    all_to_all x1, starting transfers between devices, on_device(): pairs = lax.all_to_all(pairs, 'ctx', 0, 0, tiled=True)  10.5 us
    all_to_all x1, starting transfers between devices, on_device(): parts = lax.all_to_all(parts, 'dp', 0, 0, tiled=True)  9.8 us
    all_to_all x1, waiting for transfers between devices, on_device(): pairs = lax.all_to_all(pairs, 'ctx', 0, 0, tiled=True)  9.21 us
    all_gather x1, blocking collectives, on_device(): full_cot = lax.all_gather(cot, 'tp', axis=0, tiled=True)  8.02 us
    pallas_call x1, Pallas kernels, on_device(): call(grad_kernel, [shape((SHARDS, OUT_ROWS, HALF), half)] + [shape((HD, R...  7.69 us
    all_to_all x1, waiting for transfers between devices, on_device(): parts = lax.all_to_all(parts, 'dp', 0, 0, tiled=True)  4.43 us
  transfers between devices with their start and end apart: 9, of which 5 were waited for; matrix products, arithmetic and copies ran while one was open for 0% of the time, Pallas kernels for 11%

profile of v2, /device:TPU:24, one launch (start us, length us, event | category | flops | bytes accessed | tf_op | source)
XLA Modules:
  0.0 95.5 jit_solution(2201339590742837786)
XLA Ops:
  0.6 1.9 %shard_map.94 = bf16[8,320,128]{2,1,0:T(8,128)(2,1)} custom-call(bf16[320,256]{1,0:T(8,128)(2,1)} %bitcast.12, bf16[320,256]{1,0:T(8,128)(2,1)} %bitcast.13), custom_call_target="tpu_custom_call" | custom-call | bytes 2097152 | tf_op jit(solution)/shard_map/pallas_call | solution.py:192
  2.6 0.0 copy-start.3
  2.6 0.0 copy-start
  2.6 10.5 %all-to-all-start.1 = ((bf16[8,320,128]{2,1,0:T(8,128)(2,1)}), bf16[8,320,128]{2,1,0:T(8,128)(2,1)S(1)}, u32[]{:S(2)}, u32[]{:S(2)}) async-start(bf16[8,320,128]{2,1,0:T(8,128)(2,1)} %shard_map.94), calls=%async_computation.1 | async-start | bytes 1310720 | tf_op jit(solution)/shard_map/all_to_all | solution.py:200
  13.1 0.0 copy-done.3
  13.1 0.0 copy-start.1
  13.1 0.0 copy-start.2
  13.1 8.0 %all_gather.3.cot_ref = bf16[1280,256]{1,0:T(8,128)(2,1)S(1)} all-gather(bf16[320,256]{1,0:T(8,128)(2,1)S(1)} %bitcast.11), channel_id=1, replica_groups=mesh['dp'=16,'ctx'=8,'tp'=4] {'tp'}, dimensions={0}, use_global_device_ids=true | all-gather | bytes 819200 | tf_op jit(solution)/shard_map/all_gather | solution.py:202
  21.1 0.0 copy-done
  21.1 0.0 copy-done.1
  21.1 0.0 copy-done.2
  21.1 3.0 %shard_map.93 = (bf16[176,256]{1,0:T(8,128)(2,1)S(1)}, bf16[176,256]{1,0:T(8,128)(2,1)S(1)}, bf16[176,256]{1,0:T(8,128)(2,1)S(1)}, bf16[176,256]{1,0:T(8,128)(2,1)S(1)}, bf16[16,208,128]{2,1,0:T(8,128)(2,1)}) custom-call(bf16[320,256]{1,0:T(8,128)(2,1)S(1)} %bitcast.9, bf16[320,256]{1,0:T(8,128)(2,1)S(1)} %bitcast.10, ...), custom_call_target="tpu_custom_call" | custom-call | flops 419430400 | bytes 2097152 | tf_op jit(solution)/shard_map/pallas_call | solution.py:204
  24.2 9.2 %all-to-all-done.1.x_ref = bf16[8,320,128]{2,1,0:T(8,128)(2,1)S(1)} async-done(((bf16[8,320,128]{2,1,0:T(8,128)(2,1)}), bf16[8,320,128]{2,1,0:T(8,128)(2,1)S(1)}, u32[]{:S(2)}, u32[]{:S(2)}) %all-to-all-start.1) | async-done | bytes 655392 | tf_op jit(solution)/shard_map/all_to_all | solution.py:200
  33.4 9.8 %all-to-all-start = ((bf16[16,208,128]{2,1,0:T(8,128)(2,1)}), bf16[16,208,128]{2,1,0:T(8,128)(2,1)S(1)}, u32[]{:S(2)}, u32[]{:S(2)}) async-start(bf16[16,208,128]{2,1,0:T(8,128)(2,1)} %get-tuple-element.18), calls=%async_computation | async-start | bytes 1703936 | tf_op jit(solution)/shard_map/all_to_all | solution.py:214
  43.2 2.2 %collective-permute-start = (bf16[176,256]{1,0:T(8,128)(2,1)S(1)}, bf16[176,256]{1,0:T(8,128)(2,1)S(1)}, u32[]{:S(2)}, u32[]{:S(2)}) collective-permute-start(bf16[176,256]{1,0:T(8,128)(2,1)S(1)} %get-tuple-element.20), channel_id=1, source_target_pairs={{0,24},{4,28},{8,0},{12,4},{16,8},{20,12},{24,16},{28,20},{1,25},{... | collective-permute-start | bytes 270344 | tf_op jit(solution)/shard_map/ppermute | solution.py:182
  45.4 2.1 %collective-permute-start.1 = (bf16[176,256]{1,0:T(8,128)(2,1)S(1)}, bf16[176,256]{1,0:T(8,128)(2,1)S(1)}, u32[]{:S(2)}, u32[]{:S(2)}) collective-permute-start(bf16[176,256]{1,0:T(8,128)(2,1)S(1)} %get-tuple-element.21), channel_id=1, source_target_pairs={{0,4},{4,8},{8,12},{12,16},{16,20},{20,24},{24,28},{28,0},{1,5},{5... | collective-permute-start | bytes 270344 | tf_op jit(solution)/shard_map/ppermute | solution.py:182
  47.6 4.9 %collective-permute-start.2 = (bf16[176,256]{1,0:T(8,128)(2,1)S(1)}, bf16[176,256]{1,0:T(8,128)(2,1)S(1)}, u32[]{:S(2)}, u32[]{:S(2)}) collective-permute-start(bf16[176,256]{1,0:T(8,128)(2,1)S(1)} %get-tuple-element.22), channel_id=1, source_target_pairs={{0,28},{4,0},{8,4},{12,8},{16,12},{20,16},{24,20},{28,24},{1,29},{... | collective-permute-start | bytes 270344 | tf_op jit(solution)/shard_map/ppermute | solution.py:182
  52.5 0.0 collective-permute-done.refs_1_
  52.5 0.6 collective-permute-done.1.refs_2_
  53.1 1.8 %collective-permute-done.2.refs_3_ = bf16[176,256]{1,0:T(8,128)(2,1)S(1)} collective-permute-done((bf16[176,256]{1,0:T(8,128)(2,1)S(1)}, bf16[176,256]{1,0:T(8,128)(2,1)S(1)}, u32[]{:S(2)}, u32[]{:S(2)}) %collective-permute-start.2) | collective-permute-done | bytes 90144 | tf_op jit(solution)/shard_map/ppermute | solution.py:182
  54.9 7.7 %shard_map.95 = (bf16[8,368,128]{2,1,0:T(8,128)(2,1)}, bf16[80,256]{1,0:T(8,128)(2,1)S(1)}, bf16[80,256]{1,0:T(8,128)(2,1)S(1)}, bf16[80,256]{1,0:T(8,128)(2,1)S(1)}, bf16[80,256]{1,0:T(8,128)(2,1)S(1)}) custom-call(bf16[8,320,128]{2,1,0:T(8,128)(2,1)S(1)} %all-to-all-done.1.x_ref, bf16[176,256]{1,0:T(8,128)(2,1)S(1)} %get-tuple-element.19.refs_0_, ...), custom_call_target="tpu_custom_call" | custom-call | flops 1677721600 | bytes 2097152 | tf_op jit(solution)/shard_map/pallas_call | solution.py:217
  62.6 4.4 %all-to-all-done.parts_ref = bf16[16,208,128]{2,1,0:T(8,128)(2,1)S(1)} async-done(((bf16[16,208,128]{2,1,0:T(8,128)(2,1)}), bf16[16,208,128]{2,1,0:T(8,128)(2,1)S(1)}, u32[]{:S(2)}, u32[]{:S(2)}) %all-to-all-start) | async-done | bytes 852000 | tf_op jit(solution)/shard_map/all_to_all | solution.py:214
  67.0 0.8 shard_map.96
  67.8 3.6 %all-to-all-start.2 = ((bf16[8,368,128]{2,1,0:T(8,128)(2,1)}), bf16[8,368,128]{2,1,0:T(8,128)(2,1)S(1)}, u32[]{:S(2)}, u32[]{:S(2)}) async-start(bf16[8,368,128]{2,1,0:T(8,128)(2,1)} %shard_map.96), calls=%async_computation.2 | async-start | bytes 1507328 | tf_op jit(solution)/shard_map/all_to_all | solution.py:242
  71.4 4.7 %collective-permute-start.3 = (bf16[80,256]{1,0:T(8,128)(2,1)S(1)}, bf16[80,256]{1,0:T(8,128)(2,1)S(1)}, u32[]{:S(2)}, u32[]{:S(2)}) collective-permute-start(bf16[80,256]{1,0:T(8,128)(2,1)S(1)} %get-tuple-element.25), channel_id=1, source_target_pairs={{0,8},{4,12},{8,16},{12,20},{16,24},{20,28},{24,0},{28,4},{1,9},{5... | collective-permute-start | bytes 122888 | tf_op jit(solution)/shard_map/ppermute | solution.py:182
  76.1 3.7 %collective-permute-start.4 = (bf16[80,256]{1,0:T(8,128)(2,1)S(1)}, bf16[80,256]{1,0:T(8,128)(2,1)S(1)}, u32[]{:S(2)}, u32[]{:S(2)}) collective-permute-start(bf16[80,256]{1,0:T(8,128)(2,1)S(1)} %get-tuple-element.26), channel_id=1, source_target_pairs={{0,28},{4,0},{8,4},{12,8},{16,12},{20,16},{24,20},{28,24},{1,29},{... | collective-permute-start | bytes 122888 | tf_op jit(solution)/shard_map/ppermute | solution.py:182
  79.8 2.2 %collective-permute-start.5 = (bf16[80,256]{1,0:T(8,128)(2,1)S(1)}, bf16[80,256]{1,0:T(8,128)(2,1)S(1)}, u32[]{:S(2)}, u32[]{:S(2)}) collective-permute-start(bf16[80,256]{1,0:T(8,128)(2,1)S(1)} %get-tuple-element.27), channel_id=1, source_target_pairs={{0,4},{4,8},{8,12},{12,16},{16,20},{20,24},{24,28},{28,0},{1,5},{5... | collective-permute-start | bytes 122888 | tf_op jit(solution)/shard_map/ppermute | solution.py:182
  82.0 12.7 %collective-permute-done.3.refs_1_ = bf16[80,256]{1,0:T(8,128)(2,1)S(1)} collective-permute-done((bf16[80,256]{1,0:T(8,128)(2,1)S(1)}, bf16[80,256]{1,0:T(8,128)(2,1)S(1)}, u32[]{:S(2)}, u32[]{:S(2)}) %collective-permute-start.3) | collective-permute-done | bytes 40992 | tf_op jit(solution)/shard_map/ppermute | solution.py:182
  94.6 0.0 collective-permute-done.4.refs_2_
  94.6 0.0 collective-permute-done.5.refs_3_
  94.6 0.0 all-to-all-done.2.x_ref
  94.6 0.8 shard_map.97
Async XLA Ops:
  2.6 10.5 %copy-start.3 = (bf16[256,320]{0,1:T(8,128)(2,1)S(1)}, bf16[256,320]{0,1:T(8,128)(2,1)}, u32[]{:S(2)}) copy-start(bf16[256,320]{0,1:T(8,128)(2,1)} %param.10) | copy-start | bytes 491524
  2.6 18.5 %copy-start = (bf16[320,1280]{1,0:T(8,128)(2,1)S(1)}, bf16[320,1280]{1,0:T(8,128)(2,1)}, u32[]{:S(2)}) copy-start(bf16[320,1280]{1,0:T(8,128)(2,1)} %w_ref.1) | copy-start | bytes 2457604
  2.6 30.8 %all-to-all-start.1 = ((bf16[8,320,128]{2,1,0:T(8,128)(2,1)}), bf16[8,320,128]{2,1,0:T(8,128)(2,1)S(1)}, u32[]{:S(2)}, u32[]{:S(2)}) async-start(bf16[8,320,128]{2,1,0:T(8,128)(2,1)} %shard_map.94), calls=%async_computation.1 | async-start | bytes 1310720 | tf_op jit(solution)/shard_map/all_to_all | solution.py:200
  13.1 8.0 %copy-start.1 = (bf16[256,320]{0,1:T(8,128)(2,1)S(1)}, bf16[256,320]{0,1:T(8,128)(2,1)}, u32[]{:S(2)}) copy-start(bf16[256,320]{0,1:T(8,128)(2,1)} %param.6) | copy-start | bytes 491524
  13.1 8.0 %copy-start.2 = (bf16[256,320]{0,1:T(8,128)(2,1)S(1)}, bf16[256,320]{0,1:T(8,128)(2,1)}, u32[]{:S(2)}) copy-start(bf16[256,320]{0,1:T(8,128)(2,1)} %param.9) | copy-start | bytes 491524
  33.4 33.6 %all-to-all-start = ((bf16[16,208,128]{2,1,0:T(8,128)(2,1)}), bf16[16,208,128]{2,1,0:T(8,128)(2,1)S(1)}, u32[]{:S(2)}, u32[]{:S(2)}) async-start(bf16[16,208,128]{2,1,0:T(8,128)(2,1)} %get-tuple-element.18), calls=%async_computation | async-start | bytes 1703936 | tf_op jit(solution)/shard_map/all_to_all | solution.py:214
  43.2 9.3 %collective-permute-start = (bf16[176,256]{1,0:T(8,128)(2,1)S(1)}, bf16[176,256]{1,0:T(8,128)(2,1)S(1)}, u32[]{:S(2)}, u32[]{:S(2)}) collective-permute-start(bf16[176,256]{1,0:T(8,128)(2,1)S(1)} %get-tuple-element.20), channel_id=1, source_target_pairs={{0,24},{4,28},{8,0},{12,4},{16,8},{20,12},{24,16},{28,20},{1,25},{... | collective-permute-start | bytes 270344 | tf_op jit(solution)/shard_map/ppermute | solution.py:182
  45.4 7.6 %collective-permute-start.1 = (bf16[176,256]{1,0:T(8,128)(2,1)S(1)}, bf16[176,256]{1,0:T(8,128)(2,1)S(1)}, u32[]{:S(2)}, u32[]{:S(2)}) collective-permute-start(bf16[176,256]{1,0:T(8,128)(2,1)S(1)} %get-tuple-element.21), channel_id=1, source_target_pairs={{0,4},{4,8},{8,12},{12,16},{16,20},{20,24},{24,28},{28,0},{1,5},{5... | collective-permute-start | bytes 270344 | tf_op jit(solution)/shard_map/ppermute | solution.py:182
  47.6 7.3 %collective-permute-start.2 = (bf16[176,256]{1,0:T(8,128)(2,1)S(1)}, bf16[176,256]{1,0:T(8,128)(2,1)S(1)}, u32[]{:S(2)}, u32[]{:S(2)}) collective-permute-start(bf16[176,256]{1,0:T(8,128)(2,1)S(1)} %get-tuple-element.22), channel_id=1, source_target_pairs={{0,28},{4,0},{8,4},{12,8},{16,12},{20,16},{24,20},{28,24},{1,29},{... | collective-permute-start | bytes 270344 | tf_op jit(solution)/shard_map/ppermute | solution.py:182
  67.8 26.8 %all-to-all-start.2 = ((bf16[8,368,128]{2,1,0:T(8,128)(2,1)}), bf16[8,368,128]{2,1,0:T(8,128)(2,1)S(1)}, u32[]{:S(2)}, u32[]{:S(2)}) async-start(bf16[8,368,128]{2,1,0:T(8,128)(2,1)} %shard_map.96), calls=%async_computation.2 | async-start | bytes 1507328 | tf_op jit(solution)/shard_map/all_to_all | solution.py:242
  71.4 23.2 %collective-permute-start.3 = (bf16[80,256]{1,0:T(8,128)(2,1)S(1)}, bf16[80,256]{1,0:T(8,128)(2,1)S(1)}, u32[]{:S(2)}, u32[]{:S(2)}) collective-permute-start(bf16[80,256]{1,0:T(8,128)(2,1)S(1)} %get-tuple-element.25), channel_id=1, source_target_pairs={{0,8},{4,12},{8,16},{12,20},{16,24},{20,28},{24,0},{28,4},{1,9},{5... | collective-permute-start | bytes 122888 | tf_op jit(solution)/shard_map/ppermute | solution.py:182
  76.1 18.5 %collective-permute-start.4 = (bf16[80,256]{1,0:T(8,128)(2,1)S(1)}, bf16[80,256]{1,0:T(8,128)(2,1)S(1)}, u32[]{:S(2)}, u32[]{:S(2)}) collective-permute-start(bf16[80,256]{1,0:T(8,128)(2,1)S(1)} %get-tuple-element.26), channel_id=1, source_target_pairs={{0,28},{4,0},{8,4},{12,8},{16,12},{20,16},{24,20},{28,24},{1,29},{... | collective-permute-start | bytes 122888 | tf_op jit(solution)/shard_map/ppermute | solution.py:182
  79.8 14.8 %collective-permute-start.5 = (bf16[80,256]{1,0:T(8,128)(2,1)S(1)}, bf16[80,256]{1,0:T(8,128)(2,1)S(1)}, u32[]{:S(2)}, u32[]{:S(2)}) collective-permute-start(bf16[80,256]{1,0:T(8,128)(2,1)S(1)} %get-tuple-element.27), channel_id=1, source_target_pairs={{0,4},{4,8},{8,12},{12,16},{16,20},{20,24},{24,28},{28,0},{1,5},{5... | collective-permute-start | bytes 122888 | tf_op jit(solution)/shard_map/ppermute | solution.py:182

commit v3 on v2

--- a/solution.py
+++ b/solution.py
@@ -19,7 +19,7 @@
 EXT = 96
 QG_ROWS = HD + EXT
 K_AT, V_AT, KV_ROWS = 0, 2 * HD, 4 * HD
-PG_AT, OUT_ROWS = 4 * HD, 4 * HD + 48
+PG_AT, OUT_ROWS = 4 * HD, 4 * HD + 32
 PG_COLS = 10
 PG_ROWS = 80
 PG_USED = 208
@@ -48,8 +48,8 @@
                 out_ref[s, at : at + HD] = ref[j * HD : (j + 1) * HD, b * HALF : (b + 1) * HALF]
 
 
-def pack_queries_and_proj_kernel(q_hbm, o_hbm, cot_ref, w_ref, *refs):
-    out_refs, (out_ref, q_ref, o_ref, g_ref, extra_ref, sems) = refs[: len(NEAR)], refs[len(NEAR) :]
+def pack_queries_kernel(q_hbm, o_hbm, cot_ref, w_ref, *refs):
+    out_refs, (q_ref, o_ref, g_ref, extra_ref, sems) = refs[: len(NEAR)], refs[len(NEAR) :]
     pairs = ((q_hbm, q_ref), (o_hbm, o_ref))
     copies = [pltpu.make_async_copy(x, y, sems.at[i]) for i, (x, y) in enumerate(pairs)]
     for copy in copies:
@@ -81,29 +81,44 @@
         ref[HD : 2 * HD] = g_ref[cols]
         rows = pl.ds(pl.multiple_of(j * (EXT - HD), 16), EXT - HD)
         ref[2 * HD :] = extra_ref[rows]
+
+
+def proj_kernel(cot_ref, o_ref, kept_ref, given_ref):
+    parity = lax.rem(lax.div(lax.axis_index("dp"), 2), 2)
     empty = jnp.zeros((PG_USED - 200, HALF), jnp.float32)
-    for d in range(DP):
-        part = dot(cot_ref[d * PG_ROWS : (d + 1) * PG_ROWS], o_ref[...], NT)
-        for c in range(2):
-            at = c * PG_ROWS
-            out_ref[d, at : at + PG_ROWS] = part[:, HALF * c : HALF * (c + 1)].astype(out_ref.dtype)
-        last = part[:, 2 * HALF :]
-        last = jnp.concatenate([last[: PG_ROWS // 2], last[PG_ROWS // 2 :]], axis=1)
-        out_ref[d, 2 * PG_ROWS :] = jnp.concatenate([last, empty], axis=0).astype(out_ref.dtype)
+    for ref, wanted in ((given_ref, 1 - parity), (kept_ref, parity)):
+        for k in range(SHARDS):
+            d = (k // 2 * 2 + wanted) * 2 + k % 2
+            start = pl.multiple_of(d * PG_ROWS, 16)
+            part = dot(cot_ref[pl.ds(start, PG_ROWS)], o_ref[...], NT)
+            for c in range(2):
+                at = c * PG_ROWS
+                ref[k, at : at + PG_ROWS] = part[:, HALF * c : HALF * (c + 1)].astype(ref.dtype)
+            last = part[:, 2 * HALF :]
+            last = jnp.concatenate([last[: PG_ROWS // 2], last[PG_ROWS // 2 :]], axis=1)
+            ref[k, 2 * PG_ROWS :] = jnp.concatenate([last, empty], axis=0).astype(ref.dtype)
+
+
+def add_kernel(kept_ref, taken_ref, out_ref):
+    out_ref[...] = (kept_ref[...] + taken_ref[...].astype(jnp.float32)).astype(jnp.bfloat16)
+
+
+def after_kernel(*refs):
+    pass
 
 
 def add_share_kernel(parts_ref, sent_in_ref, sent_ref, pieces, sem):
     total = parts_ref[0].astype(jnp.float32)
-    for k in range(1, DP):
+    for k in range(1, SHARDS):
         total = total + parts_ref[k].astype(jnp.float32)
+    empty = jnp.zeros((1, HALF), jnp.float32)
     for s in range(SHARDS):
-        last = total[2 * PG_ROWS + s % 4 * PG_COLS :][:PG_COLS]
-        last = last[:, s // 4 * 64 :][:, :64]
         blocks = [total[c * PG_ROWS + s * PG_COLS :][:PG_COLS] for c in range(2)]
-        blocks.append(jnp.concatenate([last, jnp.zeros_like(last)], axis=1))
-        for c, block in enumerate(blocks):
-            block = jnp.concatenate([block, jnp.zeros((6, HALF), jnp.float32)], axis=0)
-            pieces[s, 16 * c : 16 * (c + 1)] = block.astype(jnp.bfloat16)
+        third = total[2 * PG_ROWS + s % 4 * PG_COLS :][:PG_COLS, s // 4 * 64 :][:, :64]
+        blocks.append(jnp.concatenate([third[:5], third[5:]], axis=1))
+        first = jnp.concatenate([blocks[0], blocks[2], empty], axis=0)
+        second = jnp.concatenate([blocks[1], jnp.zeros((6, HALF), jnp.float32)], axis=0)
+        pieces[s] = jnp.concatenate([first, second], axis=0).astype(jnp.bfloat16)
     copy = pltpu.make_async_copy(pieces, sent_ref.at[:, pl.ds(PG_AT, OUT_ROWS - PG_AT)], sem)
     copy.start()
     copy.wait()
@@ -161,8 +176,9 @@
     total = x_ref[0, PG_AT:].astype(jnp.float32)
     for s in range(1, SHARDS):
         total = total + x_ref[s, PG_AT:].astype(jnp.float32)
-    wide = jnp.concatenate([total[16 * c : 16 * (c + 1)] for c in range(3)], axis=1)
-    pg_ref[...] = wide[:PG_COLS, :WIDE]
+    last = total[PG_COLS : PG_COLS + 5]
+    last = jnp.concatenate([last[:, :64], last[:, 64:]], axis=0)
+    pg_ref[...] = jnp.concatenate([total[:PG_COLS], total[16 : 16 + PG_COLS], last], axis=1)
 
 
 def call(kernel, outs, flops, transcendentals=0, scratch=(), mib=48, **more):
@@ -201,17 +217,30 @@
 
     full_cot = lax.all_gather(cot, "tp", axis=0, tiled=True)
     flops = 2 * ROWS * WIDE * 4 * WIDE
-    *near, parts = call(
-        pack_queries_and_proj_kernel,
-        [shape((QG_ROWS, ROWS), half)] * len(NEAR) + [shape((DP, PG_USED, HALF), half)],
-        2 * flops,
+    block = (SHARDS, PG_USED, HALF)
+    kept, given = call(proj_kernel, (shape(block, single), shape(block, half)), flops)(full_cot, o)
+    taken = lax.ppermute(given, "dp", [(i, i ^ 2) for i in range(DP)])
+    near = call(
+        pack_queries_kernel,
+        [shape((QG_ROWS, ROWS), half)] * len(NEAR),
+        flops,
         scratch=[whole] * 3
         + [pltpu.VMEM((HEADS_HERE * (EXT - HD), ROWS), half), pltpu.SemaphoreType.DMA((2,))],
         in_specs=[anywhere] * 2 + [vmem] * 2,
         mib=48,
     )(q, o, full_cot, proj_weight)
     near = [near[0]] + [shifted_round(x, away) for away, x in zip(NEAR[1:], near[1:])]
-    parts = lax.all_to_all(parts, "dp", 0, 0, tiled=True)
+    parts = call(add_kernel, shape(block, half), 0)(kept, taken)
+    parts = call(
+        after_kernel,
+        shape(block, half),
+        0,
+        in_specs=[anywhere] * len(near),
+        out_specs=anywhere,
+        input_output_aliases={0: 0},
+    )(parts, *near[1:])
+    same_parity = [[(k // 2 * 2 + y) * 2 + k % 2 for k in range(SHARDS)] for y in range(2)]
+    parts = lax.all_to_all(parts, "dp", 0, 0, tiled=True, axis_index_groups=same_parity)
 
     tokens = SHARDS * ROWS
     sent, *dq = call(

time: 96 us -> 92.7 us (0.966)
  the two profiles are of different devices: /device:TPU:24 before, /device:TPU:8 now
where the time goes in v3:
time: 92.7 us; the launch traced here: 92.2 us
  starting transfers between devices  49.8 us (54%)
  waiting for transfers between devices  19.7 us (21%)
  Pallas kernels  13.8 us (15%)
  blocking collectives  8.02 us (9%)
    ppermute x6, starting transfers between devices, shifted_round(): lax.ppermute(x, 'ctx', [(z, (z + away) % SHARDS) for z in range(SHARDS)])  23.7 us
    ppermute x6, waiting for transfers between devices, shifted_round(): lax.ppermute(x, 'ctx', [(z, (z + away) % SHARDS) for z in range(SHARDS)])  12.5 us
    all_to_all x1, starting transfers between devices, on_device(): pairs = lax.all_to_all(pairs, 'ctx', 0, 0, tiled=True)  10.5 us
    all_to_all x1, starting transfers between devices, on_device(): lax.all_to_all(parts, 'dp', 0, 0, tiled=True, axis_index_groups=same_parity)  9.27 us
    all_gather x1, blocking collectives, on_device(): full_cot = lax.all_gather(cot, 'tp', axis=0, tiled=True)  8.02 us
    pallas_call x1, Pallas kernels, on_device(): call(grad_kernel, [shape((SHARDS, OUT_ROWS, HALF), half)] + [shape((HD, R...  7.66 us
    all_to_all x1, waiting for transfers between devices, on_device(): lax.all_to_all(parts, 'dp', 0, 0, tiled=True, axis_index_groups=same_parity)  7.15 us
    all_to_all x1, starting transfers between devices, on_device(): back = lax.all_to_all(sent, 'ctx', 0, 0, tiled=True)  4.02 us
  transfers between devices with their start and end apart: 10, of which 3 were waited for; matrix products, arithmetic and copies ran while one was open for 0% of the time, Pallas kernels for 11%

profile of v3, /device:TPU:8, one launch (start us, length us, event | category | flops | bytes accessed | tf_op | source)
XLA Modules:
  0.0 92.2 jit_solution(7242200319465949259)
XLA Ops:
  0.6 1.9 %shard_map.97 = bf16[8,320,128]{2,1,0:T(8,128)(2,1)} custom-call(bf16[320,256]{1,0:T(8,128)(2,1)} %bitcast.13, bf16[320,256]{1,0:T(8,128)(2,1)} %bitcast.14), custom_call_target="tpu_custom_call" | custom-call | bytes 2097152 | tf_op jit(solution)/shard_map/pallas_call | solution.py:208
  2.5 0.0 copy-start.3
  2.6 0.0 copy-start.1
  2.6 10.5 %all-to-all-start.1 = ((bf16[8,320,128]{2,1,0:T(8,128)(2,1)}), bf16[8,320,128]{2,1,0:T(8,128)(2,1)S(1)}, u32[]{:S(2)}, u32[]{:S(2)}) async-start(bf16[8,320,128]{2,1,0:T(8,128)(2,1)} %shard_map.97), calls=%async_computation.1 | async-start | bytes 1310720 | tf_op jit(solution)/shard_map/all_to_all | solution.py:216
  13.0 0.0 copy-done.3
  13.0 0.0 copy-start
  13.0 8.0 %all_gather.3.cot_ref = bf16[1280,256]{1,0:T(8,128)(2,1)S(1)} all-gather(bf16[320,256]{1,0:T(8,128)(2,1)S(1)} %bitcast.12), channel_id=1, replica_groups=mesh['dp'=16,'ctx'=8,'tp'=4] {'tp'}, dimensions={0}, use_global_device_ids=true | all-gather | bytes 819200 | tf_op jit(solution)/shard_map/all_gather | solution.py:218
  21.1 0.0 copy-done.1
  21.1 0.0 copy-start.2
  21.1 1.0 %shard_map.93 = (f32[8,208,128]{2,1,0:T(8,128)S(1)}, bf16[8,208,128]{2,1,0:T(8,128)(2,1)S(1)}) custom-call(bf16[1280,256]{1,0:T(8,128)(2,1)S(1)} %all_gather.3.cot_ref, bf16[320,256]{1,0:T(8,128)(2,1)S(1)} %bitcast.9), custom_call_target="tpu_custom_call" | custom-call | flops 209715200 | bytes 2097152 | tf_op jit(solution)/shard_map/pallas_call | solution.py:221
  22.0 2.3 %collective-permute-start = (bf16[8,208,128]{2,1,0:T(8,128)(2,1)S(1)}, bf16[8,208,128]{2,1,0:T(8,128)(2,1)S(1)}, u32[]{:S(2)}, u32[]{:S(2)}) collective-permute-start(bf16[8,208,128]{2,1,0:T(8,128)(2,1)S(1)} %get-tuple-element.20), channel_id=1, source_target_pairs={{0,64},{32,96},{64,0},{96,32},{128,192},{160,224},{192,128},{224,1... | collective-permute-start | bytes 1277960 | tf_op jit(solution)/shard_map/ppermute | solution.py:222
  24.4 0.0 copy-done
  24.4 0.0 copy-done.2
  24.4 0.9 shard_map.95
  25.3 6.0 %collective-permute-start.1 = (bf16[176,256]{1,0:T(8,128)(2,1)S(1)}, bf16[176,256]{1,0:T(8,128)(2,1)S(1)}, u32[]{:S(2)}, u32[]{:S(2)}) collective-permute-start(bf16[176,256]{1,0:T(8,128)(2,1)S(1)} %get-tuple-element.21), channel_id=1, source_target_pairs={{0,24},{4,28},{8,0},{12,4},{16,8},{20,12},{24,16},{28,20},{1,25},{... | collective-permute-start | bytes 270344 | tf_op jit(solution)/shard_map/ppermute | solution.py:198
  31.3 2.5 %collective-permute-start.2 = (bf16[176,256]{1,0:T(8,128)(2,1)S(1)}, bf16[176,256]{1,0:T(8,128)(2,1)S(1)}, u32[]{:S(2)}, u32[]{:S(2)}) collective-permute-start(bf16[176,256]{1,0:T(8,128)(2,1)S(1)} %get-tuple-element.22), channel_id=1, source_target_pairs={{0,4},{4,8},{8,12},{12,16},{16,20},{20,24},{24,28},{28,0},{1,5},{5... | collective-permute-start | bytes 270344 | tf_op jit(solution)/shard_map/ppermute | solution.py:198
  33.8 4.6 %collective-permute-start.3 = (bf16[176,256]{1,0:T(8,128)(2,1)S(1)}, bf16[176,256]{1,0:T(8,128)(2,1)S(1)}, u32[]{:S(2)}, u32[]{:S(2)}) collective-permute-start(bf16[176,256]{1,0:T(8,128)(2,1)S(1)} %get-tuple-element.23), channel_id=1, source_target_pairs={{0,28},{4,0},{8,4},{12,8},{16,12},{20,16},{24,20},{28,24},{1,29},{... | collective-permute-start | bytes 270344 | tf_op jit(solution)/shard_map/ppermute | solution.py:198
  38.4 0.0 collective-permute-done.taken_ref
  38.4 0.9 shard_map.94.refs_0_
  39.3 0.0 collective-permute-done.1.refs_1_
  39.3 0.0 collective-permute-done.2.refs_2_
  39.3 1.2 %collective-permute-done.3.refs_3_ = bf16[176,256]{1,0:T(8,128)(2,1)S(1)} collective-permute-done((bf16[176,256]{1,0:T(8,128)(2,1)S(1)}, bf16[176,256]{1,0:T(8,128)(2,1)S(1)}, u32[]{:S(2)}, u32[]{:S(2)}) %collective-permute-start.3) | collective-permute-done | bytes 90144 | tf_op jit(solution)/shard_map/ppermute | solution.py:198
  40.5 0.0 all-to-all-done.1.x_ref
  40.5 9.3 %all-to-all-start = ((bf16[8,208,128]{2,1,0:T(8,128)(2,1)}), bf16[8,208,128]{2,1,0:T(8,128)(2,1)S(1)}, u32[]{:S(2)}, u32[]{:S(2)}) async-start(bf16[8,208,128]{2,1,0:T(8,128)(2,1)} %shard_map.96), calls=%async_computation | async-start | bytes 851968 | tf_op jit(solution)/shard_map/all_to_all | solution.py:243
  49.8 7.7 %shard_map.98 = (bf16[8,352,128]{2,1,0:T(8,128)(2,1)}, bf16[80,256]{1,0:T(8,128)(2,1)S(1)}, bf16[80,256]{1,0:T(8,128)(2,1)S(1)}, bf16[80,256]{1,0:T(8,128)(2,1)S(1)}, bf16[80,256]{1,0:T(8,128)(2,1)S(1)}) custom-call(bf16[8,320,128]{2,1,0:T(8,128)(2,1)S(1)} %all-to-all-done.1.x_ref, bf16[176,256]{1,0:T(8,128)(2,1)S(1)} %get-tuple-element.24.refs_0_, ...), custom_call_target="tpu_custom_call" | custom-call | flops 1677721600 | bytes 2097152 | tf_op jit(solution)/shard_map/pallas_call | solution.py:246
  57.5 7.2 %all-to-all-done.parts_ref = bf16[8,208,128]{2,1,0:T(8,128)(2,1)S(1)} async-done(((bf16[8,208,128]{2,1,0:T(8,128)(2,1)}), bf16[8,208,128]{2,1,0:T(8,128)(2,1)S(1)}, u32[]{:S(2)}, u32[]{:S(2)}) %all-to-all-start) | async-done | bytes 426016 | tf_op jit(solution)/shard_map/all_to_all | solution.py:243
  64.6 0.7 shard_map.99
  65.3 4.0 %all-to-all-start.2 = ((bf16[8,352,128]{2,1,0:T(8,128)(2,1)}), bf16[8,352,128]{2,1,0:T(8,128)(2,1)S(1)}, u32[]{:S(2)}, u32[]{:S(2)}) async-start(bf16[8,352,128]{2,1,0:T(8,128)(2,1)} %shard_map.99), calls=%async_computation.2 | async-start | bytes 1441792 | tf_op jit(solution)/shard_map/all_to_all | solution.py:271
  69.4 4.8 %collective-permute-start.4 = (bf16[80,256]{1,0:T(8,128)(2,1)S(1)}, bf16[80,256]{1,0:T(8,128)(2,1)S(1)}, u32[]{:S(2)}, u32[]{:S(2)}) collective-permute-start(bf16[80,256]{1,0:T(8,128)(2,1)S(1)} %get-tuple-element.27), channel_id=1, source_target_pairs={{0,8},{4,12},{8,16},{12,20},{16,24},{20,28},{24,0},{28,4},{1,9},{5... | collective-permute-start | bytes 122888 | tf_op jit(solution)/shard_map/ppermute | solution.py:198
  74.2 3.7 %collective-permute-start.5 = (bf16[80,256]{1,0:T(8,128)(2,1)S(1)}, bf16[80,256]{1,0:T(8,128)(2,1)S(1)}, u32[]{:S(2)}, u32[]{:S(2)}) collective-permute-start(bf16[80,256]{1,0:T(8,128)(2,1)S(1)} %get-tuple-element.28), channel_id=1, source_target_pairs={{0,28},{4,0},{8,4},{12,8},{16,12},{20,16},{24,20},{28,24},{1,29},{... | collective-permute-start | bytes 122888 | tf_op jit(solution)/shard_map/ppermute | solution.py:198
  77.9 2.2 %collective-permute-start.6 = (bf16[80,256]{1,0:T(8,128)(2,1)S(1)}, bf16[80,256]{1,0:T(8,128)(2,1)S(1)}, u32[]{:S(2)}, u32[]{:S(2)}) collective-permute-start(bf16[80,256]{1,0:T(8,128)(2,1)S(1)} %get-tuple-element.29), channel_id=1, source_target_pairs={{0,4},{4,8},{8,12},{12,16},{16,20},{20,24},{24,28},{28,0},{1,5},{5... | collective-permute-start | bytes 122888 | tf_op jit(solution)/shard_map/ppermute | solution.py:198
  80.1 11.3 %collective-permute-done.4.refs_1_ = bf16[80,256]{1,0:T(8,128)(2,1)S(1)} collective-permute-done((bf16[80,256]{1,0:T(8,128)(2,1)S(1)}, bf16[80,256]{1,0:T(8,128)(2,1)S(1)}, u32[]{:S(2)}, u32[]{:S(2)}) %collective-permute-start.4) | collective-permute-done | bytes 40992 | tf_op jit(solution)/shard_map/ppermute | solution.py:198
  91.3 0.0 collective-permute-done.5.refs_2_
  91.4 0.0 collective-permute-done.6.refs_3_
  91.4 0.0 all-to-all-done.2.x_ref
  91.4 0.8 shard_map.100
  (1 shorter events, 0.0 us)
Async XLA Ops:
  2.5 10.5 %copy-start.3 = (bf16[256,320]{0,1:T(8,128)(2,1)S(1)}, bf16[256,320]{0,1:T(8,128)(2,1)}, u32[]{:S(2)}) copy-start(bf16[256,320]{0,1:T(8,128)(2,1)} %param.10) | copy-start | bytes 491524
  2.6 18.5 %copy-start.1 = (bf16[256,320]{0,1:T(8,128)(2,1)S(1)}, bf16[256,320]{0,1:T(8,128)(2,1)}, u32[]{:S(2)}) copy-start(bf16[256,320]{0,1:T(8,128)(2,1)} %param.9) | copy-start | bytes 491524
  2.6 38.0 %all-to-all-start.1 = ((bf16[8,320,128]{2,1,0:T(8,128)(2,1)}), bf16[8,320,128]{2,1,0:T(8,128)(2,1)S(1)}, u32[]{:S(2)}, u32[]{:S(2)}) async-start(bf16[8,320,128]{2,1,0:T(8,128)(2,1)} %shard_map.97), calls=%async_computation.1 | async-start | bytes 1310720 | tf_op jit(solution)/shard_map/all_to_all | solution.py:216
  13.0 11.4 %copy-start = (bf16[320,1280]{1,0:T(8,128)(2,1)S(1)}, bf16[320,1280]{1,0:T(8,128)(2,1)}, u32[]{:S(2)}) copy-start(bf16[320,1280]{1,0:T(8,128)(2,1)} %w_ref.1) | copy-start | bytes 2457604
  21.1 3.3 %copy-start.2 = (bf16[256,320]{0,1:T(8,128)(2,1)S(1)}, bf16[256,320]{0,1:T(8,128)(2,1)}, u32[]{:S(2)}) copy-start(bf16[256,320]{0,1:T(8,128)(2,1)} %param.6) | copy-start | bytes 491524
  22.0 16.4 %collective-permute-start = (bf16[8,208,128]{2,1,0:T(8,128)(2,1)S(1)}, bf16[8,208,128]{2,1,0:T(8,128)(2,1)S(1)}, u32[]{:S(2)}, u32[]{:S(2)}) collective-permute-start(bf16[8,208,128]{2,1,0:T(8,128)(2,1)S(1)} %get-tuple-element.20), channel_id=1, source_target_pairs={{0,64},{32,96},{64,0},{96,32},{128,192},{160,224},{192,128},{224,1... | collective-permute-start | bytes 1277960 | tf_op jit(solution)/shard_map/ppermute | solution.py:222
  25.3 14.0 %collective-permute-start.1 = (bf16[176,256]{1,0:T(8,128)(2,1)S(1)}, bf16[176,256]{1,0:T(8,128)(2,1)S(1)}, u32[]{:S(2)}, u32[]{:S(2)}) collective-permute-start(bf16[176,256]{1,0:T(8,128)(2,1)S(1)} %get-tuple-element.21), channel_id=1, source_target_pairs={{0,24},{4,28},{8,0},{12,4},{16,8},{20,12},{24,16},{28,20},{1,25},{... | collective-permute-start | bytes 270344 | tf_op jit(solution)/shard_map/ppermute | solution.py:198
  31.3 7.9 %collective-permute-start.2 = (bf16[176,256]{1,0:T(8,128)(2,1)S(1)}, bf16[176,256]{1,0:T(8,128)(2,1)S(1)}, u32[]{:S(2)}, u32[]{:S(2)}) collective-permute-start(bf16[176,256]{1,0:T(8,128)(2,1)S(1)} %get-tuple-element.22), channel_id=1, source_target_pairs={{0,4},{4,8},{8,12},{12,16},{16,20},{20,24},{24,28},{28,0},{1,5},{5... | collective-permute-start | bytes 270344 | tf_op jit(solution)/shard_map/ppermute | solution.py:198
  33.8 6.7 %collective-permute-start.3 = (bf16[176,256]{1,0:T(8,128)(2,1)S(1)}, bf16[176,256]{1,0:T(8,128)(2,1)S(1)}, u32[]{:S(2)}, u32[]{:S(2)}) collective-permute-start(bf16[176,256]{1,0:T(8,128)(2,1)S(1)} %get-tuple-element.23), channel_id=1, source_target_pairs={{0,28},{4,0},{8,4},{12,8},{16,12},{20,16},{24,20},{28,24},{1,29},{... | collective-permute-start | bytes 270344 | tf_op jit(solution)/shard_map/ppermute | solution.py:198
  40.5 24.1 %all-to-all-start = ((bf16[8,208,128]{2,1,0:T(8,128)(2,1)}), bf16[8,208,128]{2,1,0:T(8,128)(2,1)S(1)}, u32[]{:S(2)}, u32[]{:S(2)}) async-start(bf16[8,208,128]{2,1,0:T(8,128)(2,1)} %shard_map.96), calls=%async_computation | async-start | bytes 851968 | tf_op jit(solution)/shard_map/all_to_all | solution.py:243
  65.3 26.0 %all-to-all-start.2 = ((bf16[8,352,128]{2,1,0:T(8,128)(2,1)}), bf16[8,352,128]{2,1,0:T(8,128)(2,1)S(1)}, u32[]{:S(2)}, u32[]{:S(2)}) async-start(bf16[8,352,128]{2,1,0:T(8,128)(2,1)} %shard_map.99), calls=%async_computation.2 | async-start | bytes 1441792 | tf_op jit(solution)/shard_map/all_to_all | solution.py:271
  69.4 22.0 %collective-permute-start.4 = (bf16[80,256]{1,0:T(8,128)(2,1)S(1)}, bf16[80,256]{1,0:T(8,128)(2,1)S(1)}, u32[]{:S(2)}, u32[]{:S(2)}) collective-permute-start(bf16[80,256]{1,0:T(8,128)(2,1)S(1)} %get-tuple-element.27), channel_id=1, source_target_pairs={{0,8},{4,12},{8,16},{12,20},{16,24},{20,28},{24,0},{28,4},{1,9},{5... | collective-permute-start | bytes 122888 | tf_op jit(solution)/shard_map/ppermute | solution.py:198
  74.2 17.2 %collective-permute-start.5 = (bf16[80,256]{1,0:T(8,128)(2,1)S(1)}, bf16[80,256]{1,0:T(8,128)(2,1)S(1)}, u32[]{:S(2)}, u32[]{:S(2)}) collective-permute-start(bf16[80,256]{1,0:T(8,128)(2,1)S(1)} %get-tuple-element.28), channel_id=1, source_target_pairs={{0,28},{4,0},{8,4},{12,8},{16,12},{20,16},{24,20},{28,24},{1,29},{... | collective-permute-start | bytes 122888 | tf_op jit(solution)/shard_map/ppermute | solution.py:198
  77.9 13.5 %collective-permute-start.6 = (bf16[80,256]{1,0:T(8,128)(2,1)S(1)}, bf16[80,256]{1,0:T(8,128)(2,1)S(1)}, u32[]{:S(2)}, u32[]{:S(2)}) collective-permute-start(bf16[80,256]{1,0:T(8,128)(2,1)S(1)} %get-tuple-element.29), channel_id=1, source_target_pairs={{0,4},{4,8},{8,12},{12,16},{16,20},{20,24},{24,28},{28,0},{1,5},{5... | collective-permute-start | bytes 122888 | tf_op jit(solution)/shard_map/ppermute | solution.py:198

commit v4 on v3

--- a/solution.py
+++ b/solution.py
@@ -23,7 +23,7 @@
 PG_COLS = 10
 PG_ROWS = 80
 PG_USED = 208
-NEAR = (0, 6, 1, 7)
+NEAR = (0, 2, 1, 7)
 
 NT = (((1,), (1,)), ((), ()))
 TN = (((0,), (0,)), ((), ()))
@@ -84,11 +84,11 @@
 
 
 def proj_kernel(cot_ref, o_ref, kept_ref, given_ref):
-    parity = lax.rem(lax.div(lax.axis_index("dp"), 2), 2)
+    upper = lax.rem(lax.axis_index("dp"), 2)
     empty = jnp.zeros((PG_USED - 200, HALF), jnp.float32)
-    for ref, wanted in ((given_ref, 1 - parity), (kept_ref, parity)):
+    for ref, wanted in ((given_ref, 1 - upper), (kept_ref, upper)):
         for k in range(SHARDS):
-            d = (k // 2 * 2 + wanted) * 2 + k % 2
+            d = 2 * k + wanted
             start = pl.multiple_of(d * PG_ROWS, 16)
             part = dot(cot_ref[pl.ds(start, PG_ROWS)], o_ref[...], NT)
             for c in range(2):
@@ -194,8 +194,11 @@
     )
 
 
-def shifted_round(x, away):
-    return lax.ppermute(x, "ctx", [(z, (z + away) % SHARDS) for z in range(SHARDS)])
+def shifted_round(x, away, back=False):
+    pairs = [
+        (z, (z - away if away == 2 and z % 2 == 0 else z + away) % SHARDS) for z in range(SHARDS)
+    ]
+    return lax.ppermute(x, "ctx", [pair[::-1] for pair in pairs] if back else pairs)
 
 
 def on_device(queries, keys, values, saved_out, cotangent, proj_weight):
@@ -219,7 +222,7 @@
     flops = 2 * ROWS * WIDE * 4 * WIDE
     block = (SHARDS, PG_USED, HALF)
     kept, given = call(proj_kernel, (shape(block, single), shape(block, half)), flops)(full_cot, o)
-    taken = lax.ppermute(given, "dp", [(i, i ^ 2) for i in range(DP)])
+    taken = lax.ppermute(given, "dp", [(i, i ^ 1) for i in range(DP)])
     near = call(
         pack_queries_kernel,
         [shape((QG_ROWS, ROWS), half)] * len(NEAR),
@@ -239,8 +242,8 @@
         out_specs=anywhere,
         input_output_aliases={0: 0},
     )(parts, *near[1:])
-    same_parity = [[(k // 2 * 2 + y) * 2 + k % 2 for k in range(SHARDS)] for y in range(2)]
-    parts = lax.all_to_all(parts, "dp", 0, 0, tiled=True, axis_index_groups=same_parity)
+    along_y = [list(range(x, DP, 2)) for x in range(2)]
+    parts = lax.all_to_all(parts, "dp", 0, 0, tiled=True, axis_index_groups=along_y)
 
     tokens = SHARDS * ROWS
     sent, *dq = call(
@@ -269,7 +272,7 @@
         input_output_aliases={1: 0},
     )(parts, sent)
     back = lax.all_to_all(sent, "ctx", 0, 0, tiled=True)
-    dq = [dq[0]] + [shifted_round(x, -away) for away, x in zip(NEAR[1:], dq[1:])]
+    dq = [dq[0]] + [shifted_round(x, away, back=True) for away, x in zip(NEAR[1:], dq[1:])]
     grad = shape((WIDE, ROWS), half)
     outs = call(unpack_kernel, (grad, grad, grad, shape((PG_COLS, WIDE), single)), 0)(back, *dq)
     return tuple(x.T for x in outs)

time: 92.7 us -> 90.7 us (0.978)
  the two profiles are of different devices: /device:TPU:8 before, /device:TPU:4 now
where the time goes in v4:
time: 90.7 us; the launch traced here: 90.2 us
  starting transfers between devices  50.3 us (55%)
  waiting for transfers between devices  17.6 us (19%)
  Pallas kernels  13.8 us (15%)
  blocking collectives  7.72 us (9%)
    ppermute x6, starting transfers between devices, shifted_round(): lax.ppermute(x, 'ctx', [pair[::-1] for pair in pairs] if back else pairs)  24.4 us
    all_to_all x1, starting transfers between devices, on_device(): pairs = lax.all_to_all(pairs, 'ctx', 0, 0, tiled=True)  10.5 us
    ppermute x6, waiting for transfers between devices, shifted_round(): lax.ppermute(x, 'ctx', [pair[::-1] for pair in pairs] if back else pairs)  8.86 us
    all_gather x1, blocking collectives, on_device(): full_cot = lax.all_gather(cot, 'tp', axis=0, tiled=True)  7.72 us
    pallas_call x1, Pallas kernels, on_device(): call(grad_kernel, [shape((SHARDS, OUT_ROWS, HALF), half)] + [shape((HD, R...  7.65 us
    all_to_all x1, starting transfers between devices, on_device(): lax.all_to_all(parts, 'dp', 0, 0, tiled=True, axis_index_groups=along_y)  7.1 us
    all_to_all x1, waiting for transfers between devices, on_device(): lax.all_to_all(parts, 'dp', 0, 0, tiled=True, axis_index_groups=along_y)  6.55 us
    all_to_all x1, starting transfers between devices, on_device(): back = lax.all_to_all(sent, 'ctx', 0, 0, tiled=True)  5.62 us
  transfers between devices with their start and end apart: 10, of which 4 were waited for; matrix products, arithmetic and copies ran while one was open for 0% of the time, Pallas kernels for 11%

profile of v4, /device:TPU:4, one launch (start us, length us, event | category | flops | bytes accessed | tf_op | source)
XLA Modules:
  0.0 90.2 jit_solution(13997528444942494274)
XLA Ops:
  0.6 1.9 %shard_map.97 = bf16[8,320,128]{2,1,0:T(8,128)(2,1)} custom-call(bf16[320,256]{1,0:T(8,128)(2,1)} %bitcast.13, bf16[320,256]{1,0:T(8,128)(2,1)} %bitcast.14), custom_call_target="tpu_custom_call" | custom-call | bytes 2097152 | tf_op jit(solution)/shard_map/pallas_call | solution.py:211
  2.5 0.0 copy-start.3
  2.6 0.0 copy-start.1
  2.6 10.5 %all-to-all-start.1 = ((bf16[8,320,128]{2,1,0:T(8,128)(2,1)}), bf16[8,320,128]{2,1,0:T(8,128)(2,1)S(1)}, u32[]{:S(2)}, u32[]{:S(2)}) async-start(bf16[8,320,128]{2,1,0:T(8,128)(2,1)} %shard_map.97), calls=%async_computation.1 | async-start | bytes 1310720 | tf_op jit(solution)/shard_map/all_to_all | solution.py:219
  13.0 0.0 copy-done.3
  13.0 0.0 copy-start
  13.0 7.7 %all_gather.3.cot_ref = bf16[1280,256]{1,0:T(8,128)(2,1)S(1)} all-gather(bf16[320,256]{1,0:T(8,128)(2,1)S(1)} %bitcast.12), channel_id=1, replica_groups=mesh['dp'=16,'ctx'=8,'tp'=4] {'tp'}, dimensions={0}, use_global_device_ids=true | all-gather | bytes 819200 | tf_op jit(solution)/shard_map/all_gather | solution.py:221
  20.8 0.0 copy-done.1
  20.8 0.0 copy-start.2
  20.8 1.0 %shard_map.93 = (f32[8,208,128]{2,1,0:T(8,128)S(1)}, bf16[8,208,128]{2,1,0:T(8,128)(2,1)S(1)}) custom-call(bf16[1280,256]{1,0:T(8,128)(2,1)S(1)} %all_gather.3.cot_ref, bf16[320,256]{1,0:T(8,128)(2,1)S(1)} %bitcast.9), custom_call_target="tpu_custom_call" | custom-call | flops 209715200 | bytes 2097152 | tf_op jit(solution)/shard_map/pallas_call | solution.py:224
  21.7 2.7 %collective-permute-start = (bf16[8,208,128]{2,1,0:T(8,128)(2,1)S(1)}, bf16[8,208,128]{2,1,0:T(8,128)(2,1)S(1)}, u32[]{:S(2)}, u32[]{:S(2)}) collective-permute-start(bf16[8,208,128]{2,1,0:T(8,128)(2,1)S(1)} %get-tuple-element.20), channel_id=1, source_target_pairs={{0,32},{32,0},{64,96},{96,64},{128,160},{160,128},{192,224},{224,1... | collective-permute-start | bytes 1277960 | tf_op jit(solution)/shard_map/ppermute | solution.py:225
  24.4 0.0 copy-done
  24.4 0.0 copy-done.2
  24.5 0.9 shard_map.95
  25.3 6.0 %collective-permute-start.1 = (bf16[176,256]{1,0:T(8,128)(2,1)S(1)}, bf16[176,256]{1,0:T(8,128)(2,1)S(1)}, u32[]{:S(2)}, u32[]{:S(2)}) collective-permute-start(bf16[176,256]{1,0:T(8,128)(2,1)S(1)} %get-tuple-element.21), channel_id=1, source_target_pairs={{0,24},{4,12},{8,0},{12,20},{16,8},{20,28},{24,16},{28,4},{1,25},{... | collective-permute-start | bytes 270344 | tf_op jit(solution)/shard_map/ppermute | solution.py:201
  31.4 2.2 %collective-permute-start.2 = (bf16[176,256]{1,0:T(8,128)(2,1)S(1)}, bf16[176,256]{1,0:T(8,128)(2,1)S(1)}, u32[]{:S(2)}, u32[]{:S(2)}) collective-permute-start(bf16[176,256]{1,0:T(8,128)(2,1)S(1)} %get-tuple-element.22), channel_id=1, source_target_pairs={{0,4},{4,8},{8,12},{12,16},{16,20},{20,24},{24,28},{28,0},{1,5},{5... | collective-permute-start | bytes 270344 | tf_op jit(solution)/shard_map/ppermute | solution.py:201
  33.5 4.9 %collective-permute-start.3 = (bf16[176,256]{1,0:T(8,128)(2,1)S(1)}, bf16[176,256]{1,0:T(8,128)(2,1)S(1)}, u32[]{:S(2)}, u32[]{:S(2)}) collective-permute-start(bf16[176,256]{1,0:T(8,128)(2,1)S(1)} %get-tuple-element.23), channel_id=1, source_target_pairs={{0,28},{4,0},{8,4},{12,8},{16,12},{20,16},{24,20},{28,24},{1,29},{... | collective-permute-start | bytes 270344 | tf_op jit(solution)/shard_map/ppermute | solution.py:201
  38.4 0.0 collective-permute-done.taken_ref
  38.5 0.9 shard_map.94.refs_0_
  39.3 0.0 collective-permute-done.1.refs_1_
  39.3 0.0 collective-permute-done.2.refs_2_
  39.3 1.2 %collective-permute-done.3.refs_3_ = bf16[176,256]{1,0:T(8,128)(2,1)S(1)} collective-permute-done((bf16[176,256]{1,0:T(8,128)(2,1)S(1)}, bf16[176,256]{1,0:T(8,128)(2,1)S(1)}, u32[]{:S(2)}, u32[]{:S(2)}) %collective-permute-start.3) | collective-permute-done | bytes 90144 | tf_op jit(solution)/shard_map/ppermute | solution.py:201
  40.6 0.0 all-to-all-done.1.x_ref
  40.6 7.1 %all-to-all-start = ((bf16[8,208,128]{2,1,0:T(8,128)(2,1)}), bf16[8,208,128]{2,1,0:T(8,128)(2,1)S(1)}, u32[]{:S(2)}, u32[]{:S(2)}) async-start(bf16[8,208,128]{2,1,0:T(8,128)(2,1)} %shard_map.96), calls=%async_computation | async-start | bytes 851968 | tf_op jit(solution)/shard_map/all_to_all | solution.py:246
  47.7 7.7 %shard_map.98 = (bf16[8,352,128]{2,1,0:T(8,128)(2,1)}, bf16[80,256]{1,0:T(8,128)(2,1)S(1)}, bf16[80,256]{1,0:T(8,128)(2,1)S(1)}, bf16[80,256]{1,0:T(8,128)(2,1)S(1)}, bf16[80,256]{1,0:T(8,128)(2,1)S(1)}) custom-call(bf16[8,320,128]{2,1,0:T(8,128)(2,1)S(1)} %all-to-all-done.1.x_ref, bf16[176,256]{1,0:T(8,128)(2,1)S(1)} %get-tuple-element.24.refs_0_, ...), custom_call_target="tpu_custom_call" | custom-call | flops 1677721600 | bytes 2097152 | tf_op jit(solution)/shard_map/pallas_call | solution.py:249
  55.3 6.6 %all-to-all-done.parts_ref = bf16[8,208,128]{2,1,0:T(8,128)(2,1)S(1)} async-done(((bf16[8,208,128]{2,1,0:T(8,128)(2,1)}), bf16[8,208,128]{2,1,0:T(8,128)(2,1)S(1)}, u32[]{:S(2)}, u32[]{:S(2)}) %all-to-all-start) | async-done | bytes 426016 | tf_op jit(solution)/shard_map/all_to_all | solution.py:246
  61.9 0.7 shard_map.99
  62.6 5.6 %all-to-all-start.2 = ((bf16[8,352,128]{2,1,0:T(8,128)(2,1)}), bf16[8,352,128]{2,1,0:T(8,128)(2,1)S(1)}, u32[]{:S(2)}, u32[]{:S(2)}) async-start(bf16[8,352,128]{2,1,0:T(8,128)(2,1)} %shard_map.99), calls=%async_computation.2 | async-start | bytes 1441792 | tf_op jit(solution)/shard_map/all_to_all | solution.py:274
  68.2 4.8 %collective-permute-start.4 = (bf16[80,256]{1,0:T(8,128)(2,1)S(1)}, bf16[80,256]{1,0:T(8,128)(2,1)S(1)}, u32[]{:S(2)}, u32[]{:S(2)}) collective-permute-start(bf16[80,256]{1,0:T(8,128)(2,1)S(1)} %get-tuple-element.27), channel_id=1, source_target_pairs={{24,0},{12,4},{0,8},{20,12},{8,16},{28,20},{16,24},{4,28},{25,1},{... | collective-permute-start | bytes 122888 | tf_op jit(solution)/shard_map/ppermute | solution.py:201
  73.1 4.6 %collective-permute-start.5 = (bf16[80,256]{1,0:T(8,128)(2,1)S(1)}, bf16[80,256]{1,0:T(8,128)(2,1)S(1)}, u32[]{:S(2)}, u32[]{:S(2)}) collective-permute-start(bf16[80,256]{1,0:T(8,128)(2,1)S(1)} %get-tuple-element.28), channel_id=1, source_target_pairs={{4,0},{8,4},{12,8},{16,12},{20,16},{24,20},{28,24},{0,28},{5,1},{9... | collective-permute-start | bytes 122888 | tf_op jit(solution)/shard_map/ppermute | solution.py:201
  77.6 1.9 %collective-permute-start.6 = (bf16[80,256]{1,0:T(8,128)(2,1)S(1)}, bf16[80,256]{1,0:T(8,128)(2,1)S(1)}, u32[]{:S(2)}, u32[]{:S(2)}) collective-permute-start(bf16[80,256]{1,0:T(8,128)(2,1)S(1)} %get-tuple-element.29), channel_id=1, source_target_pairs={{28,0},{0,4},{4,8},{8,12},{12,16},{16,20},{20,24},{24,28},{29,1},{... | collective-permute-start | bytes 122888 | tf_op jit(solution)/shard_map/ppermute | solution.py:201
  79.6 7.6 %collective-permute-done.4.refs_1_ = bf16[80,256]{1,0:T(8,128)(2,1)S(1)} collective-permute-done((bf16[80,256]{1,0:T(8,128)(2,1)S(1)}, bf16[80,256]{1,0:T(8,128)(2,1)S(1)}, u32[]{:S(2)}, u32[]{:S(2)}) %collective-permute-start.4) | collective-permute-done | bytes 40992 | tf_op jit(solution)/shard_map/ppermute | solution.py:201
  87.2 0.0 collective-permute-done.5.refs_2_
  87.2 0.0 collective-permute-done.6.refs_3_
  87.2 2.2 %all-to-all-done.2.x_ref = bf16[8,352,128]{2,1,0:T(8,128)(2,1)S(1)} async-done(((bf16[8,352,128]{2,1,0:T(8,128)(2,1)}), bf16[8,352,128]{2,1,0:T(8,128)(2,1)S(1)}, u32[]{:S(2)}, u32[]{:S(2)}) %all-to-all-start.2) | async-done | bytes 720928 | tf_op jit(solution)/shard_map/all_to_all | solution.py:274
  89.4 0.8 shard_map.100
  (1 shorter events, 0.0 us)
Async XLA Ops:
  2.5 10.5 %copy-start.3 = (bf16[256,320]{0,1:T(8,128)(2,1)S(1)}, bf16[256,320]{0,1:T(8,128)(2,1)}, u32[]{:S(2)}) copy-start(bf16[256,320]{0,1:T(8,128)(2,1)} %param.10) | copy-start | bytes 491524
  2.6 18.2 %copy-start.1 = (bf16[256,320]{0,1:T(8,128)(2,1)S(1)}, bf16[256,320]{0,1:T(8,128)(2,1)}, u32[]{:S(2)}) copy-start(bf16[256,320]{0,1:T(8,128)(2,1)} %param.9) | copy-start | bytes 491524
  2.6 38.0 %all-to-all-start.1 = ((bf16[8,320,128]{2,1,0:T(8,128)(2,1)}), bf16[8,320,128]{2,1,0:T(8,128)(2,1)S(1)}, u32[]{:S(2)}, u32[]{:S(2)}) async-start(bf16[8,320,128]{2,1,0:T(8,128)(2,1)} %shard_map.97), calls=%async_computation.1 | async-start | bytes 1310720 | tf_op jit(solution)/shard_map/all_to_all | solution.py:219
  13.0 11.4 %copy-start = (bf16[320,1280]{1,0:T(8,128)(2,1)S(1)}, bf16[320,1280]{1,0:T(8,128)(2,1)}, u32[]{:S(2)}) copy-start(bf16[320,1280]{1,0:T(8,128)(2,1)} %w_ref.1) | copy-start | bytes 2457604
  20.8 3.7 %copy-start.2 = (bf16[256,320]{0,1:T(8,128)(2,1)S(1)}, bf16[256,320]{0,1:T(8,128)(2,1)}, u32[]{:S(2)}) copy-start(bf16[256,320]{0,1:T(8,128)(2,1)} %param.6) | copy-start | bytes 491524
  21.7 16.7 %collective-permute-start = (bf16[8,208,128]{2,1,0:T(8,128)(2,1)S(1)}, bf16[8,208,128]{2,1,0:T(8,128)(2,1)S(1)}, u32[]{:S(2)}, u32[]{:S(2)}) collective-permute-start(bf16[8,208,128]{2,1,0:T(8,128)(2,1)S(1)} %get-tuple-element.20), channel_id=1, source_target_pairs={{0,32},{32,0},{64,96},{96,64},{128,160},{160,128},{192,224},{224,1... | collective-permute-start | bytes 1277960 | tf_op jit(solution)/shard_map/ppermute | solution.py:225
  25.3 14.0 %collective-permute-start.1 = (bf16[176,256]{1,0:T(8,128)(2,1)S(1)}, bf16[176,256]{1,0:T(8,128)(2,1)S(1)}, u32[]{:S(2)}, u32[]{:S(2)}) collective-permute-start(bf16[176,256]{1,0:T(8,128)(2,1)S(1)} %get-tuple-element.21), channel_id=1, source_target_pairs={{0,24},{4,12},{8,0},{12,20},{16,8},{20,28},{24,16},{28,4},{1,25},{... | collective-permute-start | bytes 270344 | tf_op jit(solution)/shard_map/ppermute | solution.py:201
  31.4 7.9 %collective-permute-start.2 = (bf16[176,256]{1,0:T(8,128)(2,1)S(1)}, bf16[176,256]{1,0:T(8,128)(2,1)S(1)}, u32[]{:S(2)}, u32[]{:S(2)}) collective-permute-start(bf16[176,256]{1,0:T(8,128)(2,1)S(1)} %get-tuple-element.22), channel_id=1, source_target_pairs={{0,4},{4,8},{8,12},{12,16},{16,20},{20,24},{24,28},{28,0},{1,5},{5... | collective-permute-start | bytes 270344 | tf_op jit(solution)/shard_map/ppermute | solution.py:201
  33.5 7.0 %collective-permute-start.3 = (bf16[176,256]{1,0:T(8,128)(2,1)S(1)}, bf16[176,256]{1,0:T(8,128)(2,1)S(1)}, u32[]{:S(2)}, u32[]{:S(2)}) collective-permute-start(bf16[176,256]{1,0:T(8,128)(2,1)S(1)} %get-tuple-element.23), channel_id=1, source_target_pairs={{0,28},{4,0},{8,4},{12,8},{16,12},{20,16},{24,20},{28,24},{1,29},{... | collective-permute-start | bytes 270344 | tf_op jit(solution)/shard_map/ppermute | solution.py:201
  40.6 21.3 %all-to-all-start = ((bf16[8,208,128]{2,1,0:T(8,128)(2,1)}), bf16[8,208,128]{2,1,0:T(8,128)(2,1)S(1)}, u32[]{:S(2)}, u32[]{:S(2)}) async-start(bf16[8,208,128]{2,1,0:T(8,128)(2,1)} %shard_map.96), calls=%async_computation | async-start | bytes 851968 | tf_op jit(solution)/shard_map/all_to_all | solution.py:246
  62.6 26.7 %all-to-all-start.2 = ((bf16[8,352,128]{2,1,0:T(8,128)(2,1)}), bf16[8,352,128]{2,1,0:T(8,128)(2,1)S(1)}, u32[]{:S(2)}, u32[]{:S(2)}) async-start(bf16[8,352,128]{2,1,0:T(8,128)(2,1)} %shard_map.99), calls=%async_computation.2 | async-start | bytes 1441792 | tf_op jit(solution)/shard_map/all_to_all | solution.py:274
  68.2 19.0 %collective-permute-start.4 = (bf16[80,256]{1,0:T(8,128)(2,1)S(1)}, bf16[80,256]{1,0:T(8,128)(2,1)S(1)}, u32[]{:S(2)}, u32[]{:S(2)}) collective-permute-start(bf16[80,256]{1,0:T(8,128)(2,1)S(1)} %get-tuple-element.27), channel_id=1, source_target_pairs={{24,0},{12,4},{0,8},{20,12},{8,16},{28,20},{16,24},{4,28},{25,1},{... | collective-permute-start | bytes 122888 | tf_op jit(solution)/shard_map/ppermute | solution.py:201
  73.1 14.1 %collective-permute-start.5 = (bf16[80,256]{1,0:T(8,128)(2,1)S(1)}, bf16[80,256]{1,0:T(8,128)(2,1)S(1)}, u32[]{:S(2)}, u32[]{:S(2)}) collective-permute-start(bf16[80,256]{1,0:T(8,128)(2,1)S(1)} %get-tuple-element.28), channel_id=1, source_target_pairs={{4,0},{8,4},{12,8},{16,12},{20,16},{24,20},{28,24},{0,28},{5,1},{9... | collective-permute-start | bytes 122888 | tf_op jit(solution)/shard_map/ppermute | solution.py:201
  77.6 9.6 %collective-permute-start.6 = (bf16[80,256]{1,0:T(8,128)(2,1)S(1)}, bf16[80,256]{1,0:T(8,128)(2,1)S(1)}, u32[]{:S(2)}, u32[]{:S(2)}) collective-permute-start(bf16[80,256]{1,0:T(8,128)(2,1)S(1)} %get-tuple-element.29), channel_id=1, source_target_pairs={{28,0},{0,4},{4,8},{8,12},{12,16},{16,20},{20,24},{24,28},{29,1},{... | collective-permute-start | bytes 122888 | tf_op jit(solution)/shard_map/ppermute | solution.py:201

commit v5 on v4

--- a/solution.py
+++ b/solution.py
@@ -34,18 +34,30 @@
     return lax.dot_general(left, right, dims, preferred_element_type=jnp.float32)
 
 
-def pack_keys_kernel(k_hbm, v_hbm, out_ref, k_ref, v_ref, sems):
-    pairs = ((k_hbm, k_ref), (v_hbm, v_ref))
-    copies = [pltpu.make_async_copy(x, y, sems.at[i]) for i, (x, y) in enumerate(pairs)]
-    for copy in copies:
-        copy.start()
-    for copy, ref, first in zip(copies, (k_ref, v_ref), (K_AT, V_AT)):
-        copy.wait()
-        for s in range(SHARDS):
-            j = s % HEADS_HERE
+def pack_keys_kernel(k_hbm, v_hbm, out_hbm, k_ref, v_ref, out_ref, in_sems, out_sems):
+    arrays = ((k_hbm, k_ref, K_AT), (v_hbm, v_ref, V_AT))
+    loads = []
+    for j in range(HEADS_HERE):
+        cols = pl.ds(j * HD, HD)
+        for i, (hbm, ref, _) in enumerate(arrays):
+            load = pltpu.make_async_copy(hbm.at[cols], ref.at[cols], in_sems.at[j, i])
+            load.start()
+            loads.append(load)
+    stores = []
+    for j in range(HEADS_HERE):
+        for i, (_, ref, first) in enumerate(arrays):
+            loads[2 * j + i].wait()
             for b in range(2):
                 at = first + b * HD
-                out_ref[s, at : at + HD] = ref[j * HD : (j + 1) * HD, b * HALF : (b + 1) * HALF]
+                block = ref[j * HD : (j + 1) * HD, b * HALF : (b + 1) * HALF]
+                out_ref[j, at : at + HD] = block
+        for h in range(2):
+            there = h * HEADS_HERE + j
+            store = pltpu.make_async_copy(out_ref.at[j], out_hbm.at[there], out_sems.at[there])
+            store.start()
+            stores.append(store)
+    for store in stores:
+        store.wait()
 
 
 def pack_queries_kernel(q_hbm, o_hbm, cot_ref, w_ref, *refs):
@@ -83,14 +95,14 @@
         ref[2 * HD :] = extra_ref[rows]
 
 
-def proj_kernel(cot_ref, o_ref, kept_ref, given_ref):
+def proj_kernel(cot_ref, o_ref, kept_ref, given_ref, term_ref):
     upper = lax.rem(lax.axis_index("dp"), 2)
     empty = jnp.zeros((PG_USED - 200, HALF), jnp.float32)
+    term_ref[...] = dot(cot_ref[...], o_ref[...], NT)
     for ref, wanted in ((given_ref, 1 - upper), (kept_ref, upper)):
         for k in range(SHARDS):
-            d = 2 * k + wanted
-            start = pl.multiple_of(d * PG_ROWS, 16)
-            part = dot(cot_ref[pl.ds(start, PG_ROWS)], o_ref[...], NT)
+            start = pl.multiple_of((2 * k + wanted) * PG_ROWS, 8)
+            part = term_ref[pl.ds(start, PG_ROWS)]
             for c in range(2):
                 at = c * PG_ROWS
                 ref[k, at : at + PG_ROWS] = part[:, HALF * c : HALF * (c + 1)].astype(ref.dtype)
@@ -212,8 +224,14 @@
         pack_keys_kernel,
         shape((SHARDS, KV_ROWS, HALF), half),
         0,
-        scratch=[whole] * 2 + [pltpu.SemaphoreType.DMA((2,))],
+        scratch=[whole] * 2
+        + [
+            pltpu.VMEM((HEADS_HERE, KV_ROWS, HALF), half),
+            pltpu.SemaphoreType.DMA((HEADS_HERE, 2)),
+            pltpu.SemaphoreType.DMA((SHARDS,)),
+        ],
         in_specs=[anywhere] * 2,
+        out_specs=anywhere,
         mib=60,
     )(k, v)
     pairs = lax.all_to_all(pairs, "ctx", 0, 0, tiled=True)
@@ -221,7 +239,12 @@
     full_cot = lax.all_gather(cot, "tp", axis=0, tiled=True)
     flops = 2 * ROWS * WIDE * 4 * WIDE
     block = (SHARDS, PG_USED, HALF)
-    kept, given = call(proj_kernel, (shape(block, single), shape(block, half)), flops)(full_cot, o)
+    kept, given = call(
+        proj_kernel,
+        (shape(block, single), shape(block, half)),
+        flops,
+        scratch=[pltpu.VMEM((DP * PG_ROWS, WIDE), single)],
+    )(full_cot, o)
     taken = lax.ppermute(given, "dp", [(i, i ^ 1) for i in range(DP)])
     near = call(
         pack_queries_kernel,

time: 90.7 us -> 90.6 us (level)
  no operation moved by 1% of the time
where the time goes in v5:
time: 90.6 us; the launch traced here: 90 us
  starting transfers between devices  50.3 us (56%)
  waiting for transfers between devices  17.6 us (19%)
  Pallas kernels  13.5 us (15%)
  blocking collectives  7.72 us (9%)
    ppermute x6, starting transfers between devices, shifted_round(): lax.ppermute(x, 'ctx', [pair[::-1] for pair in pairs] if back else pairs)  24.4 us
    all_to_all x1, starting transfers between devices, on_device(): pairs = lax.all_to_all(pairs, 'ctx', 0, 0, tiled=True)  10.5 us
    ppermute x6, waiting for transfers between devices, shifted_round(): lax.ppermute(x, 'ctx', [pair[::-1] for pair in pairs] if back else pairs)  8.88 us
    all_gather x1, blocking collectives, on_device(): full_cot = lax.all_gather(cot, 'tp', axis=0, tiled=True)  7.72 us
    pallas_call x1, Pallas kernels, on_device(): call(grad_kernel, [shape((SHARDS, OUT_ROWS, HALF), half)] + [shape((HD, R...  7.65 us
    all_to_all x1, starting transfers between devices, on_device(): lax.all_to_all(parts, 'dp', 0, 0, tiled=True, axis_index_groups=along_y)  7.1 us
    all_to_all x1, waiting for transfers between devices, on_device(): lax.all_to_all(parts, 'dp', 0, 0, tiled=True, axis_index_groups=along_y)  6.56 us
    all_to_all x1, starting transfers between devices, on_device(): back = lax.all_to_all(sent, 'ctx', 0, 0, tiled=True)  5.68 us
  transfers between devices with their start and end apart: 10, of which 4 were waited for; matrix products, arithmetic and copies ran while one was open for 0% of the time, Pallas kernels for 11%

profile of v5, /device:TPU:4, one launch (start us, length us, event | category | flops | bytes accessed | tf_op | source)
XLA Modules:
  0.0 90.0 jit_solution(13369863729994001584)
XLA Ops:
  0.6 1.8 %shard_map.97 = bf16[8,320,128]{2,1,0:T(8,128)(2,1)} custom-call(bf16[320,256]{1,0:T(8,128)(2,1)} %bitcast.13, bf16[320,256]{1,0:T(8,128)(2,1)} %bitcast.14), custom_call_target="tpu_custom_call" | custom-call | bytes 2097152 | tf_op jit(solution)/shard_map/pallas_call | solution.py:223
  2.4 0.0 copy-start.3
  2.4 0.0 copy-start.1
  2.5 10.5 %all-to-all-start.1 = ((bf16[8,320,128]{2,1,0:T(8,128)(2,1)}), bf16[8,320,128]{2,1,0:T(8,128)(2,1)S(1)}, u32[]{:S(2)}, u32[]{:S(2)}) async-start(bf16[8,320,128]{2,1,0:T(8,128)(2,1)} %shard_map.97), calls=%async_computation.1 | async-start | bytes 1310720 | tf_op jit(solution)/shard_map/all_to_all | solution.py:237
  12.9 0.0 copy-done.3
  12.9 0.0 copy-start
  12.9 7.7 %all_gather.3.cot_ref = bf16[1280,256]{1,0:T(8,128)(2,1)S(1)} all-gather(bf16[320,256]{1,0:T(8,128)(2,1)S(1)} %bitcast.12), channel_id=1, replica_groups=mesh['dp'=16,'ctx'=8,'tp'=4] {'tp'}, dimensions={0}, use_global_device_ids=true | all-gather | bytes 819200 | tf_op jit(solution)/shard_map/all_gather | solution.py:239
  20.7 0.0 copy-done.1
  20.7 0.0 copy-start.2
  20.7 0.8 shard_map.93
  21.5 2.6 %collective-permute-start = (bf16[8,208,128]{2,1,0:T(8,128)(2,1)S(1)}, bf16[8,208,128]{2,1,0:T(8,128)(2,1)S(1)}, u32[]{:S(2)}, u32[]{:S(2)}) collective-permute-start(bf16[8,208,128]{2,1,0:T(8,128)(2,1)S(1)} %get-tuple-element.20), channel_id=1, source_target_pairs={{0,32},{32,0},{64,96},{96,64},{128,160},{160,128},{192,224},{224,1... | collective-permute-start | bytes 1277960 | tf_op jit(solution)/shard_map/ppermute | solution.py:248
  24.1 0.0 copy-done
  24.2 0.0 copy-done.2
  24.2 0.9 shard_map.95
  25.0 6.0 %collective-permute-start.1 = (bf16[176,256]{1,0:T(8,128)(2,1)S(1)}, bf16[176,256]{1,0:T(8,128)(2,1)S(1)}, u32[]{:S(2)}, u32[]{:S(2)}) collective-permute-start(bf16[176,256]{1,0:T(8,128)(2,1)S(1)} %get-tuple-element.21), channel_id=1, source_target_pairs={{0,24},{4,12},{8,0},{12,20},{16,8},{20,28},{24,16},{28,4},{1,25},{... | collective-permute-start | bytes 270344 | tf_op jit(solution)/shard_map/ppermute | solution.py:213
  31.1 2.2 %collective-permute-start.2 = (bf16[176,256]{1,0:T(8,128)(2,1)S(1)}, bf16[176,256]{1,0:T(8,128)(2,1)S(1)}, u32[]{:S(2)}, u32[]{:S(2)}) collective-permute-start(bf16[176,256]{1,0:T(8,128)(2,1)S(1)} %get-tuple-element.22), channel_id=1, source_target_pairs={{0,4},{4,8},{8,12},{12,16},{16,20},{20,24},{24,28},{28,0},{1,5},{5... | collective-permute-start | bytes 270344 | tf_op jit(solution)/shard_map/ppermute | solution.py:213
  33.3 4.9 %collective-permute-start.3 = (bf16[176,256]{1,0:T(8,128)(2,1)S(1)}, bf16[176,256]{1,0:T(8,128)(2,1)S(1)}, u32[]{:S(2)}, u32[]{:S(2)}) collective-permute-start(bf16[176,256]{1,0:T(8,128)(2,1)S(1)} %get-tuple-element.23), channel_id=1, source_target_pairs={{0,28},{4,0},{8,4},{12,8},{16,12},{20,16},{24,20},{28,24},{1,29},{... | collective-permute-start | bytes 270344 | tf_op jit(solution)/shard_map/ppermute | solution.py:213
  38.2 0.0 collective-permute-done.taken_ref
  38.2 0.9 shard_map.94.refs_0_
  39.0 0.0 collective-permute-done.1.refs_1_
  39.0 0.0 collective-permute-done.2.refs_2_
  39.0 1.2 %collective-permute-done.3.refs_3_ = bf16[176,256]{1,0:T(8,128)(2,1)S(1)} collective-permute-done((bf16[176,256]{1,0:T(8,128)(2,1)S(1)}, bf16[176,256]{1,0:T(8,128)(2,1)S(1)}, u32[]{:S(2)}, u32[]{:S(2)}) %collective-permute-start.3) | collective-permute-done | bytes 90144 | tf_op jit(solution)/shard_map/ppermute | solution.py:213
  40.3 0.0 all-to-all-done.1.x_ref
  40.3 7.1 %all-to-all-start = ((bf16[8,208,128]{2,1,0:T(8,128)(2,1)}), bf16[8,208,128]{2,1,0:T(8,128)(2,1)S(1)}, u32[]{:S(2)}, u32[]{:S(2)}) async-start(bf16[8,208,128]{2,1,0:T(8,128)(2,1)} %shard_map.96), calls=%async_computation | async-start | bytes 851968 | tf_op jit(solution)/shard_map/all_to_all | solution.py:269
  47.4 7.7 %shard_map.98 = (bf16[8,352,128]{2,1,0:T(8,128)(2,1)}, bf16[80,256]{1,0:T(8,128)(2,1)S(1)}, bf16[80,256]{1,0:T(8,128)(2,1)S(1)}, bf16[80,256]{1,0:T(8,128)(2,1)S(1)}, bf16[80,256]{1,0:T(8,128)(2,1)S(1)}) custom-call(bf16[8,320,128]{2,1,0:T(8,128)(2,1)S(1)} %all-to-all-done.1.x_ref, bf16[176,256]{1,0:T(8,128)(2,1)S(1)} %get-tuple-element.24.refs_0_, ...), custom_call_target="tpu_custom_call" | custom-call | flops 1677721600 | bytes 2097152 | tf_op jit(solution)/shard_map/pallas_call | solution.py:272
  55.0 6.6 %all-to-all-done.parts_ref = bf16[8,208,128]{2,1,0:T(8,128)(2,1)S(1)} async-done(((bf16[8,208,128]{2,1,0:T(8,128)(2,1)}), bf16[8,208,128]{2,1,0:T(8,128)(2,1)S(1)}, u32[]{:S(2)}, u32[]{:S(2)}) %all-to-all-start) | async-done | bytes 426016 | tf_op jit(solution)/shard_map/all_to_all | solution.py:269
  61.6 0.7 shard_map.99
  62.3 5.7 %all-to-all-start.2 = ((bf16[8,352,128]{2,1,0:T(8,128)(2,1)}), bf16[8,352,128]{2,1,0:T(8,128)(2,1)S(1)}, u32[]{:S(2)}, u32[]{:S(2)}) async-start(bf16[8,352,128]{2,1,0:T(8,128)(2,1)} %shard_map.99), calls=%async_computation.2 | async-start | bytes 1441792 | tf_op jit(solution)/shard_map/all_to_all | solution.py:297
  68.0 4.8 %collective-permute-start.4 = (bf16[80,256]{1,0:T(8,128)(2,1)S(1)}, bf16[80,256]{1,0:T(8,128)(2,1)S(1)}, u32[]{:S(2)}, u32[]{:S(2)}) collective-permute-start(bf16[80,256]{1,0:T(8,128)(2,1)S(1)} %get-tuple-element.27), channel_id=1, source_target_pairs={{24,0},{12,4},{0,8},{20,12},{8,16},{28,20},{16,24},{4,28},{25,1},{... | collective-permute-start | bytes 122888 | tf_op jit(solution)/shard_map/ppermute | solution.py:213
  72.8 4.6 %collective-permute-start.5 = (bf16[80,256]{1,0:T(8,128)(2,1)S(1)}, bf16[80,256]{1,0:T(8,128)(2,1)S(1)}, u32[]{:S(2)}, u32[]{:S(2)}) collective-permute-start(bf16[80,256]{1,0:T(8,128)(2,1)S(1)} %get-tuple-element.28), channel_id=1, source_target_pairs={{4,0},{8,4},{12,8},{16,12},{20,16},{24,20},{28,24},{0,28},{5,1},{9... | collective-permute-start | bytes 122888 | tf_op jit(solution)/shard_map/ppermute | solution.py:213
  77.4 1.9 %collective-permute-start.6 = (bf16[80,256]{1,0:T(8,128)(2,1)S(1)}, bf16[80,256]{1,0:T(8,128)(2,1)S(1)}, u32[]{:S(2)}, u32[]{:S(2)}) collective-permute-start(bf16[80,256]{1,0:T(8,128)(2,1)S(1)} %get-tuple-element.29), channel_id=1, source_target_pairs={{28,0},{0,4},{4,8},{8,12},{12,16},{16,20},{20,24},{24,28},{29,1},{... | collective-permute-start | bytes 122888 | tf_op jit(solution)/shard_map/ppermute | solution.py:213
  79.3 7.6 %collective-permute-done.4.refs_1_ = bf16[80,256]{1,0:T(8,128)(2,1)S(1)} collective-permute-done((bf16[80,256]{1,0:T(8,128)(2,1)S(1)}, bf16[80,256]{1,0:T(8,128)(2,1)S(1)}, u32[]{:S(2)}, u32[]{:S(2)}) %collective-permute-start.4) | collective-permute-done | bytes 40992 | tf_op jit(solution)/shard_map/ppermute | solution.py:213
  87.0 0.0 collective-permute-done.5.refs_2_
  87.0 0.0 collective-permute-done.6.refs_3_
  87.0 2.1 %all-to-all-done.2.x_ref = bf16[8,352,128]{2,1,0:T(8,128)(2,1)S(1)} async-done(((bf16[8,352,128]{2,1,0:T(8,128)(2,1)}), bf16[8,352,128]{2,1,0:T(8,128)(2,1)S(1)}, u32[]{:S(2)}, u32[]{:S(2)}) %all-to-all-start.2) | async-done | bytes 720928 | tf_op jit(solution)/shard_map/all_to_all | solution.py:297
  89.1 0.8 shard_map.100
  (1 shorter events, 0.0 us)
Async XLA Ops:
  2.4 10.5 %copy-start.3 = (bf16[256,320]{0,1:T(8,128)(2,1)S(1)}, bf16[256,320]{0,1:T(8,128)(2,1)}, u32[]{:S(2)}) copy-start(bf16[256,320]{0,1:T(8,128)(2,1)} %param.10) | copy-start | bytes 491524
  2.4 18.2 %copy-start.1 = (bf16[256,320]{0,1:T(8,128)(2,1)S(1)}, bf16[256,320]{0,1:T(8,128)(2,1)}, u32[]{:S(2)}) copy-start(bf16[256,320]{0,1:T(8,128)(2,1)} %param.9) | copy-start | bytes 491524
  2.5 37.8 %all-to-all-start.1 = ((bf16[8,320,128]{2,1,0:T(8,128)(2,1)}), bf16[8,320,128]{2,1,0:T(8,128)(2,1)S(1)}, u32[]{:S(2)}, u32[]{:S(2)}) async-start(bf16[8,320,128]{2,1,0:T(8,128)(2,1)} %shard_map.97), calls=%async_computation.1 | async-start | bytes 1310720 | tf_op jit(solution)/shard_map/all_to_all | solution.py:237
  12.9 11.2 %copy-start = (bf16[320,1280]{1,0:T(8,128)(2,1)S(1)}, bf16[320,1280]{1,0:T(8,128)(2,1)}, u32[]{:S(2)}) copy-start(bf16[320,1280]{1,0:T(8,128)(2,1)} %w_ref.1) | copy-start | bytes 2457604
  20.7 3.5 %copy-start.2 = (bf16[256,320]{0,1:T(8,128)(2,1)S(1)}, bf16[256,320]{0,1:T(8,128)(2,1)}, u32[]{:S(2)}) copy-start(bf16[256,320]{0,1:T(8,128)(2,1)} %param.6) | copy-start | bytes 491524
  21.5 16.7 %collective-permute-start = (bf16[8,208,128]{2,1,0:T(8,128)(2,1)S(1)}, bf16[8,208,128]{2,1,0:T(8,128)(2,1)S(1)}, u32[]{:S(2)}, u32[]{:S(2)}) collective-permute-start(bf16[8,208,128]{2,1,0:T(8,128)(2,1)S(1)} %get-tuple-element.20), channel_id=1, source_target_pairs={{0,32},{32,0},{64,96},{96,64},{128,160},{160,128},{192,224},{224,1... | collective-permute-start | bytes 1277960 | tf_op jit(solution)/shard_map/ppermute | solution.py:248
  25.0 14.0 %collective-permute-start.1 = (bf16[176,256]{1,0:T(8,128)(2,1)S(1)}, bf16[176,256]{1,0:T(8,128)(2,1)S(1)}, u32[]{:S(2)}, u32[]{:S(2)}) collective-permute-start(bf16[176,256]{1,0:T(8,128)(2,1)S(1)} %get-tuple-element.21), channel_id=1, source_target_pairs={{0,24},{4,12},{8,0},{12,20},{16,8},{20,28},{24,16},{28,4},{1,25},{... | collective-permute-start | bytes 270344 | tf_op jit(solution)/shard_map/ppermute | solution.py:213
  31.1 7.9 %collective-permute-start.2 = (bf16[176,256]{1,0:T(8,128)(2,1)S(1)}, bf16[176,256]{1,0:T(8,128)(2,1)S(1)}, u32[]{:S(2)}, u32[]{:S(2)}) collective-permute-start(bf16[176,256]{1,0:T(8,128)(2,1)S(1)} %get-tuple-element.22), channel_id=1, source_target_pairs={{0,4},{4,8},{8,12},{12,16},{16,20},{20,24},{24,28},{28,0},{1,5},{5... | collective-permute-start | bytes 270344 | tf_op jit(solution)/shard_map/ppermute | solution.py:213
  33.3 7.0 %collective-permute-start.3 = (bf16[176,256]{1,0:T(8,128)(2,1)S(1)}, bf16[176,256]{1,0:T(8,128)(2,1)S(1)}, u32[]{:S(2)}, u32[]{:S(2)}) collective-permute-start(bf16[176,256]{1,0:T(8,128)(2,1)S(1)} %get-tuple-element.23), channel_id=1, source_target_pairs={{0,28},{4,0},{8,4},{12,8},{16,12},{20,16},{24,20},{28,24},{1,29},{... | collective-permute-start | bytes 270344 | tf_op jit(solution)/shard_map/ppermute | solution.py:213
  40.3 21.3 %all-to-all-start = ((bf16[8,208,128]{2,1,0:T(8,128)(2,1)}), bf16[8,208,128]{2,1,0:T(8,128)(2,1)S(1)}, u32[]{:S(2)}, u32[]{:S(2)}) async-start(bf16[8,208,128]{2,1,0:T(8,128)(2,1)} %shard_map.96), calls=%async_computation | async-start | bytes 851968 | tf_op jit(solution)/shard_map/all_to_all | solution.py:269
  62.3 26.8 %all-to-all-start.2 = ((bf16[8,352,128]{2,1,0:T(8,128)(2,1)}), bf16[8,352,128]{2,1,0:T(8,128)(2,1)S(1)}, u32[]{:S(2)}, u32[]{:S(2)}) async-start(bf16[8,352,128]{2,1,0:T(8,128)(2,1)} %shard_map.99), calls=%async_computation.2 | async-start | bytes 1441792 | tf_op jit(solution)/shard_map/all_to_all | solution.py:297
  68.0 19.0 %collective-permute-start.4 = (bf16[80,256]{1,0:T(8,128)(2,1)S(1)}, bf16[80,256]{1,0:T(8,128)(2,1)S(1)}, u32[]{:S(2)}, u32[]{:S(2)}) collective-permute-start(bf16[80,256]{1,0:T(8,128)(2,1)S(1)} %get-tuple-element.27), channel_id=1, source_target_pairs={{24,0},{12,4},{0,8},{20,12},{8,16},{28,20},{16,24},{4,28},{25,1},{... | collective-permute-start | bytes 122888 | tf_op jit(solution)/shard_map/ppermute | solution.py:213
  72.8 14.2 %collective-permute-start.5 = (bf16[80,256]{1,0:T(8,128)(2,1)S(1)}, bf16[80,256]{1,0:T(8,128)(2,1)S(1)}, u32[]{:S(2)}, u32[]{:S(2)}) collective-permute-start(bf16[80,256]{1,0:T(8,128)(2,1)S(1)} %get-tuple-element.28), channel_id=1, source_target_pairs={{4,0},{8,4},{12,8},{16,12},{20,16},{24,20},{28,24},{0,28},{5,1},{9... | collective-permute-start | bytes 122888 | tf_op jit(solution)/shard_map/ppermute | solution.py:213
  77.4 9.6 %collective-permute-start.6 = (bf16[80,256]{1,0:T(8,128)(2,1)S(1)}, bf16[80,256]{1,0:T(8,128)(2,1)S(1)}, u32[]{:S(2)}, u32[]{:S(2)}) collective-permute-start(bf16[80,256]{1,0:T(8,128)(2,1)S(1)} %get-tuple-element.29), channel_id=1, source_target_pairs={{28,0},{0,4},{4,8},{8,12},{12,16},{16,20},{20,24},{24,28},{29,1},{... | collective-permute-start | bytes 122888 | tf_op jit(solution)/shard_map/ppermute | solution.py:213

commit v6 on v5

--- a/solution.py
+++ b/solution.py
@@ -18,7 +18,7 @@
 LOG2E = math.log2(math.e)
 EXT = 96
 QG_ROWS = HD + EXT
-K_AT, V_AT, KV_ROWS = 0, 2 * HD, 4 * HD
+K_AT, V_AT = 0, 2 * HD
 PG_AT, OUT_ROWS = 4 * HD, 4 * HD + 32
 PG_COLS = 10
 PG_ROWS = 80
@@ -34,28 +34,27 @@
     return lax.dot_general(left, right, dims, preferred_element_type=jnp.float32)
 
 
-def pack_keys_kernel(k_hbm, v_hbm, out_hbm, k_ref, v_ref, out_ref, in_sems, out_sems):
-    arrays = ((k_hbm, k_ref, K_AT), (v_hbm, v_ref, V_AT))
-    loads = []
+def pack_keys_kernel(k_hbm, v_hbm, out_hbm, k_ref, v_ref, in_sems, out_sems):
+    arrays = ((k_hbm, k_ref), (v_hbm, v_ref))
+    loads, stores = [], []
     for j in range(HEADS_HERE):
         cols = pl.ds(j * HD, HD)
-        for i, (hbm, ref, _) in enumerate(arrays):
+        for i, (hbm, ref) in enumerate(arrays):
             load = pltpu.make_async_copy(hbm.at[cols], ref.at[cols], in_sems.at[j, i])
             load.start()
             loads.append(load)
-    stores = []
     for j in range(HEADS_HERE):
-        for i, (_, ref, first) in enumerate(arrays):
+        for i, (_, ref) in enumerate(arrays):
             loads[2 * j + i].wait()
-            for b in range(2):
-                at = first + b * HD
-                block = ref[j * HD : (j + 1) * HD, b * HALF : (b + 1) * HALF]
-                out_ref[j, at : at + HD] = block
-        for h in range(2):
-            there = h * HEADS_HERE + j
-            store = pltpu.make_async_copy(out_ref.at[j], out_hbm.at[there], out_sems.at[there])
-            store.start()
-            stores.append(store)
+            for h in range(2):
+                there = h * HEADS_HERE + j
+                store = pltpu.make_async_copy(
+                    ref.at[pl.ds(j * HD, HD)],
+                    out_hbm.at[there, pl.ds(i * HD, HD)],
+                    out_sems.at[there, i],
+                )
+                store.start()
+                stores.append(store)
     for store in stores:
         store.wait()
 
@@ -140,10 +139,9 @@
     near, (out_ref, *dq_refs) = refs[: len(NEAR)], refs[len(NEAR) : 2 * len(NEAR) + 1]
     k_t, v_t, dk, dv = refs[2 * len(NEAR) + 1 :]
     for s in range(SHARDS):
-        for b in range(2):
-            tokens = slice((2 * s + b) * HALF, (2 * s + b + 1) * HALF)
-            k_t[:, tokens] = x_ref[s, K_AT + b * HD : K_AT + (b + 1) * HD]
-            v_t[:HD, tokens] = x_ref[s, V_AT + b * HD : V_AT + (b + 1) * HD]
+        tokens = slice(s * ROWS, (s + 1) * ROWS)
+        k_t[:, tokens] = x_ref[s, :HD]
+        v_t[:HD, tokens] = x_ref[s, HD:]
     row = lax.broadcasted_iota(jnp.int32, (EXT - HD, SHARDS * ROWS), 0)
     v_t[HD:] = jnp.where(row < 3, -1.0, 0.0).astype(jnp.bfloat16)
     for i, (block, dq_ref) in enumerate(zip(near, dq_refs)):
@@ -222,14 +220,10 @@
 
     pairs = call(
         pack_keys_kernel,
-        shape((SHARDS, KV_ROWS, HALF), half),
+        shape((SHARDS, 2 * HD, ROWS), half),
         0,
         scratch=[whole] * 2
-        + [
-            pltpu.VMEM((HEADS_HERE, KV_ROWS, HALF), half),
-            pltpu.SemaphoreType.DMA((HEADS_HERE, 2)),
-            pltpu.SemaphoreType.DMA((SHARDS,)),
-        ],
+        + [pltpu.SemaphoreType.DMA((HEADS_HERE, 2)), pltpu.SemaphoreType.DMA((SHARDS, 2))],
         in_specs=[anywhere] * 2,
         out_specs=anywhere,
         mib=60,

time: 90.6 us -> 90.6 us (level)
  no operation moved by 1% of the time
where the time goes in v6:
time: 90.6 us; the launch traced here: 90 us
  starting transfers between devices  50.3 us (56%)
  waiting for transfers between devices  17.6 us (19%)
  Pallas kernels  13.6 us (15%)
  blocking collectives  7.72 us (9%)
    ppermute x6, starting transfers between devices, shifted_round(): lax.ppermute(x, 'ctx', [pair[::-1] for pair in pairs] if back else pairs)  24.4 us
    all_to_all x1, starting transfers between devices, on_device(): pairs = lax.all_to_all(pairs, 'ctx', 0, 0, tiled=True)  10.5 us
    ppermute x6, waiting for transfers between devices, shifted_round(): lax.ppermute(x, 'ctx', [pair[::-1] for pair in pairs] if back else pairs)  8.88 us
    all_gather x1, blocking collectives, on_device(): full_cot = lax.all_gather(cot, 'tp', axis=0, tiled=True)  7.72 us
    pallas_call x1, Pallas kernels, on_device(): call(grad_kernel, [shape((SHARDS, OUT_ROWS, HALF), half)] + [shape((HD, R...  7.62 us
    all_to_all x1, starting transfers between devices, on_device(): lax.all_to_all(parts, 'dp', 0, 0, tiled=True, axis_index_groups=along_y)  7.1 us
    all_to_all x1, waiting for transfers between devices, on_device(): lax.all_to_all(parts, 'dp', 0, 0, tiled=True, axis_index_groups=along_y)  6.59 us
    all_to_all x1, starting transfers between devices, on_device(): back = lax.all_to_all(sent, 'ctx', 0, 0, tiled=True)  5.68 us
  transfers between devices with their start and end apart: 10, of which 4 were waited for; matrix products, arithmetic and copies ran while one was open for 0% of the time, Pallas kernels for 11%

profile of v6, /device:TPU:4, one launch (start us, length us, event | category | flops | bytes accessed | tf_op | source)
XLA Modules:
  0.0 90.0 jit_solution(14785915078454380188)
XLA Ops:
  0.6 1.8 %shard_map.97 = bf16[8,160,256]{2,1,0:T(8,128)(2,1)} custom-call(bf16[320,256]{1,0:T(8,128)(2,1)} %bitcast.13, bf16[320,256]{1,0:T(8,128)(2,1)} %bitcast.14), custom_call_target="tpu_custom_call" | custom-call | bytes 2097152 | tf_op jit(solution)/shard_map/pallas_call | solution.py:221
  2.5 0.0 copy-start.3
  2.5 0.0 copy-start.1
  2.5 10.5 %all-to-all-start.1 = ((bf16[8,160,256]{2,1,0:T(8,128)(2,1)}), bf16[8,160,256]{2,1,0:T(8,128)(2,1)S(1)}, u32[]{:S(2)}, u32[]{:S(2)}) async-start(bf16[8,160,256]{2,1,0:T(8,128)(2,1)} %shard_map.97), calls=%async_computation.1 | async-start | bytes 1310720 | tf_op jit(solution)/shard_map/all_to_all | solution.py:231
  13.0 0.0 copy-done.3
  13.0 0.0 copy-start
  13.0 7.7 %all_gather.3.cot_ref = bf16[1280,256]{1,0:T(8,128)(2,1)S(1)} all-gather(bf16[320,256]{1,0:T(8,128)(2,1)S(1)} %bitcast.12), channel_id=1, replica_groups=mesh['dp'=16,'ctx'=8,'tp'=4] {'tp'}, dimensions={0}, use_global_device_ids=true | all-gather | bytes 819200 | tf_op jit(solution)/shard_map/all_gather | solution.py:233
  20.7 0.0 copy-done.1
  20.7 0.0 copy-start.2
  20.7 0.8 shard_map.93
  21.5 2.7 %collective-permute-start = (bf16[8,208,128]{2,1,0:T(8,128)(2,1)S(1)}, bf16[8,208,128]{2,1,0:T(8,128)(2,1)S(1)}, u32[]{:S(2)}, u32[]{:S(2)}) collective-permute-start(bf16[8,208,128]{2,1,0:T(8,128)(2,1)S(1)} %get-tuple-element.20), channel_id=1, source_target_pairs={{0,32},{32,0},{64,96},{96,64},{128,160},{160,128},{192,224},{224,1... | collective-permute-start | bytes 1277960 | tf_op jit(solution)/shard_map/ppermute | solution.py:242
  24.2 0.0 copy-done
  24.2 0.0 copy-done.2
  24.2 0.9 shard_map.95
  25.1 6.0 %collective-permute-start.1 = (bf16[176,256]{1,0:T(8,128)(2,1)S(1)}, bf16[176,256]{1,0:T(8,128)(2,1)S(1)}, u32[]{:S(2)}, u32[]{:S(2)}) collective-permute-start(bf16[176,256]{1,0:T(8,128)(2,1)S(1)} %get-tuple-element.21), channel_id=1, source_target_pairs={{0,24},{4,12},{8,0},{12,20},{16,8},{20,28},{24,16},{28,4},{1,25},{... | collective-permute-start | bytes 270344 | tf_op jit(solution)/shard_map/ppermute | solution.py:211
  31.1 2.2 %collective-permute-start.2 = (bf16[176,256]{1,0:T(8,128)(2,1)S(1)}, bf16[176,256]{1,0:T(8,128)(2,1)S(1)}, u32[]{:S(2)}, u32[]{:S(2)}) collective-permute-start(bf16[176,256]{1,0:T(8,128)(2,1)S(1)} %get-tuple-element.22), channel_id=1, source_target_pairs={{0,4},{4,8},{8,12},{12,16},{16,20},{20,24},{24,28},{28,0},{1,5},{5... | collective-permute-start | bytes 270344 | tf_op jit(solution)/shard_map/ppermute | solution.py:211
  33.3 4.9 %collective-permute-start.3 = (bf16[176,256]{1,0:T(8,128)(2,1)S(1)}, bf16[176,256]{1,0:T(8,128)(2,1)S(1)}, u32[]{:S(2)}, u32[]{:S(2)}) collective-permute-start(bf16[176,256]{1,0:T(8,128)(2,1)S(1)} %get-tuple-element.23), channel_id=1, source_target_pairs={{0,28},{4,0},{8,4},{12,8},{16,12},{20,16},{24,20},{28,24},{1,29},{... | collective-permute-start | bytes 270344 | tf_op jit(solution)/shard_map/ppermute | solution.py:211
  38.2 0.0 collective-permute-done.taken_ref
  38.2 0.9 shard_map.94.refs_0_
  39.1 0.0 collective-permute-done.1.refs_1_
  39.1 0.0 collective-permute-done.2.refs_2_
  39.1 1.2 %collective-permute-done.3.refs_3_ = bf16[176,256]{1,0:T(8,128)(2,1)S(1)} collective-permute-done((bf16[176,256]{1,0:T(8,128)(2,1)S(1)}, bf16[176,256]{1,0:T(8,128)(2,1)S(1)}, u32[]{:S(2)}, u32[]{:S(2)}) %collective-permute-start.3) | collective-permute-done | bytes 90144 | tf_op jit(solution)/shard_map/ppermute | solution.py:211
  40.3 0.0 all-to-all-done.1.x_ref
  40.3 7.1 %all-to-all-start = ((bf16[8,208,128]{2,1,0:T(8,128)(2,1)}), bf16[8,208,128]{2,1,0:T(8,128)(2,1)S(1)}, u32[]{:S(2)}, u32[]{:S(2)}) async-start(bf16[8,208,128]{2,1,0:T(8,128)(2,1)} %shard_map.96), calls=%async_computation | async-start | bytes 851968 | tf_op jit(solution)/shard_map/all_to_all | solution.py:263
  47.4 7.6 %shard_map.98 = (bf16[8,352,128]{2,1,0:T(8,128)(2,1)}, bf16[80,256]{1,0:T(8,128)(2,1)S(1)}, bf16[80,256]{1,0:T(8,128)(2,1)S(1)}, bf16[80,256]{1,0:T(8,128)(2,1)S(1)}, bf16[80,256]{1,0:T(8,128)(2,1)S(1)}) custom-call(bf16[8,160,256]{2,1,0:T(8,128)(2,1)S(1)} %all-to-all-done.1.x_ref, bf16[176,256]{1,0:T(8,128)(2,1)S(1)} %get-tuple-element.24.refs_0_, ...), custom_call_target="tpu_custom_call" | custom-call | flops 1677721600 | bytes 2097152 | tf_op jit(solution)/shard_map/pallas_call | solution.py:266
  55.0 6.6 %all-to-all-done.parts_ref = bf16[8,208,128]{2,1,0:T(8,128)(2,1)S(1)} async-done(((bf16[8,208,128]{2,1,0:T(8,128)(2,1)}), bf16[8,208,128]{2,1,0:T(8,128)(2,1)S(1)}, u32[]{:S(2)}, u32[]{:S(2)}) %all-to-all-start) | async-done | bytes 426016 | tf_op jit(solution)/shard_map/all_to_all | solution.py:263
  61.6 0.7 shard_map.99
  62.4 5.7 %all-to-all-start.2 = ((bf16[8,352,128]{2,1,0:T(8,128)(2,1)}), bf16[8,352,128]{2,1,0:T(8,128)(2,1)S(1)}, u32[]{:S(2)}, u32[]{:S(2)}) async-start(bf16[8,352,128]{2,1,0:T(8,128)(2,1)} %shard_map.99), calls=%async_computation.2 | async-start | bytes 1441792 | tf_op jit(solution)/shard_map/all_to_all | solution.py:291
  68.0 4.8 %collective-permute-start.4 = (bf16[80,256]{1,0:T(8,128)(2,1)S(1)}, bf16[80,256]{1,0:T(8,128)(2,1)S(1)}, u32[]{:S(2)}, u32[]{:S(2)}) collective-permute-start(bf16[80,256]{1,0:T(8,128)(2,1)S(1)} %get-tuple-element.27), channel_id=1, source_target_pairs={{24,0},{12,4},{0,8},{20,12},{8,16},{28,20},{16,24},{4,28},{25,1},{... | collective-permute-start | bytes 122888 | tf_op jit(solution)/shard_map/ppermute | solution.py:211
  72.9 4.6 %collective-permute-start.5 = (bf16[80,256]{1,0:T(8,128)(2,1)S(1)}, bf16[80,256]{1,0:T(8,128)(2,1)S(1)}, u32[]{:S(2)}, u32[]{:S(2)}) collective-permute-start(bf16[80,256]{1,0:T(8,128)(2,1)S(1)} %get-tuple-element.28), channel_id=1, source_target_pairs={{4,0},{8,4},{12,8},{16,12},{20,16},{24,20},{28,24},{0,28},{5,1},{9... | collective-permute-start | bytes 122888 | tf_op jit(solution)/shard_map/ppermute | solution.py:211
  77.5 1.9 %collective-permute-start.6 = (bf16[80,256]{1,0:T(8,128)(2,1)S(1)}, bf16[80,256]{1,0:T(8,128)(2,1)S(1)}, u32[]{:S(2)}, u32[]{:S(2)}) collective-permute-start(bf16[80,256]{1,0:T(8,128)(2,1)S(1)} %get-tuple-element.29), channel_id=1, source_target_pairs={{28,0},{0,4},{4,8},{8,12},{12,16},{16,20},{20,24},{24,28},{29,1},{... | collective-permute-start | bytes 122888 | tf_op jit(solution)/shard_map/ppermute | solution.py:211
  79.4 7.6 %collective-permute-done.4.refs_1_ = bf16[80,256]{1,0:T(8,128)(2,1)S(1)} collective-permute-done((bf16[80,256]{1,0:T(8,128)(2,1)S(1)}, bf16[80,256]{1,0:T(8,128)(2,1)S(1)}, u32[]{:S(2)}, u32[]{:S(2)}) %collective-permute-start.4) | collective-permute-done | bytes 40992 | tf_op jit(solution)/shard_map/ppermute | solution.py:211
  87.0 0.0 collective-permute-done.5.refs_2_
  87.0 0.0 collective-permute-done.6.refs_3_
  87.0 2.1 %all-to-all-done.2.x_ref = bf16[8,352,128]{2,1,0:T(8,128)(2,1)S(1)} async-done(((bf16[8,352,128]{2,1,0:T(8,128)(2,1)}), bf16[8,352,128]{2,1,0:T(8,128)(2,1)S(1)}, u32[]{:S(2)}, u32[]{:S(2)}) %all-to-all-start.2) | async-done | bytes 720928 | tf_op jit(solution)/shard_map/all_to_all | solution.py:291
  89.2 0.8 shard_map.100
  (1 shorter events, 0.0 us)
Async XLA Ops:
  2.5 10.5 %copy-start.3 = (bf16[256,320]{0,1:T(8,128)(2,1)S(1)}, bf16[256,320]{0,1:T(8,128)(2,1)}, u32[]{:S(2)}) copy-start(bf16[256,320]{0,1:T(8,128)(2,1)} %param.10) | copy-start | bytes 491524
  2.5 18.2 %copy-start.1 = (bf16[256,320]{0,1:T(8,128)(2,1)S(1)}, bf16[256,320]{0,1:T(8,128)(2,1)}, u32[]{:S(2)}) copy-start(bf16[256,320]{0,1:T(8,128)(2,1)} %param.9) | copy-start | bytes 491524
  2.5 37.8 %all-to-all-start.1 = ((bf16[8,160,256]{2,1,0:T(8,128)(2,1)}), bf16[8,160,256]{2,1,0:T(8,128)(2,1)S(1)}, u32[]{:S(2)}, u32[]{:S(2)}) async-start(bf16[8,160,256]{2,1,0:T(8,128)(2,1)} %shard_map.97), calls=%async_computation.1 | async-start | bytes 1310720 | tf_op jit(solution)/shard_map/all_to_all | solution.py:231
  13.0 11.2 %copy-start = (bf16[320,1280]{1,0:T(8,128)(2,1)S(1)}, bf16[320,1280]{1,0:T(8,128)(2,1)}, u32[]{:S(2)}) copy-start(bf16[320,1280]{1,0:T(8,128)(2,1)} %w_ref.1) | copy-start | bytes 2457604
  20.7 3.5 %copy-start.2 = (bf16[256,320]{0,1:T(8,128)(2,1)S(1)}, bf16[256,320]{0,1:T(8,128)(2,1)}, u32[]{:S(2)}) copy-start(bf16[256,320]{0,1:T(8,128)(2,1)} %param.6) | copy-start | bytes 491524
  21.5 16.7 %collective-permute-start = (bf16[8,208,128]{2,1,0:T(8,128)(2,1)S(1)}, bf16[8,208,128]{2,1,0:T(8,128)(2,1)S(1)}, u32[]{:S(2)}, u32[]{:S(2)}) collective-permute-start(bf16[8,208,128]{2,1,0:T(8,128)(2,1)S(1)} %get-tuple-element.20), channel_id=1, source_target_pairs={{0,32},{32,0},{64,96},{96,64},{128,160},{160,128},{192,224},{224,1... | collective-permute-start | bytes 1277960 | tf_op jit(solution)/shard_map/ppermute | solution.py:242
  25.1 14.0 %collective-permute-start.1 = (bf16[176,256]{1,0:T(8,128)(2,1)S(1)}, bf16[176,256]{1,0:T(8,128)(2,1)S(1)}, u32[]{:S(2)}, u32[]{:S(2)}) collective-permute-start(bf16[176,256]{1,0:T(8,128)(2,1)S(1)} %get-tuple-element.21), channel_id=1, source_target_pairs={{0,24},{4,12},{8,0},{12,20},{16,8},{20,28},{24,16},{28,4},{1,25},{... | collective-permute-start | bytes 270344 | tf_op jit(solution)/shard_map/ppermute | solution.py:211
  31.1 7.9 %collective-permute-start.2 = (bf16[176,256]{1,0:T(8,128)(2,1)S(1)}, bf16[176,256]{1,0:T(8,128)(2,1)S(1)}, u32[]{:S(2)}, u32[]{:S(2)}) collective-permute-start(bf16[176,256]{1,0:T(8,128)(2,1)S(1)} %get-tuple-element.22), channel_id=1, source_target_pairs={{0,4},{4,8},{8,12},{12,16},{16,20},{20,24},{24,28},{28,0},{1,5},{5... | collective-permute-start | bytes 270344 | tf_op jit(solution)/shard_map/ppermute | solution.py:211
  33.3 7.0 %collective-permute-start.3 = (bf16[176,256]{1,0:T(8,128)(2,1)S(1)}, bf16[176,256]{1,0:T(8,128)(2,1)S(1)}, u32[]{:S(2)}, u32[]{:S(2)}) collective-permute-start(bf16[176,256]{1,0:T(8,128)(2,1)S(1)} %get-tuple-element.23), channel_id=1, source_target_pairs={{0,28},{4,0},{8,4},{12,8},{16,12},{20,16},{24,20},{28,24},{1,29},{... | collective-permute-start | bytes 270344 | tf_op jit(solution)/shard_map/ppermute | solution.py:211
  40.3 21.3 %all-to-all-start = ((bf16[8,208,128]{2,1,0:T(8,128)(2,1)}), bf16[8,208,128]{2,1,0:T(8,128)(2,1)S(1)}, u32[]{:S(2)}, u32[]{:S(2)}) async-start(bf16[8,208,128]{2,1,0:T(8,128)(2,1)} %shard_map.96), calls=%async_computation | async-start | bytes 851968 | tf_op jit(solution)/shard_map/all_to_all | solution.py:263
  62.4 26.8 %all-to-all-start.2 = ((bf16[8,352,128]{2,1,0:T(8,128)(2,1)}), bf16[8,352,128]{2,1,0:T(8,128)(2,1)S(1)}, u32[]{:S(2)}, u32[]{:S(2)}) async-start(bf16[8,352,128]{2,1,0:T(8,128)(2,1)} %shard_map.99), calls=%async_computation.2 | async-start | bytes 1441792 | tf_op jit(solution)/shard_map/all_to_all | solution.py:291
  68.0 19.0 %collective-permute-start.4 = (bf16[80,256]{1,0:T(8,128)(2,1)S(1)}, bf16[80,256]{1,0:T(8,128)(2,1)S(1)}, u32[]{:S(2)}, u32[]{:S(2)}) collective-permute-start(bf16[80,256]{1,0:T(8,128)(2,1)S(1)} %get-tuple-element.27), channel_id=1, source_target_pairs={{24,0},{12,4},{0,8},{20,12},{8,16},{28,20},{16,24},{4,28},{25,1},{... | collective-permute-start | bytes 122888 | tf_op jit(solution)/shard_map/ppermute | solution.py:211
  72.9 14.2 %collective-permute-start.5 = (bf16[80,256]{1,0:T(8,128)(2,1)S(1)}, bf16[80,256]{1,0:T(8,128)(2,1)S(1)}, u32[]{:S(2)}, u32[]{:S(2)}) collective-permute-start(bf16[80,256]{1,0:T(8,128)(2,1)S(1)} %get-tuple-element.28), channel_id=1, source_target_pairs={{4,0},{8,4},{12,8},{16,12},{20,16},{24,20},{28,24},{0,28},{5,1},{9... | collective-permute-start | bytes 122888 | tf_op jit(solution)/shard_map/ppermute | solution.py:211
  77.5 9.6 %collective-permute-start.6 = (bf16[80,256]{1,0:T(8,128)(2,1)S(1)}, bf16[80,256]{1,0:T(8,128)(2,1)S(1)}, u32[]{:S(2)}, u32[]{:S(2)}) collective-permute-start(bf16[80,256]{1,0:T(8,128)(2,1)S(1)} %get-tuple-element.29), channel_id=1, source_target_pairs={{28,0},{0,4},{4,8},{8,12},{12,16},{16,20},{20,24},{24,28},{29,1},{... | collective-permute-start | bytes 122888 | tf_op jit(solution)/shard_map/ppermute | solution.py:211

commit v7 on v5

--- a/solution.py
+++ b/solution.py
@@ -111,7 +111,7 @@
             ref[k, 2 * PG_ROWS :] = jnp.concatenate([last, empty], axis=0).astype(ref.dtype)
 
 
-def add_kernel(kept_ref, taken_ref, out_ref):
+def add_kernel(kept_ref, taken_ref, _, out_ref):
     out_ref[...] = (kept_ref[...] + taken_ref[...].astype(jnp.float32)).astype(jnp.bfloat16)
 
 
@@ -136,39 +136,51 @@
     copy.wait()
 
 
-def grad_kernel(x_ref, *refs):
-    near, (out_ref, *dq_refs) = refs[: len(NEAR)], refs[len(NEAR) : 2 * len(NEAR) + 1]
-    k_t, v_t, dk, dv = refs[2 * len(NEAR) + 1 :]
+def grad_blocks(blocks, dq_refs, k_ref, v_ref, dk, dv):
+    for block, dq_ref in zip(blocks, dq_refs):
+        q, g = block[:HD], block[HD:]
+        scores = dot(q, k_ref[...], TN)
+        peak = jnp.max(scores, axis=1, keepdims=True) * (FACTOR * LOG2E)
+        raised = jnp.exp2(scores * (FACTOR * LOG2E) - peak)
+        prob = raised * (1.0 / jnp.sum(raised, axis=1, keepdims=True))
+        shifted = dot(g, v_ref[...], TN)
+        dscore = (prob * shifted).astype(jnp.bfloat16)
+        dv_part = dot(g[:HD], prob.astype(jnp.bfloat16), NN)
+        dk_part = dot(q, dscore, NN)
+        dk = dk_part if dk is None else dk + dk_part
+        dv = dv_part if dv is None else dv + dv_part
+        dq_ref[...] = (dot(k_ref[...], dscore, NT) * FACTOR).astype(jnp.bfloat16)
+    return dk, dv
+
+
+def own_grad_kernel(x_ref, block_ref, k_ref, v_ref, dk_ref, dv_ref, dq_ref):
     for s in range(SHARDS):
         for b in range(2):
             tokens = slice((2 * s + b) * HALF, (2 * s + b + 1) * HALF)
-            k_t[:, tokens] = x_ref[s, K_AT + b * HD : K_AT + (b + 1) * HD]
-            v_t[:HD, tokens] = x_ref[s, V_AT + b * HD : V_AT + (b + 1) * HD]
+            k_ref[:, tokens] = x_ref[s, K_AT + b * HD : K_AT + (b + 1) * HD]
+            v_ref[:HD, tokens] = x_ref[s, V_AT + b * HD : V_AT + (b + 1) * HD]
     row = lax.broadcasted_iota(jnp.int32, (EXT - HD, SHARDS * ROWS), 0)
-    v_t[HD:] = jnp.where(row < 3, -1.0, 0.0).astype(jnp.bfloat16)
-    for i, (block, dq_ref) in enumerate(zip(near, dq_refs)):
-        q, g = block[:HD], block[HD:]
-        scores = dot(q, k_t[...], TN)
-        peak = jnp.max(scores, axis=1, keepdims=True) * (FACTOR * LOG2E)
-        raised = jnp.exp2(scores * (FACTOR * LOG2E) - peak)
-        prob = raised * (1.0 / jnp.sum(raised, axis=1, keepdims=True))
-        shifted = dot(g, v_t[...], TN)
-        dscore = (prob * shifted).astype(jnp.bfloat16)
-        dv_part = dot(g[:HD], prob.astype(jnp.bfloat16), NN)
-        dk_part = dot(q, dscore, NN)
-        if i == 0:
-            dv[...] = dv_part
-            dk[...] = dk_part
-        else:
-            dv[...] += dv_part
-            dk[...] += dk_part
-        dq_ref[...] = (dot(k_t[...], dscore, NT) * FACTOR).astype(jnp.bfloat16)
+    v_ref[HD:] = jnp.where(row < 3, -1.0, 0.0).astype(jnp.bfloat16)
+    dk_ref[...], dv_ref[...] = grad_blocks([block_ref], [dq_ref], k_ref, v_ref, None, None)
+
+
+def near_grad_kernel(k_ref, v_ref, dk_in_ref, dv_in_ref, *refs):
+    number = (len(refs) - 2) // 2
+    blocks, (dk_ref, dv_ref), dq_refs = refs[:number], refs[number : number + 2], refs[-number:]
+    dk_ref[...], dv_ref[...] = grad_blocks(
+        blocks, dq_refs, k_ref, v_ref, dk_in_ref[...], dv_in_ref[...]
+    )
+
+
+def last_grad_kernel(k_ref, v_ref, dk_in_ref, dv_in_ref, block_ref, out_ref, dq_ref):
+    dk, dv = grad_blocks([block_ref], [dq_ref], k_ref, v_ref, dk_in_ref[...], dv_in_ref[...])
+    dk, dv = (dk * FACTOR).astype(jnp.bfloat16), dv.astype(jnp.bfloat16)
     for s in range(SHARDS):
         for b in range(2):
             tokens = slice((2 * s + b) * HALF, (2 * s + b + 1) * HALF)
             at = b * HD
-            out_ref[s, K_AT + at : K_AT + at + HD] = (dk[:, tokens] * FACTOR).astype(jnp.bfloat16)
-            out_ref[s, V_AT + at : V_AT + at + HD] = dv[:, tokens].astype(jnp.bfloat16)
+            out_ref[s, K_AT + at : K_AT + at + HD] = dk[:, tokens]
+            out_ref[s, V_AT + at : V_AT + at + HD] = dv[:, tokens]
 
 
 def unpack_kernel(x_ref, *refs):
@@ -256,32 +268,35 @@
         mib=48,
     )(q, o, full_cot, proj_weight)
     near = [near[0]] + [shifted_round(x, away) for away, x in zip(NEAR[1:], near[1:])]
-    parts = call(add_kernel, shape(block, half), 0)(kept, taken)
+    tokens = SHARDS * ROWS
+    sums = [shape((HD, tokens), single)] * 2
+    grad = shape((HD, ROWS), half)
+    cost = (5 * 2 * tokens * ROWS * HD, tokens * ROWS)
+    both = [shape((HD, tokens), half), shape((EXT, tokens), half)]
+    k_all, v_all, dk, dv, dq_own = call(own_grad_kernel, both + sums + [grad], *cost, mib=32)(
+        pairs, near[0]
+    )
+    parts = call(
+        add_kernel, shape(block, half), 0, in_specs=[vmem, vmem, anywhere]
+    )(kept, taken, dq_own)
     parts = call(
         after_kernel,
         shape(block, half),
         0,
-        in_specs=[anywhere] * len(near),
+        in_specs=[anywhere] * 4,
         out_specs=anywhere,
         input_output_aliases={0: 0},
-    )(parts, *near[1:])
+    )(parts, *near[1:3], dq_own)
     along_y = [list(range(x, DP, 2)) for x in range(2)]
     parts = lax.all_to_all(parts, "dp", 0, 0, tiled=True, axis_index_groups=along_y)
 
-    tokens = SHARDS * ROWS
-    sent, *dq = call(
-        grad_kernel,
-        [shape((SHARDS, OUT_ROWS, HALF), half)]
-        + [shape((HD, ROWS), half)] * len(NEAR),
-        5 * 2 * tokens * (tokens // 2) * HD,
-        tokens * (tokens // 2),
-        [
-            pltpu.VMEM((HD, tokens), half),
-            pltpu.VMEM((EXT, tokens), half),
-            pltpu.VMEM((HD, tokens), single),
-            pltpu.VMEM((HD, tokens), single),
-        ],
-    )(pairs, *near)
+    dk, dv, *dq_near = call(
+        near_grad_kernel, sums + [grad] * 2, 2 * cost[0], 2 * cost[1], mib=32
+    )(k_all, v_all, dk, dv, *near[1:3])
+    sent, dq_last = call(
+        last_grad_kernel, [shape((SHARDS, OUT_ROWS, HALF), half), grad], *cost, mib=32
+    )(k_all, v_all, dk, dv, near[3])
+    dq = [dq_own, *dq_near, dq_last]
     sent = call(
         add_share_kernel,
         shape(sent.shape, half),

time: 90.6 us -> 91.9 us (1.014)
  the two profiles are of different devices: /device:TPU:4 before, /device:TPU:2 now
where the time goes in v7:
time: 91.9 us; the launch traced here: 91.2 us
  starting transfers between devices  51.5 us (56%)
  Pallas kernels  15.8 us (17%)
  waiting for transfers between devices  11.3 us (12%)
  blocking collectives  7.34 us (8%)
  local copies, waits for them, and re-layouts  4.33 us (5%)
    ppermute x6, starting transfers between devices, shifted_round(): lax.ppermute(x, 'ctx', [pair[::-1] for pair in pairs] if back else pairs)  24.9 us
    all_to_all x1, starting transfers between devices, on_device(): pairs = lax.all_to_all(pairs, 'ctx', 0, 0, tiled=True)  10.5 us
    ppermute x6, waiting for transfers between devices, shifted_round(): lax.ppermute(x, 'ctx', [pair[::-1] for pair in pairs] if back else pairs)  7.83 us
    all_gather x1, blocking collectives, on_device(): full_cot = lax.all_gather(cot, 'tp', axis=0, tiled=True)  7.34 us
    all_to_all x1, starting transfers between devices, on_device(): lax.all_to_all(parts, 'dp', 0, 0, tiled=True, axis_index_groups=along_y)  7.25 us
    all_to_all x1, starting transfers between devices, on_device(): back = lax.all_to_all(sent, 'ctx', 0, 0, tiled=True)  4.82 us
    unnamed x20, local copies, waits for them, and re-layouts  4.33 us
    ppermute x1, starting transfers between devices, on_device(): taken = lax.ppermute(given, 'dp', [(i, i ^ 1) for i in range(DP)])  4.1 us
  transfers between devices with their start and end apart: 10, of which 4 were waited for; matrix products, arithmetic and copies ran while one was open for 0% of the time, Pallas kernels for 14%

profile of v7, /device:TPU:2, one launch (start us, length us, event | category | flops | bytes accessed | tf_op | source)
XLA Modules:
  0.0 91.2 jit_solution(273660339144501423)
XLA Ops:
  0.6 1.8 %shard_map.94 = bf16[8,320,128]{2,1,0:T(8,128)(2,1)} custom-call(bf16[320,256]{1,0:T(8,128)(2,1)} %bitcast.13, bf16[320,256]{1,0:T(8,128)(2,1)} %bitcast.14), custom_call_target="tpu_custom_call" | custom-call | bytes 2097152 | tf_op jit(solution)/shard_map/pallas_call | solution.py:235
  2.4 0.0 copy-start.9
  2.4 0.0 copy-start.1
  2.5 10.5 %all-to-all-start = ((bf16[8,320,128]{2,1,0:T(8,128)(2,1)}), bf16[8,320,128]{2,1,0:T(8,128)(2,1)S(1)}, u32[]{:S(2)}, u32[]{:S(2)}) async-start(bf16[8,320,128]{2,1,0:T(8,128)(2,1)} %shard_map.94), calls=%async_computation | async-start | bytes 1310720 | tf_op jit(solution)/shard_map/all_to_all | solution.py:249
  12.9 0.0 copy-done.9
  12.9 0.0 copy-start
  12.9 7.3 %all_gather.3.cot_ref = bf16[1280,256]{1,0:T(8,128)(2,1)S(1)} all-gather(bf16[320,256]{1,0:T(8,128)(2,1)S(1)} %bitcast.12), channel_id=1, replica_groups=mesh['dp'=16,'ctx'=8,'tp'=4] {'tp'}, dimensions={0}, use_global_device_ids=true | all-gather | bytes 819200 | tf_op jit(solution)/shard_map/all_gather | solution.py:251
  20.3 0.0 copy-done.1
  20.3 0.0 copy-start.2
  20.3 0.8 shard_map.93
  21.1 4.1 %collective-permute-start = (bf16[8,208,128]{2,1,0:T(8,128)(2,1)S(1)}, bf16[8,208,128]{2,1,0:T(8,128)(2,1)S(1)}, u32[]{:S(2)}, u32[]{:S(2)}) collective-permute-start(bf16[8,208,128]{2,1,0:T(8,128)(2,1)S(1)} %get-tuple-element.26), channel_id=1, source_target_pairs={{0,32},{32,0},{64,96},{96,64},{128,160},{160,128},{192,224},{224,1... | collective-permute-start | bytes 1277960 | tf_op jit(solution)/shard_map/ppermute | solution.py:260
  25.2 0.0 copy-done
  25.2 0.0 copy-done.2
  25.2 1.5 %shard_map.95 = (bf16[176,256]{1,0:T(8,128)(2,1)S(1)}, bf16[176,256]{1,0:T(8,128)(2,1)}, bf16[176,256]{1,0:T(8,128)(2,1)}, bf16[176,256]{1,0:T(8,128)(2,1)S(1)}) custom-call(bf16[320,256]{1,0:T(8,128)(2,1)S(1)} %bitcast.11, bf16[320,256]{1,0:T(8,128)(2,1)S(1)} %bitcast.10, bf16[1280,256]{1,0:T(8,128)(2,1)S(1)} %all_gather.3.cot_ref, ...), custom_call_target="tpu_custom_call" | custom-call | flops 209715200 | bytes 2097152 | tf_op jit(solution)/shard_map/pallas_call | solution.py:261
  26.7 0.0 copy-start.3
  26.7 0.6 copy-done.3
  27.4 6.0 %collective-permute-start.1 = (bf16[176,256]{1,0:T(8,128)(2,1)}, bf16[176,256]{1,0:T(8,128)(2,1)S(1)}, u32[]{:S(2)}, u32[]{:S(2)}) collective-permute-start(bf16[176,256]{1,0:T(8,128)(2,1)} %get-tuple-element.29), channel_id=1, source_target_pairs={{0,24},{4,12},{8,0},{12,20},{16,8},{20,28},{24,16},{28,4},{1,25},{... | collective-permute-start | bytes 270344 | tf_op jit(solution)/shard_map/ppermute | solution.py:225
  33.4 2.2 %collective-permute-start.2 = (bf16[176,256]{1,0:T(8,128)(2,1)}, bf16[176,256]{1,0:T(8,128)(2,1)S(1)}, u32[]{:S(2)}, u32[]{:S(2)}) collective-permute-start(bf16[176,256]{1,0:T(8,128)(2,1)} %get-tuple-element.30), channel_id=1, source_target_pairs={{0,4},{4,8},{8,12},{12,16},{16,20},{20,24},{24,28},{28,0},{1,5},{5... | collective-permute-start | bytes 270344 | tf_op jit(solution)/shard_map/ppermute | solution.py:225
  35.6 0.0 all-to-all-done.x_ref
  35.6 0.0 copy-start.4
  35.6 0.9 copy-done.4
  36.5 2.3 %shard_map.96 = (bf16[80,2048]{1,0:T(8,128)(2,1)S(1)}, bf16[96,2048]{1,0:T(8,128)(2,1)S(1)}, f32[80,2048]{1,0:T(8,128)S(1)}, f32[80,2048]{1,0:T(8,128)S(1)}, bf16[80,256]{1,0:T(8,128)(2,1)S(1)}) custom-call(bf16[8,320,128]{2,1,0:T(8,128)(2,1)S(1)} %all-to-all-done.x_ref, bf16[176,256]{1,0:T(8,128)(2,1)S(1)} %copy-done.4), custom_call_target="tpu_custom_call" | custom-call | flops 419430400 | bytes 2097152 | tf_op jit(solution)/shard_map/pallas_call | solution.py:276
  38.8 0.0 copy-start.5
  38.8 0.8 copy-done.5
  39.6 0.0 copy-start.7
  39.7 0.9 copy-done.7
  40.5 0.0 collective-permute-done.taken_ref
  40.5 0.8 shard_map.97.refs_0_
  41.4 0.0 collective-permute-done.1.refs_1_.refs_0_
  41.4 0.0 collective-permute-done.2.refs_2_.refs_1_
  41.4 0.0 copy-start.6
  41.4 7.2 %all-to-all-start.1 = ((bf16[8,208,128]{2,1,0:T(8,128)(2,1)}), bf16[8,208,128]{2,1,0:T(8,128)(2,1)S(1)}, u32[]{:S(2)}, u32[]{:S(2)}) async-start(bf16[8,208,128]{2,1,0:T(8,128)(2,1)} %shard_map.98), calls=%async_computation.1 | async-start | bytes 851968 | tf_op jit(solution)/shard_map/all_to_all | solution.py:291
  48.6 4.9 %collective-permute-start.3 = (bf16[176,256]{1,0:T(8,128)(2,1)S(1)}, bf16[176,256]{1,0:T(8,128)(2,1)S(1)}, u32[]{:S(2)}, u32[]{:S(2)}) collective-permute-start(bf16[176,256]{1,0:T(8,128)(2,1)S(1)} %get-tuple-element.37), channel_id=1, source_target_pairs={{0,28},{4,0},{8,4},{12,8},{16,12},{20,16},{24,20},{28,24},{1,29},{... | collective-permute-start | bytes 270344 | tf_op jit(solution)/shard_map/ppermute | solution.py:225
  53.5 0.0 copy-done.6
  53.5 0.0 copy-start.8
  53.5 1.1 %copy-done.8 = f32[80,2048]{1,0:T(8,128)S(1)} copy-done((f32[80,2048]{1,0:T(8,128)S(1)}, f32[80,2048]{1,0:T(8,128)}, u32[]{:S(2)}) %copy-start.8) | copy-done | bytes 655384
  54.6 4.0 %shard_map.99 = (f32[80,2048]{1,0:T(8,128)S(1)}, f32[80,2048]{1,0:T(8,128)S(1)}, bf16[80,256]{1,0:T(8,128)(2,1)S(1)}, bf16[80,256]{1,0:T(8,128)(2,1)S(1)}) custom-call(bf16[80,2048]{1,0:T(8,128)(2,1)S(1)} %get-tuple-element.31.k_ref, bf16[96,2048]{1,0:T(8,128)(2,1)S(1)} %get-tuple-element.32.v_ref, f32[80,2048]{1,0:T(8,128)S(1)} %copy-done.6, ...), custom_call_target="tpu_custom_call" | custom-call | flops 838860800 | bytes 2097152 | tf_op jit(solution)/shard_map/pallas_call | solution.py:293
  58.6 0.0 collective-permute-done.3.block_ref
  58.6 3.1 %shard_map.100 = (bf16[8,352,128]{2,1,0:T(8,128)(2,1)}, bf16[80,256]{1,0:T(8,128)(2,1)S(1)}) custom-call(bf16[80,2048]{1,0:T(8,128)(2,1)S(1)} %get-tuple-element.31.k_ref, bf16[96,2048]{1,0:T(8,128)(2,1)S(1)} %get-tuple-element.32.v_ref, f32[80,2048]{1,0:T(8,128)S(1)} %get-tuple-element.35.dk_in_ref, f32[80,2048]{1,0:T(8,128)S(1)} %get-tuple-element.36.dv_in_ref, ...), custom_call_target="tpu_custom_call" | custom-call | flops 419430400 | bytes 2097152 | tf_op jit(solution)/shard_map/pallas_call | solution.py:296
  61.6 2.1 %all-to-all-done.1.parts_ref = bf16[8,208,128]{2,1,0:T(8,128)(2,1)S(1)} async-done(((bf16[8,208,128]{2,1,0:T(8,128)(2,1)}), bf16[8,208,128]{2,1,0:T(8,128)(2,1)S(1)}, u32[]{:S(2)}, u32[]{:S(2)}) %all-to-all-start.1) | async-done | bytes 426016 | tf_op jit(solution)/shard_map/all_to_all | solution.py:291
  63.7 0.7 shard_map.101
  64.5 4.8 %all-to-all-start.2 = ((bf16[8,352,128]{2,1,0:T(8,128)(2,1)}), bf16[8,352,128]{2,1,0:T(8,128)(2,1)S(1)}, u32[]{:S(2)}, u32[]{:S(2)}) async-start(bf16[8,352,128]{2,1,0:T(8,128)(2,1)} %shard_map.101), calls=%async_computation.2 | async-start | bytes 1441792 | tf_op jit(solution)/shard_map/all_to_all | solution.py:312
  69.3 3.9 %collective-permute-start.6 = (bf16[80,256]{1,0:T(8,128)(2,1)S(1)}, bf16[80,256]{1,0:T(8,128)(2,1)S(1)}, u32[]{:S(2)}, u32[]{:S(2)}) collective-permute-start(bf16[80,256]{1,0:T(8,128)(2,1)S(1)} %get-tuple-element.41), channel_id=1, source_target_pairs={{28,0},{0,4},{4,8},{8,12},{12,16},{16,20},{20,24},{24,28},{29,1},{... | collective-permute-start | bytes 122888 | tf_op jit(solution)/shard_map/ppermute | solution.py:225
  73.2 4.3 %collective-permute-start.4 = (bf16[80,256]{1,0:T(8,128)(2,1)S(1)}, bf16[80,256]{1,0:T(8,128)(2,1)S(1)}, u32[]{:S(2)}, u32[]{:S(2)}) collective-permute-start(bf16[80,256]{1,0:T(8,128)(2,1)S(1)} %get-tuple-element.39), channel_id=1, source_target_pairs={{24,0},{12,4},{0,8},{20,12},{8,16},{28,20},{16,24},{4,28},{25,1},{... | collective-permute-start | bytes 122888 | tf_op jit(solution)/shard_map/ppermute | solution.py:225
  77.5 3.7 %collective-permute-start.5 = (bf16[80,256]{1,0:T(8,128)(2,1)S(1)}, bf16[80,256]{1,0:T(8,128)(2,1)S(1)}, u32[]{:S(2)}, u32[]{:S(2)}) collective-permute-start(bf16[80,256]{1,0:T(8,128)(2,1)S(1)} %get-tuple-element.40), channel_id=1, source_target_pairs={{4,0},{8,4},{12,8},{16,12},{20,16},{24,20},{28,24},{0,28},{5,1},{9... | collective-permute-start | bytes 122888 | tf_op jit(solution)/shard_map/ppermute | solution.py:225
  81.2 3.8 %collective-permute-done.6.refs_3_ = bf16[80,256]{1,0:T(8,128)(2,1)S(1)} collective-permute-done((bf16[80,256]{1,0:T(8,128)(2,1)S(1)}, bf16[80,256]{1,0:T(8,128)(2,1)S(1)}, u32[]{:S(2)}, u32[]{:S(2)}) %collective-permute-start.6) | collective-permute-done | bytes 40992 | tf_op jit(solution)/shard_map/ppermute | solution.py:225
  85.0 4.1 %collective-permute-done.4.refs_1_ = bf16[80,256]{1,0:T(8,128)(2,1)S(1)} collective-permute-done((bf16[80,256]{1,0:T(8,128)(2,1)S(1)}, bf16[80,256]{1,0:T(8,128)(2,1)S(1)}, u32[]{:S(2)}, u32[]{:S(2)}) %collective-permute-start.4) | collective-permute-done | bytes 40992 | tf_op jit(solution)/shard_map/ppermute | solution.py:225
  89.0 0.0 collective-permute-done.5.refs_2_
  89.0 1.4 %all-to-all-done.2.x_ref = bf16[8,352,128]{2,1,0:T(8,128)(2,1)S(1)} async-done(((bf16[8,352,128]{2,1,0:T(8,128)(2,1)}), bf16[8,352,128]{2,1,0:T(8,128)(2,1)S(1)}, u32[]{:S(2)}, u32[]{:S(2)}) %all-to-all-start.2) | async-done | bytes 720928 | tf_op jit(solution)/shard_map/all_to_all | solution.py:312
  90.4 0.8 shard_map.102
  (1 shorter events, 0.0 us)
Async XLA Ops:
  2.4 10.5 %copy-start.9 = (bf16[256,320]{0,1:T(8,128)(2,1)S(1)}, bf16[256,320]{0,1:T(8,128)(2,1)}, u32[]{:S(2)}) copy-start(bf16[256,320]{0,1:T(8,128)(2,1)} %param.10) | copy-start | bytes 491524
  2.4 17.8 %copy-start.1 = (bf16[256,320]{0,1:T(8,128)(2,1)S(1)}, bf16[256,320]{0,1:T(8,128)(2,1)}, u32[]{:S(2)}) copy-start(bf16[256,320]{0,1:T(8,128)(2,1)} %param.9) | copy-start | bytes 491524
  2.5 33.1 %all-to-all-start = ((bf16[8,320,128]{2,1,0:T(8,128)(2,1)}), bf16[8,320,128]{2,1,0:T(8,128)(2,1)S(1)}, u32[]{:S(2)}, u32[]{:S(2)}) async-start(bf16[8,320,128]{2,1,0:T(8,128)(2,1)} %shard_map.94), calls=%async_computation | async-start | bytes 1310720 | tf_op jit(solution)/shard_map/all_to_all | solution.py:249
  12.9 12.2 %copy-start = (bf16[320,1280]{1,0:T(8,128)(2,1)S(1)}, bf16[320,1280]{1,0:T(8,128)(2,1)}, u32[]{:S(2)}) copy-start(bf16[320,1280]{1,0:T(8,128)(2,1)} %w_ref.1) | copy-start | bytes 2457604
  20.3 4.9 %copy-start.2 = (bf16[256,320]{0,1:T(8,128)(2,1)S(1)}, bf16[256,320]{0,1:T(8,128)(2,1)}, u32[]{:S(2)}) copy-start(bf16[256,320]{0,1:T(8,128)(2,1)} %param.6) | copy-start | bytes 491524
  21.1 19.5 %collective-permute-start = (bf16[8,208,128]{2,1,0:T(8,128)(2,1)S(1)}, bf16[8,208,128]{2,1,0:T(8,128)(2,1)S(1)}, u32[]{:S(2)}, u32[]{:S(2)}) collective-permute-start(bf16[8,208,128]{2,1,0:T(8,128)(2,1)S(1)} %get-tuple-element.26), channel_id=1, source_target_pairs={{0,32},{32,0},{64,96},{96,64},{128,160},{160,128},{192,224},{224,1... | collective-permute-start | bytes 1277960 | tf_op jit(solution)/shard_map/ppermute | solution.py:260
  26.7 0.6 copy-start.3
  27.4 14.0 %collective-permute-start.1 = (bf16[176,256]{1,0:T(8,128)(2,1)}, bf16[176,256]{1,0:T(8,128)(2,1)S(1)}, u32[]{:S(2)}, u32[]{:S(2)}) collective-permute-start(bf16[176,256]{1,0:T(8,128)(2,1)} %get-tuple-element.29), channel_id=1, source_target_pairs={{0,24},{4,12},{8,0},{12,20},{16,8},{20,28},{24,16},{28,4},{1,25},{... | collective-permute-start | bytes 270344 | tf_op jit(solution)/shard_map/ppermute | solution.py:225
  33.4 8.0 %collective-permute-start.2 = (bf16[176,256]{1,0:T(8,128)(2,1)}, bf16[176,256]{1,0:T(8,128)(2,1)S(1)}, u32[]{:S(2)}, u32[]{:S(2)}) collective-permute-start(bf16[176,256]{1,0:T(8,128)(2,1)} %get-tuple-element.30), channel_id=1, source_target_pairs={{0,4},{4,8},{8,12},{12,16},{16,20},{20,24},{24,28},{28,0},{1,5},{5... | collective-permute-start | bytes 270344 | tf_op jit(solution)/shard_map/ppermute | solution.py:225
  35.6 0.9 copy-start.4
  38.8 0.8 copy-start.5
  39.6 0.9 copy-start.7
  41.4 12.1 %copy-start.6 = (f32[80,2048]{1,0:T(8,128)S(1)}, f32[80,2048]{1,0:T(8,128)}, u32[]{:S(2)}) copy-start(f32[80,2048]{1,0:T(8,128)} %copy-done.5) | copy-start | bytes 1966084
  41.4 22.3 %all-to-all-start.1 = ((bf16[8,208,128]{2,1,0:T(8,128)(2,1)}), bf16[8,208,128]{2,1,0:T(8,128)(2,1)S(1)}, u32[]{:S(2)}, u32[]{:S(2)}) async-start(bf16[8,208,128]{2,1,0:T(8,128)(2,1)} %shard_map.98), calls=%async_computation.1 | async-start | bytes 851968 | tf_op jit(solution)/shard_map/all_to_all | solution.py:291
  48.6 9.9 %collective-permute-start.3 = (bf16[176,256]{1,0:T(8,128)(2,1)S(1)}, bf16[176,256]{1,0:T(8,128)(2,1)S(1)}, u32[]{:S(2)}, u32[]{:S(2)}) collective-permute-start(bf16[176,256]{1,0:T(8,128)(2,1)S(1)} %get-tuple-element.37), channel_id=1, source_target_pairs={{0,28},{4,0},{8,4},{12,8},{16,12},{20,16},{24,20},{28,24},{1,29},{... | collective-permute-start | bytes 270344 | tf_op jit(solution)/shard_map/ppermute | solution.py:225
  53.5 1.1 %copy-start.8 = (f32[80,2048]{1,0:T(8,128)S(1)}, f32[80,2048]{1,0:T(8,128)}, u32[]{:S(2)}) copy-start(f32[80,2048]{1,0:T(8,128)} %copy-done.7) | copy-start | bytes 1966084
  64.5 25.9 %all-to-all-start.2 = ((bf16[8,352,128]{2,1,0:T(8,128)(2,1)}), bf16[8,352,128]{2,1,0:T(8,128)(2,1)S(1)}, u32[]{:S(2)}, u32[]{:S(2)}) async-start(bf16[8,352,128]{2,1,0:T(8,128)(2,1)} %shard_map.101), calls=%async_computation.2 | async-start | bytes 1441792 | tf_op jit(solution)/shard_map/all_to_all | solution.py:312
  69.3 15.7 %collective-permute-start.6 = (bf16[80,256]{1,0:T(8,128)(2,1)S(1)}, bf16[80,256]{1,0:T(8,128)(2,1)S(1)}, u32[]{:S(2)}, u32[]{:S(2)}) collective-permute-start(bf16[80,256]{1,0:T(8,128)(2,1)S(1)} %get-tuple-element.41), channel_id=1, source_target_pairs={{28,0},{0,4},{4,8},{8,12},{12,16},{16,20},{20,24},{24,28},{29,1},{... | collective-permute-start | bytes 122888 | tf_op jit(solution)/shard_map/ppermute | solution.py:225
  73.2 15.8 %collective-permute-start.4 = (bf16[80,256]{1,0:T(8,128)(2,1)S(1)}, bf16[80,256]{1,0:T(8,128)(2,1)S(1)}, u32[]{:S(2)}, u32[]{:S(2)}) collective-permute-start(bf16[80,256]{1,0:T(8,128)(2,1)S(1)} %get-tuple-element.39), channel_id=1, source_target_pairs={{24,0},{12,4},{0,8},{20,12},{8,16},{28,20},{16,24},{4,28},{25,1},{... | collective-permute-start | bytes 122888 | tf_op jit(solution)/shard_map/ppermute | solution.py:225
  77.5 11.5 %collective-permute-start.5 = (bf16[80,256]{1,0:T(8,128)(2,1)S(1)}, bf16[80,256]{1,0:T(8,128)(2,1)S(1)}, u32[]{:S(2)}, u32[]{:S(2)}) collective-permute-start(bf16[80,256]{1,0:T(8,128)(2,1)S(1)} %get-tuple-element.40), channel_id=1, source_target_pairs={{4,0},{8,4},{12,8},{16,12},{20,16},{24,20},{28,24},{0,28},{5,1},{9... | collective-permute-start | bytes 122888 | tf_op jit(solution)/shard_map/ppermute | solution.py:225

commit v8 on v5

--- a/solution.py
+++ b/solution.py
@@ -23,7 +23,7 @@
 PG_COLS = 10
 PG_ROWS = 80
 PG_USED = 208
-NEAR = (0, 2, 1, 7)
+NEAR = (0, 2, 7, 1)
 
 NT = (((1,), (1,)), ((), ()))
 TN = (((0,), (0,)), ((), ()))

time: 90.6 us -> 90.8 us (level)
  the two profiles are of different devices: /device:TPU:4 before, /device:TPU:2 now
where the time goes in v8:
time: 90.8 us; the launch traced here: 90.2 us
  starting transfers between devices  51.2 us (56%)
  waiting for transfers between devices  17.4 us (19%)
  Pallas kernels  13.5 us (15%)
  blocking collectives  7.34 us (8%)
    ppermute x6, starting transfers between devices, shifted_round(): lax.ppermute(x, 'ctx', [pair[::-1] for pair in pairs] if back else pairs)  23.7 us
    all_to_all x1, starting transfers between devices, on_device(): pairs = lax.all_to_all(pairs, 'ctx', 0, 0, tiled=True)  10.5 us
    ppermute x6, waiting for transfers between devices, shifted_round(): lax.ppermute(x, 'ctx', [pair[::-1] for pair in pairs] if back else pairs)  8.8 us
    pallas_call x1, Pallas kernels, on_device(): call(grad_kernel, [shape((SHARDS, OUT_ROWS, HALF), half)] + [shape((HD, R...  7.65 us
    all_gather x1, blocking collectives, on_device(): full_cot = lax.all_gather(cot, 'tp', axis=0, tiled=True)  7.34 us
    all_to_all x1, starting transfers between devices, on_device(): lax.all_to_all(parts, 'dp', 0, 0, tiled=True, axis_index_groups=along_y)  7.1 us
    all_to_all x1, waiting for transfers between devices, on_device(): lax.all_to_all(parts, 'dp', 0, 0, tiled=True, axis_index_groups=along_y)  6.26 us
    all_to_all x1, starting transfers between devices, on_device(): back = lax.all_to_all(sent, 'ctx', 0, 0, tiled=True)  5.76 us
  transfers between devices with their start and end apart: 10, of which 4 were waited for; matrix products, arithmetic and copies ran while one was open for 0% of the time, Pallas kernels for 11%

profile of v8, /device:TPU:2, one launch (start us, length us, event | category | flops | bytes accessed | tf_op | source)
XLA Modules:
  0.0 90.2 jit_solution(8961899062413428331)
XLA Ops:
  0.6 1.8 %shard_map.97 = bf16[8,320,128]{2,1,0:T(8,128)(2,1)} custom-call(bf16[320,256]{1,0:T(8,128)(2,1)} %bitcast.13, bf16[320,256]{1,0:T(8,128)(2,1)} %bitcast.14), custom_call_target="tpu_custom_call" | custom-call | bytes 2097152 | tf_op jit(solution)/shard_map/pallas_call | solution.py:223
  2.4 0.0 copy-start.3
  2.4 0.0 copy-start.1
  2.5 10.5 %all-to-all-start.1 = ((bf16[8,320,128]{2,1,0:T(8,128)(2,1)}), bf16[8,320,128]{2,1,0:T(8,128)(2,1)S(1)}, u32[]{:S(2)}, u32[]{:S(2)}) async-start(bf16[8,320,128]{2,1,0:T(8,128)(2,1)} %shard_map.97), calls=%async_computation.1 | async-start | bytes 1310720 | tf_op jit(solution)/shard_map/all_to_all | solution.py:237
  12.9 0.0 copy-done.3
  12.9 0.0 copy-start
  12.9 7.3 %all_gather.3.cot_ref = bf16[1280,256]{1,0:T(8,128)(2,1)S(1)} all-gather(bf16[320,256]{1,0:T(8,128)(2,1)S(1)} %bitcast.12), channel_id=1, replica_groups=mesh['dp'=16,'ctx'=8,'tp'=4] {'tp'}, dimensions={0}, use_global_device_ids=true | all-gather | bytes 819200 | tf_op jit(solution)/shard_map/all_gather | solution.py:239
  20.3 0.0 copy-done.1
  20.3 0.0 copy-start.2
  20.3 0.8 shard_map.93
  21.1 4.1 %collective-permute-start = (bf16[8,208,128]{2,1,0:T(8,128)(2,1)S(1)}, bf16[8,208,128]{2,1,0:T(8,128)(2,1)S(1)}, u32[]{:S(2)}, u32[]{:S(2)}) collective-permute-start(bf16[8,208,128]{2,1,0:T(8,128)(2,1)S(1)} %get-tuple-element.20), channel_id=1, source_target_pairs={{0,32},{32,0},{64,96},{96,64},{128,160},{160,128},{192,224},{224,1... | collective-permute-start | bytes 1277960 | tf_op jit(solution)/shard_map/ppermute | solution.py:248
  25.2 0.0 copy-done
  25.2 0.0 copy-done.2
  25.2 0.9 shard_map.95
  26.1 6.0 %collective-permute-start.1 = (bf16[176,256]{1,0:T(8,128)(2,1)S(1)}, bf16[176,256]{1,0:T(8,128)(2,1)S(1)}, u32[]{:S(2)}, u32[]{:S(2)}) collective-permute-start(bf16[176,256]{1,0:T(8,128)(2,1)S(1)} %get-tuple-element.21), channel_id=1, source_target_pairs={{0,24},{4,12},{8,0},{12,20},{16,8},{20,28},{24,16},{28,4},{1,25},{... | collective-permute-start | bytes 270344 | tf_op jit(solution)/shard_map/ppermute | solution.py:213
  32.1 2.5 %collective-permute-start.2 = (bf16[176,256]{1,0:T(8,128)(2,1)S(1)}, bf16[176,256]{1,0:T(8,128)(2,1)S(1)}, u32[]{:S(2)}, u32[]{:S(2)}) collective-permute-start(bf16[176,256]{1,0:T(8,128)(2,1)S(1)} %get-tuple-element.22), channel_id=1, source_target_pairs={{0,28},{4,0},{8,4},{12,8},{16,12},{20,16},{24,20},{28,24},{1,29},{... | collective-permute-start | bytes 270344 | tf_op jit(solution)/shard_map/ppermute | solution.py:213
  34.6 3.4 %collective-permute-start.3 = (bf16[176,256]{1,0:T(8,128)(2,1)S(1)}, bf16[176,256]{1,0:T(8,128)(2,1)S(1)}, u32[]{:S(2)}, u32[]{:S(2)}) collective-permute-start(bf16[176,256]{1,0:T(8,128)(2,1)S(1)} %get-tuple-element.23), channel_id=1, source_target_pairs={{0,4},{4,8},{8,12},{12,16},{16,20},{20,24},{24,28},{28,0},{1,5},{5... | collective-permute-start | bytes 270344 | tf_op jit(solution)/shard_map/ppermute | solution.py:213
  38.0 0.0 collective-permute-done.taken_ref
  38.0 0.9 shard_map.94.refs_0_
  38.8 0.0 collective-permute-done.1.refs_1_
  38.8 0.0 collective-permute-done.2.refs_2_
  38.8 3.4 %collective-permute-done.3.refs_3_ = bf16[176,256]{1,0:T(8,128)(2,1)S(1)} collective-permute-done((bf16[176,256]{1,0:T(8,128)(2,1)S(1)}, bf16[176,256]{1,0:T(8,128)(2,1)S(1)}, u32[]{:S(2)}, u32[]{:S(2)}) %collective-permute-start.3) | collective-permute-done | bytes 90144 | tf_op jit(solution)/shard_map/ppermute | solution.py:213
  42.2 0.0 all-to-all-done.1.x_ref
  42.2 7.1 %all-to-all-start = ((bf16[8,208,128]{2,1,0:T(8,128)(2,1)}), bf16[8,208,128]{2,1,0:T(8,128)(2,1)S(1)}, u32[]{:S(2)}, u32[]{:S(2)}) async-start(bf16[8,208,128]{2,1,0:T(8,128)(2,1)} %shard_map.96), calls=%async_computation | async-start | bytes 851968 | tf_op jit(solution)/shard_map/all_to_all | solution.py:269
  49.3 7.7 %shard_map.98 = (bf16[8,352,128]{2,1,0:T(8,128)(2,1)}, bf16[80,256]{1,0:T(8,128)(2,1)S(1)}, bf16[80,256]{1,0:T(8,128)(2,1)S(1)}, bf16[80,256]{1,0:T(8,128)(2,1)S(1)}, bf16[80,256]{1,0:T(8,128)(2,1)S(1)}) custom-call(bf16[8,320,128]{2,1,0:T(8,128)(2,1)S(1)} %all-to-all-done.1.x_ref, bf16[176,256]{1,0:T(8,128)(2,1)S(1)} %get-tuple-element.24.refs_0_, ...), custom_call_target="tpu_custom_call" | custom-call | flops 1677721600 | bytes 2097152 | tf_op jit(solution)/shard_map/pallas_call | solution.py:272
  57.0 6.3 %all-to-all-done.parts_ref = bf16[8,208,128]{2,1,0:T(8,128)(2,1)S(1)} async-done(((bf16[8,208,128]{2,1,0:T(8,128)(2,1)}), bf16[8,208,128]{2,1,0:T(8,128)(2,1)S(1)}, u32[]{:S(2)}, u32[]{:S(2)}) %all-to-all-start) | async-done | bytes 426016 | tf_op jit(solution)/shard_map/all_to_all | solution.py:269
  63.2 0.7 shard_map.99
  64.0 5.8 %all-to-all-start.2 = ((bf16[8,352,128]{2,1,0:T(8,128)(2,1)}), bf16[8,352,128]{2,1,0:T(8,128)(2,1)S(1)}, u32[]{:S(2)}, u32[]{:S(2)}) async-start(bf16[8,352,128]{2,1,0:T(8,128)(2,1)} %shard_map.99), calls=%async_computation.2 | async-start | bytes 1441792 | tf_op jit(solution)/shard_map/all_to_all | solution.py:297
  69.7 4.8 %collective-permute-start.4 = (bf16[80,256]{1,0:T(8,128)(2,1)S(1)}, bf16[80,256]{1,0:T(8,128)(2,1)S(1)}, u32[]{:S(2)}, u32[]{:S(2)}) collective-permute-start(bf16[80,256]{1,0:T(8,128)(2,1)S(1)} %get-tuple-element.27), channel_id=1, source_target_pairs={{24,0},{12,4},{0,8},{20,12},{8,16},{28,20},{16,24},{4,28},{25,1},{... | collective-permute-start | bytes 122888 | tf_op jit(solution)/shard_map/ppermute | solution.py:213
  74.6 3.7 %collective-permute-start.5 = (bf16[80,256]{1,0:T(8,128)(2,1)S(1)}, bf16[80,256]{1,0:T(8,128)(2,1)S(1)}, u32[]{:S(2)}, u32[]{:S(2)}) collective-permute-start(bf16[80,256]{1,0:T(8,128)(2,1)S(1)} %get-tuple-element.28), channel_id=1, source_target_pairs={{28,0},{0,4},{4,8},{8,12},{12,16},{16,20},{20,24},{24,28},{29,1},{... | collective-permute-start | bytes 122888 | tf_op jit(solution)/shard_map/ppermute | solution.py:213
  78.2 3.4 %collective-permute-start.6 = (bf16[80,256]{1,0:T(8,128)(2,1)S(1)}, bf16[80,256]{1,0:T(8,128)(2,1)S(1)}, u32[]{:S(2)}, u32[]{:S(2)}) collective-permute-start(bf16[80,256]{1,0:T(8,128)(2,1)S(1)} %get-tuple-element.29), channel_id=1, source_target_pairs={{4,0},{8,4},{12,8},{16,12},{20,16},{24,20},{28,24},{0,28},{5,1},{9... | collective-permute-start | bytes 122888 | tf_op jit(solution)/shard_map/ppermute | solution.py:213
  81.6 5.4 %collective-permute-done.4.refs_1_ = bf16[80,256]{1,0:T(8,128)(2,1)S(1)} collective-permute-done((bf16[80,256]{1,0:T(8,128)(2,1)S(1)}, bf16[80,256]{1,0:T(8,128)(2,1)S(1)}, u32[]{:S(2)}, u32[]{:S(2)}) %collective-permute-start.4) | collective-permute-done | bytes 40992 | tf_op jit(solution)/shard_map/ppermute | solution.py:213
  87.0 0.0 collective-permute-done.5.refs_2_
  87.0 0.0 collective-permute-done.6.refs_3_
  87.0 2.3 %all-to-all-done.2.x_ref = bf16[8,352,128]{2,1,0:T(8,128)(2,1)S(1)} async-done(((bf16[8,352,128]{2,1,0:T(8,128)(2,1)}), bf16[8,352,128]{2,1,0:T(8,128)(2,1)S(1)}, u32[]{:S(2)}, u32[]{:S(2)}) %all-to-all-start.2) | async-done | bytes 720928 | tf_op jit(solution)/shard_map/all_to_all | solution.py:297
  89.4 0.8 shard_map.100
  (1 shorter events, 0.0 us)
Async XLA Ops:
  2.4 10.5 %copy-start.3 = (bf16[256,320]{0,1:T(8,128)(2,1)S(1)}, bf16[256,320]{0,1:T(8,128)(2,1)}, u32[]{:S(2)}) copy-start(bf16[256,320]{0,1:T(8,128)(2,1)} %param.10) | copy-start | bytes 491524
  2.4 17.8 %copy-start.1 = (bf16[256,320]{0,1:T(8,128)(2,1)S(1)}, bf16[256,320]{0,1:T(8,128)(2,1)}, u32[]{:S(2)}) copy-start(bf16[256,320]{0,1:T(8,128)(2,1)} %param.9) | copy-start | bytes 491524
  2.5 39.8 %all-to-all-start.1 = ((bf16[8,320,128]{2,1,0:T(8,128)(2,1)}), bf16[8,320,128]{2,1,0:T(8,128)(2,1)S(1)}, u32[]{:S(2)}, u32[]{:S(2)}) async-start(bf16[8,320,128]{2,1,0:T(8,128)(2,1)} %shard_map.97), calls=%async_computation.1 | async-start | bytes 1310720 | tf_op jit(solution)/shard_map/all_to_all | solution.py:237
  12.9 12.2 %copy-start = (bf16[320,1280]{1,0:T(8,128)(2,1)S(1)}, bf16[320,1280]{1,0:T(8,128)(2,1)}, u32[]{:S(2)}) copy-start(bf16[320,1280]{1,0:T(8,128)(2,1)} %w_ref.1) | copy-start | bytes 2457604
  20.3 4.9 %copy-start.2 = (bf16[256,320]{0,1:T(8,128)(2,1)S(1)}, bf16[256,320]{0,1:T(8,128)(2,1)}, u32[]{:S(2)}) copy-start(bf16[256,320]{0,1:T(8,128)(2,1)} %param.6) | copy-start | bytes 491524
  21.1 16.9 %collective-permute-start = (bf16[8,208,128]{2,1,0:T(8,128)(2,1)S(1)}, bf16[8,208,128]{2,1,0:T(8,128)(2,1)S(1)}, u32[]{:S(2)}, u32[]{:S(2)}) collective-permute-start(bf16[8,208,128]{2,1,0:T(8,128)(2,1)S(1)} %get-tuple-element.20), channel_id=1, source_target_pairs={{0,32},{32,0},{64,96},{96,64},{128,160},{160,128},{192,224},{224,1... | collective-permute-start | bytes 1277960 | tf_op jit(solution)/shard_map/ppermute | solution.py:248
  26.1 12.8 %collective-permute-start.1 = (bf16[176,256]{1,0:T(8,128)(2,1)S(1)}, bf16[176,256]{1,0:T(8,128)(2,1)S(1)}, u32[]{:S(2)}, u32[]{:S(2)}) collective-permute-start(bf16[176,256]{1,0:T(8,128)(2,1)S(1)} %get-tuple-element.21), channel_id=1, source_target_pairs={{0,24},{4,12},{8,0},{12,20},{16,8},{20,28},{24,16},{28,4},{1,25},{... | collective-permute-start | bytes 270344 | tf_op jit(solution)/shard_map/ppermute | solution.py:213
  32.1 6.7 %collective-permute-start.2 = (bf16[176,256]{1,0:T(8,128)(2,1)S(1)}, bf16[176,256]{1,0:T(8,128)(2,1)S(1)}, u32[]{:S(2)}, u32[]{:S(2)}) collective-permute-start(bf16[176,256]{1,0:T(8,128)(2,1)S(1)} %get-tuple-element.22), channel_id=1, source_target_pairs={{0,28},{4,0},{8,4},{12,8},{16,12},{20,16},{24,20},{28,24},{1,29},{... | collective-permute-start | bytes 270344 | tf_op jit(solution)/shard_map/ppermute | solution.py:213
  34.6 7.6 %collective-permute-start.3 = (bf16[176,256]{1,0:T(8,128)(2,1)S(1)}, bf16[176,256]{1,0:T(8,128)(2,1)S(1)}, u32[]{:S(2)}, u32[]{:S(2)}) collective-permute-start(bf16[176,256]{1,0:T(8,128)(2,1)S(1)} %get-tuple-element.23), channel_id=1, source_target_pairs={{0,4},{4,8},{8,12},{12,16},{16,20},{20,24},{24,28},{28,0},{1,5},{5... | collective-permute-start | bytes 270344 | tf_op jit(solution)/shard_map/ppermute | solution.py:213
  42.2 21.0 %all-to-all-start = ((bf16[8,208,128]{2,1,0:T(8,128)(2,1)}), bf16[8,208,128]{2,1,0:T(8,128)(2,1)S(1)}, u32[]{:S(2)}, u32[]{:S(2)}) async-start(bf16[8,208,128]{2,1,0:T(8,128)(2,1)} %shard_map.96), calls=%async_computation | async-start | bytes 851968 | tf_op jit(solution)/shard_map/all_to_all | solution.py:269
  64.0 25.4 %all-to-all-start.2 = ((bf16[8,352,128]{2,1,0:T(8,128)(2,1)}), bf16[8,352,128]{2,1,0:T(8,128)(2,1)S(1)}, u32[]{:S(2)}, u32[]{:S(2)}) async-start(bf16[8,352,128]{2,1,0:T(8,128)(2,1)} %shard_map.99), calls=%async_computation.2 | async-start | bytes 1441792 | tf_op jit(solution)/shard_map/all_to_all | solution.py:297
  69.7 17.3 %collective-permute-start.4 = (bf16[80,256]{1,0:T(8,128)(2,1)S(1)}, bf16[80,256]{1,0:T(8,128)(2,1)S(1)}, u32[]{:S(2)}, u32[]{:S(2)}) collective-permute-start(bf16[80,256]{1,0:T(8,128)(2,1)S(1)} %get-tuple-element.27), channel_id=1, source_target_pairs={{24,0},{12,4},{0,8},{20,12},{8,16},{28,20},{16,24},{4,28},{25,1},{... | collective-permute-start | bytes 122888 | tf_op jit(solution)/shard_map/ppermute | solution.py:213
  74.6 12.5 %collective-permute-start.5 = (bf16[80,256]{1,0:T(8,128)(2,1)S(1)}, bf16[80,256]{1,0:T(8,128)(2,1)S(1)}, u32[]{:S(2)}, u32[]{:S(2)}) collective-permute-start(bf16[80,256]{1,0:T(8,128)(2,1)S(1)} %get-tuple-element.28), channel_id=1, source_target_pairs={{28,0},{0,4},{4,8},{8,12},{12,16},{16,20},{20,24},{24,28},{29,1},{... | collective-permute-start | bytes 122888 | tf_op jit(solution)/shard_map/ppermute | solution.py:213
  78.2 8.8 %collective-permute-start.6 = (bf16[80,256]{1,0:T(8,128)(2,1)S(1)}, bf16[80,256]{1,0:T(8,128)(2,1)S(1)}, u32[]{:S(2)}, u32[]{:S(2)}) collective-permute-start(bf16[80,256]{1,0:T(8,128)(2,1)S(1)} %get-tuple-element.29), channel_id=1, source_target_pairs={{4,0},{8,4},{12,8},{16,12},{20,16},{24,20},{28,24},{0,28},{5,1},{9... | collective-permute-start | bytes 122888 | tf_op jit(solution)/shard_map/ppermute | solution.py:213
